TPU v7x, 32 devices: a whole 2x2x4 slice. The times are simulated.
32 devices in a mesh: dp: 4 (over x, core), tensor: 8 (over z, y).
Axes of the slice: x: 2, y: 2, z: 4, core: 2. Of those that a mesh axis runs over, the one named last changes fastest.
Arguments:
- tokens: bfloat16 [8192, 2048], P(('dp', 'tensor')), may hold values from -6 to 6
- segments: int32 [8192], P('dp'), may hold values from 0 to 8, as said below
- attn_gain: float32 [2048], replicated, may hold values from 0.1 to 1.9
- ffn_gain: float32 [2048], replicated, may hold values from 0.1 to 1.9
- w_query: bfloat16 [2048, 2048], P(None, 'tensor'), may hold values from -0.1875 to 0.1875
- w_key: bfloat16 [2048, 2048], P(None, 'tensor'), may hold values from -0.1875 to 0.1875
- w_value: bfloat16 [2048, 2048], P(None, 'tensor'), may hold values from -0.125 to 0.125
- w_out: bfloat16 [2048, 2048], P('tensor'), may hold values from -0.75 to 0.75
- w_gate: bfloat16 [2048, 5504], P(None, 'tensor'), may hold values from -0.125 to 0.125
- w_up: bfloat16 [2048, 5504], P(None, 'tensor'), may hold values from -0.125 to 0.125
- w_down: bfloat16 [5504, 2048], P('tensor'), may hold values from -0.15625 to 0.15625
- cotangent: bfloat16 [8192, 2048], P(('dp', 'tensor')), may hold values from -6 to 6
Outputs:
- output: bfloat16 [8192, 2048], P(('dp', 'tensor'))
- input_grad: bfloat16 [8192, 2048], P(('dp', 'tensor'))
- grad_attn_gain: float32 [2048], replicated
- grad_ffn_gain: float32 [2048], replicated
- grad_w_query: float32 [2048, 2048], P(None, 'tensor')
- grad_w_key: float32 [2048, 2048], P(None, 'tensor')
- grad_w_value: float32 [2048, 2048], P(None, 'tensor')
- grad_w_out: float32 [2048, 2048], P('tensor')
- grad_w_gate: float32 [2048, 5504], P(None, 'tensor')
- grad_w_up: float32 [2048, 5504], P(None, 'tensor')
- grad_w_down: float32 [5504, 2048], P('tensor')
- doc_rms: float32 [3, 9], replicated
Inputs may be any that keep to these rules, and one draw needn't show every extreme that they name: segments never fall, start at 0 and rise by one at each document start; each block of 2048 tokens holds exactly two document starts, the first at one of its tokens 2048 // 8 to 767, the second at one of its tokens 3 * 256 to 1791; in some block other than the last the second start lies at its token 1024 or earlier.
All inputs are finite; a program needn't handle non-finite values.
Results may differ from a plain program's by a relative error of at most 0.025.
Values may be sent and summed in bfloat16 or wider, within the bound.
No kernel may reach another device: no remote copies, remote signals or barrier semaphores. Data moves between devices by JAX's collectives and lax.ppermute only.
A program may use at most 192 MiB of HBM per device.

v0:
```python
import math

import jax
import jax.numpy as jnp
from jax import lax
from jax.sharding import PartitionSpec as P

HEAD_DIM = 128
WINDOW = 1024


eps_norm = 1e-06
neg_large = -1e30


def shifted(value, axis, steps):
    count = lax.axis_size(axis)
    leading, last = (max(0, -steps), min(count, count - steps))
    return lax.ppermute(value, axis, [(source, source + steps) for source in range(leading, last)])


def norm_forward(values, gain_vec):
    inverse = lax.rsqrt(jnp.mean(values * values, axis=-1, keepdims=True) + eps_norm)
    unit_rows = values * inverse
    return (unit_rows * gain_vec, unit_rows, inverse)


def norm_backward(grad_in, unit_rows, inverse, gain_vec):
    scaled = grad_in * gain_vec
    inner_sum = jnp.mean(scaled * unit_rows, axis=-1, keepdims=True)
    return (inverse * (scaled - unit_rows * inner_sum), jnp.sum(grad_in * unit_rows, axis=0))


def rope_tables(positions, head_dim):
    half_dim = head_dim // 2
    frequency = jnp.exp(
        jnp.arange(half_dim, dtype=jnp.float32) * (-2.0 * math.log(10000.0) / head_dim)
    )
    angles = positions.astype(jnp.float32)[:, None] * frequency[None, :]
    return (jnp.cos(angles), jnp.sin(angles))


def rotate(values, cos_table, sin_table, head_dim, sign_back):
    row_num = values.shape[0]
    split_heads = values.reshape(row_num, -1, head_dim)
    half_dim = head_dim // 2
    first_half = split_heads[..., :half_dim]
    second_half = split_heads[..., half_dim:]
    cos_part = cos_table[:, None, :]
    sin_part = sin_table[:, None, :] * sign_back
    joined = jnp.concatenate(
        [
            first_half * cos_part - second_half * sin_part,
            second_half * cos_part + first_half * sin_part,
        ],
        axis=-1,
    )
    return joined.reshape(row_num, -1)


def contract_rows(left, right):
    return lax.dot_general(
        left, right, (((0,), (0,)), ((), ())), preferred_element_type=jnp.float32
    )


def contract_cols(left, right):
    return lax.dot_general(
        left, right, (((1,), (1,)), ((), ())), preferred_element_type=jnp.float32
    )


def shards(
    tokens,
    segments,
    attn_gain,
    ffn_gain,
    w_query,
    w_key,
    w_value,
    w_out,
    w_gate,
    w_up,
    w_down,
    cotangent,
):
    row_count = tokens.shape[0]
    block_len = row_count * lax.axis_size("tensor")
    feature_count = tokens.shape[1]
    head_cols = w_query.shape[1]
    head_count = head_cols // HEAD_DIM
    query_len = min(512, block_len)
    key_span = query_len + WINDOW
    n_blocks = block_len // query_len
    first_pos = lax.axis_index("dp") * block_len
    own_start = lax.axis_index("tensor") * row_count
    scale_qk = HEAD_DIM ** (-0.5)
    tail_start = block_len - WINDOW
    input_f = tokens.astype(jnp.float32)
    x_normed, x_unit, x_inverse = norm_forward(input_f, attn_gain)
    gathered_x = lax.all_gather(x_normed.astype(jnp.bfloat16), "tensor", axis=0, tiled=True)
    w_joint = jnp.concatenate([w_query, w_key, w_value], axis=1)
    projected = jnp.dot(gathered_x, w_joint, preferred_element_type=jnp.float32)
    positions = first_pos + jnp.arange(block_len, dtype=jnp.int32)
    cos_table, sin_table = rope_tables(positions, HEAD_DIM)
    query_rot = rotate(projected[:, :head_cols], cos_table, sin_table, HEAD_DIM, 1.0).astype(
        jnp.bfloat16
    )
    key_rot = rotate(
        projected[:, head_cols : 2 * head_cols], cos_table, sin_table, HEAD_DIM, 1.0
    ).astype(jnp.bfloat16)
    value_low = projected[:, 2 * head_cols :].astype(jnp.bfloat16)
    prev_key, prev_value, prev_seg = shifted(
        (key_rot[tail_start:], value_low[tail_start:], segments[tail_start:].astype(jnp.bfloat16)),
        "dp",
        1,
    )
    key_all = jnp.concatenate([prev_key, key_rot], axis=0)
    value_all = jnp.concatenate([prev_value, value_low], axis=0)
    seg_all = jnp.concatenate([prev_seg.astype(jnp.int32), segments], axis=0)
    pos_all = first_pos - WINDOW + jnp.arange(WINDOW + block_len, dtype=jnp.int32)

    def block_scores(row_start):
        query_blk = lax.dynamic_slice_in_dim(query_rot, row_start, query_len).reshape(
            query_len, head_count, HEAD_DIM
        )
        key_blk = lax.dynamic_slice_in_dim(key_all, row_start, key_span).reshape(
            key_span, head_count, HEAD_DIM
        )
        value_blk = lax.dynamic_slice_in_dim(value_all, row_start, key_span).reshape(
            key_span, head_count, HEAD_DIM
        )
        query_seg = lax.dynamic_slice_in_dim(segments, row_start, query_len)
        query_pos = first_pos + row_start + jnp.arange(query_len, dtype=jnp.int32)
        key_seg = lax.dynamic_slice_in_dim(seg_all, row_start, key_span)
        key_pos = lax.dynamic_slice_in_dim(pos_all, row_start, key_span)
        distance = query_pos[:, None] - key_pos[None, :]
        allowed = (
            (query_seg[:, None] == key_seg[None, :])
            & (distance >= 0)
            & (distance < WINDOW)
            & (key_pos[None, :] >= 0)
        )
        raw_scores = (
            jnp.einsum("qhd,khd->hqk", query_blk, key_blk, preferred_element_type=jnp.float32)
            * scale_qk
        )
        return (jnp.where(allowed[None], raw_scores, neg_large), query_blk, key_blk, value_blk)

    def attend(block_id):
        scores, query_blk, key_blk, value_blk = block_scores(block_id * query_len)
        row_max = jnp.max(scores, axis=-1, keepdims=True)
        exp_terms = jnp.exp(scores - row_max)
        row_total = jnp.sum(exp_terms, axis=-1, keepdims=True)
        weights_low = (exp_terms / row_total).astype(jnp.bfloat16)
        head_mix = jnp.einsum(
            "hqk,khd->qhd", weights_low, value_blk, preferred_element_type=jnp.float32
        )
        return (
            head_mix.reshape(query_len, head_cols).astype(jnp.bfloat16),
            (row_max + jnp.log(row_total))[..., 0],
        )

    attn_low, log_sums = lax.map(attend, jnp.arange(n_blocks, dtype=jnp.int32))
    attn_low = attn_low.reshape(block_len, head_cols)
    attn_branch = lax.psum_scatter(
        jnp.dot(attn_low, w_out, preferred_element_type=jnp.float32).astype(jnp.bfloat16),
        "tensor",
        scatter_dimension=0,
        tiled=True,
    ).astype(jnp.float32)
    mid_stream = input_f + attn_branch
    h_normed, h_unit, h_inverse = norm_forward(mid_stream, ffn_gain)
    gathered_h = lax.all_gather(h_normed.astype(jnp.bfloat16), "tensor", axis=0, tiled=True)
    gate_pre = jnp.dot(gathered_h, w_gate, preferred_element_type=jnp.float32)
    up_pre = jnp.dot(gathered_h, w_up, preferred_element_type=jnp.float32)
    hidden = (jax.nn.silu(gate_pre) * up_pre).astype(jnp.bfloat16)
    ffn_branch = lax.psum_scatter(
        jnp.dot(hidden, w_down, preferred_element_type=jnp.float32).astype(jnp.bfloat16),
        "tensor",
        scatter_dimension=0,
        tiled=True,
    ).astype(jnp.float32)
    result = mid_stream + ffn_branch
    gathered_dy = lax.all_gather(cotangent, "tensor", axis=0, tiled=True)
    grad_down = contract_rows(hidden, gathered_dy)
    grad_hidden = contract_cols(gathered_dy, w_down)
    sig_gate = jax.nn.sigmoid(gate_pre)
    grad_gate = (grad_hidden * up_pre * sig_gate * (1.0 + gate_pre * (1.0 - sig_gate))).astype(
        jnp.bfloat16
    )
    grad_up_pre = (grad_hidden * gate_pre * sig_gate).astype(jnp.bfloat16)
    grad_gate_w = contract_rows(gathered_h, grad_gate)
    grad_up_w = contract_rows(gathered_h, grad_up_pre)
    gate_part = contract_cols(grad_gate, w_gate)
    grad_h_normed = lax.psum_scatter(
        (gate_part + contract_cols(grad_up_pre, w_up)).astype(jnp.bfloat16),
        "tensor",
        scatter_dimension=0,
        tiled=True,
    ).astype(jnp.float32)
    grad_mid_norm, grad_ffn_part = norm_backward(grad_h_normed, h_unit, h_inverse, ffn_gain)
    grad_mid = cotangent.astype(jnp.float32) + grad_mid_norm
    gathered_dh = lax.all_gather(grad_mid.astype(jnp.bfloat16), "tensor", axis=0, tiled=True)
    grad_out_w = contract_rows(attn_low, gathered_dh)
    grad_heads = contract_cols(gathered_dh, w_out).astype(jnp.bfloat16)

    def attend_back(carry_pair, block_id):
        key_grad, value_grad = carry_pair
        row_start = block_id * query_len
        scores, query_blk, key_blk, value_blk = block_scores(row_start)
        grad_blk = lax.dynamic_slice_in_dim(grad_heads, row_start, query_len).reshape(
            query_len, head_count, HEAD_DIM
        )
        probs = jnp.exp(scores - log_sums[block_id][..., None])
        grad_probs = jnp.einsum(
            "qhd,khd->hqk", grad_blk, value_blk, preferred_element_type=jnp.float32
        )
        inner_sum = jnp.sum(probs * grad_probs, axis=-1, keepdims=True)
        grad_scores = (probs * (grad_probs - inner_sum)).astype(jnp.bfloat16)
        query_grad = (
            jnp.einsum("hqk,khd->qhd", grad_scores, key_blk, preferred_element_type=jnp.float32)
            * scale_qk
        )
        key_part = (
            jnp.einsum("hqk,qhd->khd", grad_scores, query_blk, preferred_element_type=jnp.float32)
            * scale_qk
        )
        value_part = jnp.einsum(
            "hqk,qhd->khd", probs.astype(jnp.bfloat16), grad_blk, preferred_element_type=jnp.float32
        )
        key_grad = lax.dynamic_update_slice_in_dim(
            key_grad,
            lax.dynamic_slice_in_dim(key_grad, row_start, key_span)
            + key_part.reshape(key_span, head_cols),
            row_start,
            0,
        )
        value_grad = lax.dynamic_update_slice_in_dim(
            value_grad,
            lax.dynamic_slice_in_dim(value_grad, row_start, key_span)
            + value_part.reshape(key_span, head_cols),
            row_start,
            0,
        )
        return ((key_grad, value_grad), query_grad.reshape(query_len, head_cols))

    zero_keys = jnp.zeros((WINDOW + block_len, head_cols), jnp.float32)
    (key_grad, value_grad), query_grad = lax.scan(
        attend_back, (zero_keys, zero_keys), jnp.arange(n_blocks, dtype=jnp.int32)
    )
    query_grad = query_grad.reshape(block_len, head_cols)
    back_key, back_value = (
        shifted(key_grad[:WINDOW].astype(jnp.bfloat16), "dp", -1).astype(jnp.float32),
        shifted(value_grad[:WINDOW].astype(jnp.bfloat16), "dp", -1).astype(jnp.float32),
    )
    key_own = key_grad[WINDOW:].at[tail_start:].add(back_key)
    value_own = value_grad[WINDOW:].at[tail_start:].add(back_value)
    grad_joint_in = jnp.concatenate(
        [
            rotate(query_grad, cos_table, sin_table, HEAD_DIM, -1.0),
            rotate(key_own, cos_table, sin_table, HEAD_DIM, -1.0),
            value_own,
        ],
        axis=1,
    ).astype(jnp.bfloat16)
    grad_joint_w = contract_rows(gathered_x, grad_joint_in)
    grad_x_normed = lax.psum_scatter(
        contract_cols(grad_joint_in, w_joint).astype(jnp.bfloat16),
        "tensor",
        scatter_dimension=0,
        tiled=True,
    ).astype(jnp.float32)
    grad_in_norm, grad_attn_part = norm_backward(grad_x_normed, x_unit, x_inverse, attn_gain)
    input_grad = (grad_mid + grad_in_norm).astype(jnp.bfloat16)
    summed_joint, summed_out, summed_gate, summed_up, summed_down = (
        lax.psum(grad_joint_w.astype(jnp.bfloat16), "dp").astype(jnp.float32),
        lax.psum(grad_out_w.astype(jnp.bfloat16), "dp").astype(jnp.float32),
        lax.psum(grad_gate_w.astype(jnp.bfloat16), "dp").astype(jnp.float32),
        lax.psum(grad_up_w.astype(jnp.bfloat16), "dp").astype(jnp.float32),
        lax.psum(grad_down.astype(jnp.bfloat16), "dp").astype(jnp.float32),
    )
    slot_count = 2 * lax.axis_size("dp") + 1
    own_seg = lax.dynamic_slice_in_dim(segments, own_start, row_count)
    one_hot = (own_seg[:, None] == jnp.arange(slot_count, dtype=jnp.int32)[None, :]).astype(
        jnp.float32
    )
    per_row = jnp.stack(
        [
            jnp.sum(result * result, axis=1),
            jnp.sum(attn_branch * attn_branch, axis=1),
            jnp.sum(ffn_branch * ffn_branch, axis=1),
        ],
        axis=1,
    )
    doc_table = jnp.dot(
        per_row.T, one_hot, precision=lax.Precision.HIGHEST, preferred_element_type=jnp.float32
    )
    doc_count = jnp.sum(one_hot, axis=0)
    gain_attn_sum, gain_ffn_sum, table_sum, count_sum = lax.psum(
        (grad_attn_part, grad_ffn_part, doc_table, doc_count), ("dp", "tensor")
    )
    doc_rms = jnp.sqrt(table_sum / (jnp.maximum(count_sum, 1.0) * feature_count))
    return (
        result.astype(jnp.bfloat16),
        input_grad,
        gain_attn_sum,
        gain_ffn_sum,
        summed_joint[:, :head_cols],
        summed_joint[:, head_cols : 2 * head_cols],
        summed_joint[:, 2 * head_cols :],
        summed_out,
        summed_gate,
        summed_up,
        summed_down,
        doc_rms,
    )


def solution(mesh):
    return jax.shard_map(
        shards,
        mesh=mesh,
        in_specs=(
            P(("dp", "tensor"), None),
            P("dp"),
            P(),
            P(),
            P(None, "tensor"),
            P(None, "tensor"),
            P(None, "tensor"),
            P("tensor", None),
            P(None, "tensor"),
            P(None, "tensor"),
            P("tensor", None),
            P(("dp", "tensor"), None),
        ),
        out_specs=(
            P(("dp", "tensor"), None),
            P(("dp", "tensor"), None),
            P(),
            P(),
            P(None, "tensor"),
            P(None, "tensor"),
            P(None, "tensor"),
            P("tensor", None),
            P(None, "tensor"),
            P(None, "tensor"),
            P("tensor", None),
            P(),
        ),
        check_vma=False,
    )
```

profile of v0, /device:TPU:0, one launch (start us, length us, event | category | flops | bytes accessed | tf_op | source)
XLA Modules:
  0.0 1723.9 jit_solution(10809750151415369154)
XLA Ops:
  17.5 5.7 broadcast_multiply_fusion
  23.2 116.0 %all-gather.5.cloned.1.call-done = bf16[2048,2048]{1,0:T(8,128)(2,1)} async-done(((bf16[256,2048]{1,0:T(8,128)(2,1)}), bf16[2048,2048]{1,0:T(8,128)(2,1)}) %all-gather.5.cloned.1.call-update) | async-done | bytes 8388624 | tf_op jit(solution)/shard_map/all_gather | solution.py:101
  139.3 10.4 fusion.53
  171.9 7.8 subtract_convert_fusion.2
  187.3 8.2 pad_maximum_fusion.5
  209.1 49.4 %while.28 = (s32[]{:T(128)}, bf16[4,512,256]{2,1,0:T(8,128)(2,1)}, f32[4,2,512]{2,1,0:T(2,128)}, s32[4]{0:T(128)S(1)}, bf16[3072,256]{0,1:T(8,128)(2,1)}, /*inde...) while((s32[]{:T(128)}, bf16[4,512,256]{2,1,0:T(8,128)(2,1)}, ...), condition=%wide.region_4.5_spmd, body=%wide.region_1.4_spmd.sunk | while | flops 829817856 | bytes 28919068 | solution.py:164
  258.6 7.2 convolution_convert_fusion.2
  266.0 146.2 %reduce-scatter.5.cloned.1.call-done = bf16[256,2048]{1,0:T(8,128)(2,1)} async-done(((bf16[2048,2048]{1,0:T(8,128)(2,1)}), bf16[256,2048]{1,0:T(8,128)(2,1)}) %reduce-scatter.5.cloned.1.call-update) | async-done | bytes 1048592 | tf_op jit(solution)/shard_map/reduce_scatter | solution.py:166
  416.5 123.5 %all-gather.7.cloned.1.call-done = bf16[2048,2048]{1,0:T(8,128)(2,1)} async-done(((bf16[256,2048]{1,0:T(8,128)(2,1)}), bf16[2048,2048]{1,0:T(8,128)(2,1)}) %all-gather.7.cloned.1.call-update) | async-done | bytes 8388624 | tf_op jit(solution)/shard_map/all_gather | solution.py:174
  540.0 11.0 fusion.56
  551.0 7.8 fusion.55
  558.8 106.5 %all-gather.9.cloned.1.call-done = bf16[2048,2048]{1,0:T(8,128)(2,1)} async-done(((bf16[256,2048]{1,0:T(8,128)(2,1)}), bf16[2048,2048]{1,0:T(8,128)(2,1)}) %all-gather.9.cloned.1.call-update) | async-done | bytes 8388624 | tf_op jit(solution)/shard_map/all_gather | solution.py:185
  665.3 14.7 multiply_convert_fusion.1
  681.6 9.3 convolution_convert_fusion
  692.7 12.2 fusion.57
  704.8 12.6 add_convert_fusion
  717.9 120.4 %reduce-scatter.7.cloned.1.call-done = bf16[256,2048]{1,0:T(8,128)(2,1)} async-done(((bf16[2048,2048]{1,0:T(8,128)(2,1)}), bf16[256,2048]{1,0:T(8,128)(2,1)}) %reduce-scatter.7.cloned.1.call-update) | async-done | bytes 1048592 | tf_op jit(solution)/shard_map/reduce_scatter | solution.py:178
  838.3 151.5 %reduce-scatter.9.cloned.1.call-done = bf16[256,2048]{1,0:T(8,128)(2,1)} async-done(((bf16[2048,2048]{1,0:T(8,128)(2,1)}), bf16[256,2048]{1,0:T(8,128)(2,1)}) %reduce-scatter.9.cloned.1.call-update) | async-done | bytes 1048592 | tf_op jit(solution)/shard_map/reduce_scatter | solution.py:196
  996.9 10.5 convolution_convert_fusion.6
  1007.4 10.8 convolution_convert_fusion.4
  1018.2 7.3 convolution_convert_fusion.5
  1025.6 95.3 %all-gather.11.cloned.1.call-done = bf16[2048,2048]{1,0:T(8,128)(2,1)} async-done(((bf16[256,2048]{1,0:T(8,128)(2,1)}), bf16[2048,2048]{1,0:T(8,128)(2,1)}) %all-gather.11.cloned.1.call-update) | async-done | bytes 8388624 | tf_op jit(solution)/shard_map/all_gather | solution.py:204
  1120.9 5.8 convolution_convert_fusion.8
  1130.7 95.7 %while.29 = (s32[]{:T(128)}, f32[3072,256]{0,1:T(8,128)}, f32[3072,256]{0,1:T(8,128)}, f32[4,512,256]{2,1,0:T(8,128)}, s32[4]{0:T(128)S(1)}, /*index=5*/bf16[204...) while((s32[]{:T(128)}, f32[3072,256]{0,1:T(8,128)}, ...), condition=%wide.region_12.13_spmd, body=%wide.region_10.12_spmd.sunk | while | flops 2034238464 | bytes 86840768 | solution.py:249
  1239.7 7.1 convolution_convert_fusion.7
  1256.6 10.9 subtract_convert_fusion.1
  1278.8 10.6 convolution_convert_fusion.3
  1291.0 11.1 convolution_convert_fusion.1
  1303.2 213.2 %all-reduce.4.cloned.1.call-done = (bf16[2048,768]{1,0:T(8,128)(2,1)}, bf16[256,2048]{1,0:T(8,128)(2,1)}, bf16[2048,688]{0,1:T(8,128)(2,1)}, bf16[2048,688]{0,1:T(8,128)(2,1)}, bf16[688,2048]{1,0:T(8,128)(2,1)}) async-done(((bf16[2048,768]{1,0:T(8,128)(2,1)}, bf16[256,2048]{1,0:T(8,128)(2,1)}, bf16[2048,688]{0,1:T(8,128)(2,1)}, bf16[2048,688]{0,1:T(8,128)(2,1)}, bf16[688,2048]{1,0:T(8,128)(2,1)}), ...) | async-done | bytes 12648464 | tf_op jit(solution)/shard_map/psum | solution.py:277
  1532.2 137.5 %reduce-scatter.11.cloned.1.call-done = bf16[256,2048]{1,0:T(8,128)(2,1)} async-done(((bf16[2048,2048]{1,0:T(8,128)(2,1)}), bf16[256,2048]{1,0:T(8,128)(2,1)}) %reduce-scatter.11.cloned.1.call-update) | async-done | bytes 1048592 | tf_op jit(solution)/shard_map/reduce_scatter | solution.py:268
  1671.8 39.3 %all-reduce = (f32[2048]{0:T(1024)}, f32[2048]{0:T(1024)}, f32[3,9]{1,0:T(4,128)S(1)}, f32[9]{0:T(128)S(1)}) all-reduce(f32[2048]{0:T(1024)S(1)} %get-tuple-element.239, f32[2048]{0:T(1024)S(1)} %copy-done.42, f32[3,9]{1,0:T(4,128)S(1)} %fusion.37, f32[9]{0:T(128)S(1)} %convert_reduce_fusion), channel_id=1, replica_groups=mesh['dp'=4,'tensor'=8] {'dp','tensor'}, use_global_device_ids=true, to_apply=%region_16.17 | all-reduce | flops 4132 | bytes 33056 | tf_op jit(solution)/shard_map/psum | solution.py:300
  1711.7 5.2 fusion.23
  (377 shorter events, 259.7 us)
Async XLA Ops:
  7.2 658.1 %copy-start = (bf16[688,2048]{1,0:T(8,128)(2,1)S(1)}, bf16[688,2048]{1,0:T(8,128)(2,1)}, u32[]{:S(2)}) copy-start(bf16[688,2048]{1,0:T(8,128)(2,1)} %param.30) | copy-start | bytes 8454148
  7.2 132.0 %all-gather.5.cloned.1.call-start = ((), (), s32[]{:S(2)}) async-start(), calls=%async_computation.4 | async-start | bytes 9437184 | tf_op jit(solution)/shard_map/all_gather | solution.py:101
  11.5 400.7 %reduce-scatter.5.cloned.1.call-start = ((), (), s32[]{:S(2)}) async-start(), calls=%async_computation.5 | async-start | bytes 9437184 | tf_op jit(solution)/shard_map/reduce_scatter | solution.py:166
  11.5 11.7 collective-permute-start.1
  154.1 51.1 %collective-permute-start = (bf16[1024,256]{0,1:T(8,128)(2,1)}, bf16[1024,256]{0,1:T(8,128)(2,1)}, u32[]{:S(2)}, u32[]{:S(2)}) collective-permute-start(bf16[1024,256]{0,1:T(8,128)(2,1)} %slice.135), channel_id=1, source_target_pairs={{0,8},{8,16},{16,24},{1,9},{9,17},{17,25},{2,10},{10,18},{18,26},{... | collective-permute-start | bytes 1572872 | tf_op jit(solution)/shard_map/ppermute | solution.py:19
  183.6 24.3 %collective-permute-start.2 = (bf16[1024,256]{0,1:T(8,128)(2,1)}, bf16[1024,256]{0,1:T(8,128)(2,1)S(1)}, u32[]{:S(2)}, u32[]{:S(2)}) collective-permute-start(bf16[1024,256]{0,1:T(8,128)(2,1)} %bitcast.152), channel_id=1, source_target_pairs={{0,8},{8,16},{16,24},{1,9},{9,17},{17,25},{2,10},{10,18},{18,26},{... | collective-permute-start | bytes 1572872 | tf_op jit(solution)/shard_map/ppermute | solution.py:19
  265.8 148.6 %copy-start.39 = (f32[2048]{0:T(1024)S(1)}, f32[2048]{0:T(1024)}, u32[]{:S(2)}) copy-start(f32[2048]{0:T(1024)} %param.23) | copy-start | bytes 24580
  265.8 274.2 %all-gather.7.cloned.1.call-start = ((), (), s32[]{:S(2)}) async-start(), calls=%async_computation.6 | async-start | bytes 9437184 | tf_op jit(solution)/shard_map/all_gather | solution.py:174
  414.4 579.8 %copy-start.43 = (f32[256]{0:T(256)}, f32[256]{0:T(256)S(1)}, u32[]{:S(2)}) copy-start(f32[256]{0:T(256)S(1)} %add_rsqrt_fusion) | copy-start | bytes 3076
  415.9 249.4 %all-gather.9.cloned.1.call-start = ((), (), s32[]{:S(2)}) async-start(), calls=%async_computation.8 | async-start | bytes 9437184 | tf_op jit(solution)/shard_map/all_gather | solution.py:185
  416.5 421.8 %reduce-scatter.7.cloned.1.call-start = ((), (), s32[]{:S(2)}) async-start(), calls=%async_computation.7 | async-start | bytes 9437184 | tf_op jit(solution)/shard_map/reduce_scatter | solution.py:178
  690.9 298.9 %reduce-scatter.9.cloned.1.call-start = ((), (), s32[]{:S(2)}) async-start(), calls=%async_computation.9 | async-start | bytes 9437184 | tf_op jit(solution)/shard_map/reduce_scatter | solution.py:196
  692.7 12.2 copy-start.55
  692.7 12.2 copy-start.56
  717.5 272.4 %copy-start.4 = (bf16[256,2048]{1,0:T(8,128)(2,1)S(1)}, bf16[256,2048]{1,0:T(8,128)(2,1)}, u32[]{:S(2)}) copy-start(bf16[256,2048]{1,0:T(8,128)(2,1)} %param.20) | copy-start | bytes 3145732
  717.5 272.4 %copy-start.8 = (bf16[256,2048]{1,0:T(8,128)(2,1)S(1)}, bf16[256,2048]{1,0:T(8,128)(2,1)}, u32[]{:S(2)}) copy-start(bf16[256,2048]{1,0:T(8,128)(2,1)} %reduce-scatter.5.cloned.1.call-done) | copy-start | bytes 3145732
  717.5 277.2 %copy-start.15 = (bf16[256,2048]{1,0:T(8,128)(2,1)S(1)}, bf16[256,2048]{1,0:T(8,128)(2,1)}, u32[]{:S(2)}) copy-start(bf16[256,2048]{1,0:T(8,128)(2,1)} %param.31) | copy-start | bytes 3145732
  717.5 403.4 %all-gather.11.cloned.1.call-start = ((), (), s32[]{:S(2)}) async-start(), calls=%async_computation.10 | async-start | bytes 9437184 | tf_op jit(solution)/shard_map/all_gather | solution.py:204
  996.8 519.6 %all-reduce.4.cloned.1.call-start = ((), (), s32[]{:S(2)}) async-start(), calls=%async_computation.12 | async-start | bytes 25296896 | tf_op jit(solution)/shard_map/psum | solution.py:277
  996.8 21.4 %slice-start = ((s8[8388608]{0:T(1024)(128)(4,1)}), s8[4194304]{0:T(1024)(128)(4,1)S(1)}, s32[]{:S(2)}) async-start(s8[8388608]{0:T(1024)(128)(4,1)} %bitcast.156), calls=%async_computation.13 | async-start | bytes 8388608
  1018.2 102.6 %copy-start.31 = (bf16[256,2048]{1,0:T(8,128)(2,1)S(1)}, bf16[256,2048]{1,0:T(8,128)(2,1)}, u32[]{:S(2)}) copy-start(bf16[256,2048]{1,0:T(8,128)(2,1)} %param.27) | copy-start | bytes 3145732
  1236.9 39.2 %collective-permute-start.4 = (bf16[1024,256]{0,1:T(8,128)(2,1)}, bf16[1024,256]{0,1:T(8,128)(2,1)}, u32[]{:S(2)}, u32[]{:S(2)}) collective-permute-start(bf16[1024,256]{0,1:T(8,128)(2,1)} %slice.170), channel_id=1, source_target_pairs={{8,0},{16,8},{24,16},{9,1},{17,9},{25,17},{10,2},{18,10},{26,18},{... | collective-permute-start | bytes 1572872 | tf_op jit(solution)/shard_map/ppermute | solution.py:19
  1238.4 8.4 collective-permute-start.3
  1276.1 13.4 copy-start.29
  1289.5 380.2 %reduce-scatter.11.cloned.1.call-start = ((), (), s32[]{:S(2)}) async-start(), calls=%async_computation.11 | async-start | bytes 9437184 | tf_op jit(solution)/shard_map/reduce_scatter | solution.py:268
  1529.2 140.4 %copy-start.5 = (bf16[256,2048]{1,0:T(8,128)(2,1)S(1)}, bf16[256,2048]{1,0:T(8,128)(2,1)}, u32[]{:S(2)}) copy-start(bf16[256,2048]{1,0:T(8,128)(2,1)} %param.20) | copy-start | bytes 3145732
  1529.2 140.4 %copy-start.41 = (f32[2048]{0:T(1024)S(1)}, f32[2048]{0:T(1024)}, u32[]{:S(2)}) copy-start(f32[2048]{0:T(1024)} %param.22) | copy-start | bytes 24580
  1529.2 140.4 %copy-start.46 = (f32[256]{0:T(256)S(1)}, f32[256]{0:T(256)}, u32[]{:S(2)}) copy-start(f32[256]{0:T(256)} %copy-done.45) | copy-start | bytes 3076
  1529.3 142.5 %copy-start.42 = (f32[2048]{0:T(1024)S(1)}, f32[2048]{0:T(1024)}, u32[]{:S(2)}) copy-start(f32[2048]{0:T(1024)} %get-tuple-element.237) | copy-start | bytes 24580
  1529.3 182.4 %copy-start.40 = (f32[2048]{0:T(1024)S(1)}, f32[2048]{0:T(1024)}, u32[]{:S(2)}) copy-start(f32[2048]{0:T(1024)} %param.23) | copy-start | bytes 24580
  1529.3 182.4 %copy-start.44 = (f32[256]{0:T(256)S(1)}, f32[256]{0:T(256)}, u32[]{:S(2)}) copy-start(f32[256]{0:T(256)} %copy-done.43) | copy-start | bytes 3076
  1529.3 182.4 %copy-start.48 = (f32[256]{0:T(256)S(1)}, f32[256]{0:T(256)}, u32[]{:S(2)}) copy-start(f32[256]{0:T(256)} %copy-done.47) | copy-start | bytes 3076
  (53 other events, 233.7 us)
Sparse Core Ops, SparseCore 0:
  11.6 127.6 all-gather.4
  265.9 146.2 reduce-scatter.4
  416.0 123.9 all-gather.6
  542.2 123.1 all-gather.8
  691.0 147.2 reduce-scatter.6
  841.8 147.9 reduce-scatter.8
  996.9 123.9 all-gather.10
  1289.6 226.7 all-reduce.3
  1520.5 149.1 reduce-scatter.10
where the time goes:
time: 1730 us; the launch traced here: 1720 us
  waiting for transfers between devices  1210 us (70%)
  matrix products  195 us (11%)
  other arithmetic  123 us (7%)
  local copies, waits for them, and re-layouts  115 us (7%)
  blocking collectives  39.3 us (2%)
    psum x1, waiting for transfers between devices, shards(): lax.psum(grad_joint_w.astype(jnp.bfloat16), 'dp').astype(jnp.float32)  213 us
    reduce_scatter x1, waiting for transfers between devices, shards(): lax.psum_scatter((gate_part + contract_cols(grad_up_pre, w_up)).astype(jn...  152 us
    reduce_scatter x1, waiting for transfers between devices, shards(): lax.psum_scatter(jnp.dot(attn_low, w_out, preferred_element_type=jnp.floa...  146 us
    reduce_scatter x1, waiting for transfers between devices, shards(): lax.psum_scatter(contract_cols(grad_joint_in, w_joint).astype(jnp.bfloat1...  138 us
    all_gather x1, waiting for transfers between devices, shards(): lax.all_gather(h_normed.astype(jnp.bfloat16), 'tensor', axis=0, tiled=True)  123 us
    reduce_scatter x1, waiting for transfers between devices, shards(): lax.psum_scatter(jnp.dot(hidden, w_down, preferred_element_type=jnp.float...  120 us
    all_gather x1, waiting for transfers between devices, shards(): lax.all_gather(x_normed.astype(jnp.bfloat16), 'tensor', axis=0, tiled=True)  116 us
    all_gather x1, waiting for transfers between devices, shards(): gathered_dy = lax.all_gather(cotangent, 'tensor', axis=0, tiled=True)  107 us
  transfers between devices with their start and end apart: 14, of which 9 were waited for; matrix products, arithmetic and copies ran while one was open for 11% of the time, Pallas kernels for 0%

commit v1 on v0

v1 whole, which is shorter than its diff:
```python
import functools
import math

import jax
import jax.numpy as jnp
from jax import lax
from jax.experimental import pallas as pl
from jax.experimental.pallas import tpu as pltpu
from jax.sharding import PartitionSpec as P

HEAD_DIM = 128
WINDOW = 1024
EPS = 1e-06
NEG = -1e30
F32 = jnp.float32
BF16 = jnp.bfloat16
Q_BLK = 256
GROUP = 4


def ring_cycle(count):
    if count == 8:
        return [0, 2, 4, 6, 7, 5, 3, 1]
    width = 4 if count % 4 == 0 else count
    order = []
    for row in range(count // width):
        part = list(range(row * width, (row + 1) * width))
        order += part if row % 2 == 0 else part[::-1]
    return order


def group_cycles(count):
    base = [0, 2, 3, 1] if count == 8 else list(range(GROUP))
    return [[g * GROUP + b for b in base] for g in range(count // GROUP)]


def step_pairs(cycles, step):
    return [
        (cyc[i], cyc[(i + step) % len(cyc)]) for cyc in cycles for i in range(len(cyc))
    ]


def owner_of(cycles, rel):
    table = {}
    for cyc in cycles:
        for i, dev in enumerate(cyc):
            table[dev] = cyc[(i + rel) % len(cyc)]
    rows = jnp.array([table[t] for t in range(len(table))], jnp.int32)
    return rows[lax.axis_index("tensor")]


def rel_order(size):
    order = [0]
    for k in range(1, size // 2):
        order += [-k, k]
    return order + [size // 2]


def ring_gather(own, cycles):
    size = len(cycles[0])
    ahead, back = step_pairs(cycles, 1), step_pairs(cycles, -1)
    chunks = {0: own}
    f = b = own
    for k in range(1, size // 2):
        f = lax.ppermute(f, "tensor", ahead)
        b = lax.ppermute(b, "tensor", back)
        chunks[-k], chunks[k] = f, b
    half = own.shape[0] // 2
    f = lax.ppermute(f[:half], "tensor", ahead)
    b = lax.ppermute(b[half:], "tensor", back)
    chunks[size // 2] = jnp.concatenate([f, b], axis=0)
    return chunks


def ring_scatter(partial, cycles):
    size = len(cycles[0])
    ahead, back = step_pairs(cycles, 1), step_pairs(cycles, -1)
    far = partial(size // 2).astype(BF16)
    half = far.shape[0] // 2
    f = lax.ppermute(far[:half], "tensor", ahead)
    b = lax.ppermute(far[half:], "tensor", back)
    first = True
    for k in range(size // 2 - 1, 0, -1):
        pf, pb = partial(k), partial(-k)
        if first:
            pf = jnp.concatenate([pf[:half] + f.astype(F32), pf[half:]], axis=0)
            pb = jnp.concatenate([pb[:half], pb[half:] + b.astype(F32)], axis=0)
            first = False
        else:
            pf = pf + f.astype(F32)
            pb = pb + b.astype(F32)
        f = lax.ppermute(pf.astype(BF16), "tensor", ahead)
        b = lax.ppermute(pb.astype(BF16), "tensor", back)
    return partial(0) + f.astype(F32) + b.astype(F32)


def bits_of(count):
    bit, out = 1, []
    while bit < count:
        out.append(bit)
        bit *= 2
    return out


def swap(value, axis, bit):
    count = lax.axis_size(axis)
    return lax.ppermute(value, axis, [(d, d ^ bit) for d in range(count)])


def halves_scatter(value, axis):
    me = lax.axis_index("dp")
    for bit in bits_of(lax.axis_size("dp")):
        half = value.shape[axis] // 2
        side = (me // bit) % 2
        keep = lax.dynamic_slice_in_dim(value, side * half, half, axis)
        send = lax.dynamic_slice_in_dim(value, (1 - side) * half, half, axis)
        got = swap(send, "dp", bit)
        value = (keep.astype(F32) + got.astype(F32)).astype(BF16)
    return value


def halves_gather(value, axis):
    me = lax.axis_index("dp")
    for bit in reversed(bits_of(lax.axis_size("dp"))):
        other = swap(value, "dp", bit)
        side = (me // bit) % 2
        low = jnp.where(side == 0, value, other)
        high = jnp.where(side == 0, other, value)
        value = jnp.concatenate([low, high], axis=axis)
    return value


def own_part(value, axis):
    me = lax.axis_index("dp")
    for bit in bits_of(lax.axis_size("dp")):
        half = value.shape[axis] // 2
        value = lax.dynamic_slice_in_dim(value, ((me // bit) % 2) * half, half, axis)
    return value


def sum_all(value):
    for axis in ("dp", "tensor"):
        for bit in bits_of(lax.axis_size(axis)):
            value = value + swap(value, axis, bit)
    return value


def shifted(value, axis, steps):
    count = lax.axis_size(axis)
    leading, last = max(0, -steps), min(count, count - steps)
    return lax.ppermute(value, axis, [(s, s + steps) for s in range(leading, last)])


def norm_forward(values, gain):
    inverse = lax.rsqrt(jnp.mean(values * values, axis=-1, keepdims=True) + EPS)
    unit = values * inverse
    return unit * gain, unit, inverse


def norm_backward(grad, unit, inverse, gain):
    scaled = grad * gain
    inner = jnp.mean(scaled * unit, axis=-1, keepdims=True)
    return inverse * (scaled - unit * inner)


def dot_nn(a, b):
    return jnp.dot(a, b, preferred_element_type=F32)


def dot_tn(a, b):
    return lax.dot_general(a, b, (((0,), (0,)), ((), ())), preferred_element_type=F32)


def dot_nt(a, b):
    return lax.dot_general(a, b, (((1,), (1,)), ((), ())), preferred_element_type=F32)


def rope_tables(positions):
    half = HEAD_DIM // 2
    freq = jnp.exp(jnp.arange(half, dtype=F32) * (-2.0 * math.log(10000.0) / HEAD_DIM))
    angles = positions.astype(F32)[:, None] * freq[None, :]
    cos, sin = jnp.cos(angles), jnp.sin(angles)
    return jnp.concatenate([cos, cos], axis=1), jnp.concatenate([-sin, sin], axis=1)


def params(*sem):
    return pltpu.CompilerParams(
        dimension_semantics=sem or None, vmem_limit_bytes=56 * 1024 * 1024
    )


def qkv_body(idx, x_ref, wq, wk, wv, cos_ref, sin_ref, *rest):
    q_out, k_out, v_out, x_out = rest[-4:]
    x = x_ref[...]
    cos, sin = cos_ref[...], sin_ref[...]
    for w, out in ((wq, q_out), (wk, k_out)):
        p = dot_nn(x, w[...])
        for h in range(p.shape[1] // HEAD_DIM):
            cols = slice(h * HEAD_DIM, (h + 1) * HEAD_DIM)
            seg = p[:, cols]
            out[:, cols] = (seg * cos + pltpu.roll(seg, HEAD_DIM // 2, 1) * sin).astype(BF16)
    v_out[...] = dot_nn(x, wv[...]).astype(BF16)
    x_out[...] = x


def qkv_chunk(place, x, wq, wk, wv, cos, sin, bufs):
    rows, feats = x.shape
    cols = wq.shape[1]
    total = cos.shape[0]
    full = lambda shape: pl.BlockSpec(shape, lambda i, idx: (0, 0))
    at = lambda width: pl.BlockSpec((rows, width), lambda i, idx: (idx[0], 0))
    in_specs = [
        full((rows, feats)),
        full((feats, cols)),
        full((feats, cols)),
        full((feats, cols)),
        at(HEAD_DIM),
        at(HEAD_DIM),
    ]
    out_shape = [jax.ShapeDtypeStruct((total, cols), BF16)] * 3 + [
        jax.ShapeDtypeStruct((total, feats), BF16)
    ]
    args = [place.reshape(1), x, wq, wk, wv, cos, sin]
    aliases = {}
    if bufs is not None:
        in_specs += [pl.BlockSpec(memory_space=pl.ANY)] * 4
        args += list(bufs)
        aliases = {7 + i: i for i in range(4)}
    return pl.pallas_call(
        qkv_body,
        grid_spec=pltpu.PrefetchScalarGridSpec(
            num_scalar_prefetch=1,
            grid=(1,),
            in_specs=in_specs,
            out_specs=[at(cols)] * 3 + [at(feats)],
        ),
        out_shape=out_shape,
        input_output_aliases=aliases,
        compiler_params=params("arbitrary"),
        cost_estimate=pl.CostEstimate(
            flops=2 * rows * feats * cols * 3,
            bytes_accessed=2 * (feats * cols * 3 + rows * (2 * feats + 3 * cols)),
            transcendentals=0,
        ),
        name="qkv_chunk",
    )(*args)


LOG2E = 1.4426950408889634
SCALE = HEAD_DIM ** (-0.5)


def attend_body(q_ref, k0, k1, v0, v1, lo_ref, *rest):
    o_ref, ks, vs = rest[-3:]
    i = pl.program_id(1)
    span = Q_BLK + WINDOW

    @pl.when(i == 0)
    def _():
        ks[:WINDOW] = k0[...]
        ks[WINDOW:] = k1[...]
        vs[:WINDOW] = v0[...]
        vs[WINDOW:] = v1[...]

    start = pl.multiple_of(i * Q_BLK, Q_BLK)
    kb = ks[pl.ds(start, span), :]
    vb = vs[pl.ds(start, span), :]
    s = dot_nt(q_ref[...], kb) * (SCALE * LOG2E)
    col = lax.broadcasted_iota(jnp.int32, s.shape, 1)
    row = lax.broadcasted_iota(jnp.int32, s.shape, 0)
    lo = lo_ref[...] - start
    s = jnp.where((col >= lo) & (col <= row + WINDOW), s, NEG)
    p = jnp.exp2(s - jnp.max(s, axis=1, keepdims=True))
    total = jnp.sum(p, axis=1, keepdims=True)
    o = dot_nn(p.astype(BF16), vb) * (1.0 / total)
    o_ref[...] = o.astype(BF16)


def attend(half, q, k_pair, v_pair, lo, buf):
    total, cols = q.shape
    heads = cols // HEAD_DIM
    rows = total // 2
    blocks = rows // Q_BLK
    base = half * blocks
    q_spec = pl.BlockSpec((Q_BLK, HEAD_DIM), lambda h, i: (base + i, h))
    key_spec = lambda b: pl.BlockSpec((WINDOW, HEAD_DIM), lambda h, i: (b, h))
    lo_spec = pl.BlockSpec((Q_BLK, 1), lambda h, i: (base + i, 0))
    in_specs = [
        q_spec,
        key_spec(k_pair[0][1]),
        key_spec(k_pair[1][1]),
        key_spec(v_pair[0][1]),
        key_spec(v_pair[1][1]),
        lo_spec,
    ]
    args = [q, k_pair[0][0], k_pair[1][0], v_pair[0][0], v_pair[1][0], lo]
    aliases = {}
    if buf is not None:
        in_specs.append(pl.BlockSpec(memory_space=pl.ANY))
        args.append(buf)
        aliases = {6: 0}
    return pl.pallas_call(
        attend_body,
        grid=(heads, blocks),
        in_specs=in_specs,
        out_specs=q_spec,
        out_shape=jax.ShapeDtypeStruct((total, cols), BF16),
        scratch_shapes=[pltpu.VMEM((2 * WINDOW, HEAD_DIM), BF16)] * 2,
        input_output_aliases=aliases,
        compiler_params=params("arbitrary", "arbitrary"),
        cost_estimate=pl.CostEstimate(
            flops=4 * rows * (Q_BLK + WINDOW) * cols,
            bytes_accessed=2 * cols * 6 * WINDOW,
            transcendentals=rows * (Q_BLK + WINDOW) * heads,
        ),
        name="attend",
    )(*args)


def attend_back_body(q_ref, g_ref, k0, k1, v0, v1, lo_ref, cos_ref, sin_ref, *rest):
    dq_ref, dk_ref, dv_ref, ks, vs = rest[-5:]
    i = pl.program_id(1)
    span = Q_BLK + WINDOW

    @pl.when(i == 0)
    def _():
        ks[:WINDOW] = k0[...]
        ks[WINDOW:] = k1[...]
        vs[:WINDOW] = v0[...]
        vs[WINDOW:] = v1[...]
        dk_ref[...] = jnp.zeros_like(dk_ref)
        dv_ref[...] = jnp.zeros_like(dv_ref)

    start = pl.multiple_of(i * Q_BLK, Q_BLK)
    kb = ks[pl.ds(start, span), :]
    vb = vs[pl.ds(start, span), :]
    q, g = q_ref[...], g_ref[...]
    s = dot_nt(kb, q) * (SCALE * LOG2E)
    key = lax.broadcasted_iota(jnp.int32, s.shape, 0)
    row = lax.broadcasted_iota(jnp.int32, s.shape, 1)
    lo = lo_ref[...] - start
    s = jnp.where((key >= lo) & (key <= row + WINDOW), s, NEG)
    p = jnp.exp2(s - jnp.max(s, axis=0, keepdims=True))
    p = p * (1.0 / jnp.sum(p, axis=0, keepdims=True))
    dp = dot_nt(vb, g)
    inner = jnp.sum(p * dp, axis=0, keepdims=True)
    ds = (p * (dp - inner)).astype(BF16)
    dq = dot_tn(ds, kb) * SCALE
    dq = dq * cos_ref[...] - pltpu.roll(dq, HEAD_DIM // 2, 1) * sin_ref[...]
    dq_ref[...] = dq.astype(BF16)
    dk_ref[pl.ds(start, span), :] += dot_nn(ds, q) * SCALE
    dv_ref[pl.ds(start, span), :] += dot_nn(p.astype(BF16), g)


def attend_back(half, q, g, k_pair, v_pair, lo_row, cos, sin, buf):
    total, cols = q.shape
    heads = cols // HEAD_DIM
    rows = total // 2
    blocks = rows // Q_BLK
    base = half * blocks
    q_spec = pl.BlockSpec((Q_BLK, HEAD_DIM), lambda h, i: (base + i, h))
    key_spec = lambda b: pl.BlockSpec((WINDOW, HEAD_DIM), lambda h, i: (b, h))
    rope_spec = pl.BlockSpec((Q_BLK, HEAD_DIM), lambda h, i: (base + i, 0))
    lo_spec = pl.BlockSpec((1, Q_BLK), lambda h, i: (0, base + i))
    grad_spec = pl.BlockSpec((2 * WINDOW, HEAD_DIM), lambda h, i: (0, h))
    in_specs = [
        q_spec,
        q_spec,
        key_spec(k_pair[0][1]),
        key_spec(k_pair[1][1]),
        key_spec(v_pair[0][1]),
        key_spec(v_pair[1][1]),
        lo_spec,
        rope_spec,
        rope_spec,
    ]
    args = [q, g, k_pair[0][0], k_pair[1][0], v_pair[0][0], v_pair[1][0], lo_row, cos, sin]
    aliases = {}
    if buf is not None:
        in_specs.append(pl.BlockSpec(memory_space=pl.ANY))
        args.append(buf)
        aliases = {9: 0}
    return pl.pallas_call(
        attend_back_body,
        grid=(heads, blocks),
        in_specs=in_specs,
        out_specs=[
            pl.BlockSpec((Q_BLK, HEAD_DIM), lambda h, i: (base + i, 2 * heads + h)),
            grad_spec,
            grad_spec,
        ],
        out_shape=[
            jax.ShapeDtypeStruct((total, 3 * cols), BF16),
            jax.ShapeDtypeStruct((2 * WINDOW, cols), F32),
            jax.ShapeDtypeStruct((2 * WINDOW, cols), F32),
        ],
        scratch_shapes=[pltpu.VMEM((2 * WINDOW, HEAD_DIM), BF16)] * 2,
        input_output_aliases=aliases,
        compiler_params=params("arbitrary", "arbitrary"),
        cost_estimate=pl.CostEstimate(
            flops=10 * rows * (Q_BLK + WINDOW) * cols,
            bytes_accessed=2 * cols * 14 * WINDOW,
            transcendentals=rows * (Q_BLK + WINDOW) * heads,
        ),
        name="attend_back",
    )(*args)


def finish_body(half, ak, av, ok, ov, cos_ref, sin_ref, _, out_ref):
    cols = ak.shape[1]

    def write(gk, gv):
        for h in range(cols // HEAD_DIM):
            c = slice(h * HEAD_DIM, (h + 1) * HEAD_DIM)
            seg = gk[:, c]
            seg = seg * cos_ref[...] - pltpu.roll(seg, HEAD_DIM // 2, 1) * sin_ref[...]
            out_ref[:, c] = seg.astype(BF16)
        out_ref[:, cols:] = gv.astype(BF16)

    write(ak[...] + ok[...].astype(F32), av[...] + ov[...].astype(F32))


def finish_keys(half, ak, av, ok, ov, other_base, cos, sin, buf):
    cols = ak.shape[1]
    blk = 512
    n = WINDOW // blk
    base = half * n
    own = pl.BlockSpec((blk, cols), lambda i: (base + i, 0))
    oth = pl.BlockSpec((blk, cols), lambda i: (other_base * n + i, 0))
    rope = pl.BlockSpec((blk, HEAD_DIM), lambda i: (base + i, 0))
    return pl.pallas_call(
        functools.partial(finish_body, half),
        grid=(n,),
        in_specs=[own, own, oth, oth, rope, rope, pl.BlockSpec(memory_space=pl.ANY)],
        out_specs=pl.BlockSpec((blk, 2 * cols), lambda i: (base + i, 0)),
        out_shape=jax.ShapeDtypeStruct(buf.shape, BF16),
        input_output_aliases={6: 0},
        compiler_params=params("arbitrary"),
        name="finish_keys",
    )(ak, av, ok, ov, cos, sin, buf)


def shards(
    tokens, segments, attn_gain, ffn_gain, w_query, w_key, w_value, w_out, w_gate, w_up, w_down, cotangent
):
    rows, feats = tokens.shape
    n_tensor = lax.axis_size("tensor")
    n_dp = lax.axis_size("dp")
    block_len = rows * n_tensor
    head_cols = w_query.shape[1]
    dp_idx, t_idx = lax.axis_index("dp"), lax.axis_index("tensor")
    first_pos = dp_idx * block_len
    ring = [ring_cycle(n_tensor)]
    square = group_cycles(n_tensor)
    groups = n_tensor // GROUP

    x_f = tokens.astype(F32)
    x_normed, x_unit, x_inv = norm_forward(x_f, attn_gain)
    x_chunks = ring_gather(x_normed.astype(BF16), ring)

    cos, sin = rope_tables(first_pos + jnp.arange(block_len, dtype=jnp.int32))
    bufs = None
    for rel in rel_order(n_tensor):
        bufs = qkv_chunk(
            owner_of(ring, rel), x_chunks[rel], w_query, w_key, w_value, cos, sin, bufs
        )
    query, key, value, x_all = bufs

    prev_seg = shifted(segments[block_len - WINDOW :].astype(F32), "dp", 1).astype(jnp.int32)
    seg_all = jnp.concatenate([prev_seg, segments], axis=0)
    low_key = jnp.sum((seg_all[None, :] < segments[:, None]).astype(jnp.int32), axis=1)
    low_key = jnp.where(dp_idx == 0, jnp.maximum(low_key, WINDOW), low_key)
    spot = jnp.arange(block_len, dtype=jnp.int32)
    low_key = jnp.maximum(low_key, spot + 1)
    low_key = low_key - jnp.where(spot >= block_len // 2, block_len // 2, 0)
    low_col, low_row = low_key[:, None], low_key[None, :]

    tail = block_len - WINDOW
    prev_k = shifted(key[tail:], "dp", 1)
    prev_v = shifted(value[tail:], "dp", 1)
    k_late, v_late = ((key, 0), (key, 1)), ((value, 0), (value, 1))
    k_early, v_early = ((prev_k, 0), (key, 0)), ((prev_v, 0), (value, 0))
    heads_low = attend(1, query, k_late, v_late, low_col, None)
    heads_low = attend(0, query, k_early, v_early, low_col, heads_low)

    part = own_part(w_out, 0)
    out_chunks = ring_gather(part, ring)
    w_out_all = jnp.zeros((n_tensor,) + part.shape, BF16)
    for rel in rel_order(n_tensor):
        w_out_all = lax.dynamic_update_slice(
            w_out_all, out_chunks[rel][None], (owner_of(ring, rel), 0, 0)
        )
    w_out_all = halves_gather(w_out_all, 1).reshape(-1, feats)
    my_heads = lax.all_to_all(heads_low, "tensor", split_axis=0, concat_axis=1, tiled=True)
    attn_branch = dot_nn(my_heads, w_out_all)
    mid = x_f + attn_branch
    h_normed, h_unit, h_inv = norm_forward(mid, ffn_gain)

    def spread(value, axis):
        piece = own_part(value, axis)
        out = [value]
        for s in range(1, groups):
            pairs = [((t + s * GROUP) % n_tensor, t) for t in range(n_tensor)]
            out.append(halves_gather(lax.ppermute(piece, "tensor", pairs), axis))
        return out

    wg, wu, wd = spread(w_gate, 0), spread(w_up, 0), spread(w_down, 1)

    h_chunks = ring_gather(h_normed.astype(BF16), square)
    y_chunks = ring_gather(cotangent, square)
    hidden, g_gate, g_up = {}, {}, {}
    for rel in rel_order(GROUP):
        h, dy = h_chunks[rel], y_chunks[rel]
        hid, gg, gu = [], [], []
        for s in range(groups):
            gate, up = dot_nn(h, wg[s]), dot_nn(h, wu[s])
            gh = dot_nt(dy, wd[s])
            sig = jax.nn.sigmoid(gate)
            hid.append((gate * sig * up).astype(BF16))
            gg.append((gh * up * sig * (1.0 + gate * (1.0 - sig))).astype(BF16))
            gu.append((gh * gate * sig).astype(BF16))
        hidden[rel], g_gate[rel], g_up[rel] = hid, gg, gu

    def grad_h_part(rel):
        total = 0.0
        for s in range(groups):
            total = total + dot_nt(g_gate[rel][s], wg[s]) + dot_nt(g_up[rel][s], wu[s])
        return total

    def ffn_part(rel):
        total = 0.0
        for s in range(groups):
            total = total + dot_nn(hidden[rel][s], wd[s])
        return total

    grad_h = ring_scatter(grad_h_part, square)
    grad_mid = cotangent.astype(F32) + norm_backward(grad_h, h_unit, h_inv, ffn_gain)
    grad_ffn_gain = jnp.sum(grad_h * h_unit, axis=0)
    grad_mid_low = grad_mid.astype(BF16)
    my_grad_heads = dot_nt(grad_mid_low, w_out_all).astype(BF16)
    grad_heads = lax.all_to_all(my_grad_heads, "tensor", split_axis=1, concat_axis=0, tiled=True)

    d_joint, bk, bv = attend_back(
        0, query, grad_heads, k_early, v_early, low_row, cos, sin, None
    )
    got_k = shifted(bk[:WINDOW].astype(BF16), "dp", -1)
    got_v = shifted(bv[:WINDOW].astype(BF16), "dp", -1)
    d_joint, ak, av = attend_back(
        1, query, grad_heads, k_late, v_late, low_row, cos, sin, d_joint
    )
    d_joint = finish_keys(0, ak, av, bk, bv, 1, cos, sin, d_joint)
    d_joint = finish_keys(1, ak, av, got_k, got_v, 0, cos, sin, d_joint)
    w_joint = jnp.concatenate([w_key, w_value, w_query], axis=1)

    def grad_x_part(rel):
        mine = lax.dynamic_slice_in_dim(d_joint, owner_of(ring, rel) * rows, rows)
        return dot_nt(mine, w_joint)

    grad_x = ring_scatter(grad_x_part, ring)
    input_grad = (grad_mid + norm_backward(grad_x, x_unit, x_inv, attn_gain)).astype(BF16)

    ffn_branch = ring_scatter(ffn_part, square)
    result = mid + ffn_branch

    order = rel_order(GROUP)
    h_cat = jnp.concatenate([h_chunks[r] for r in order], axis=0)
    y_cat = jnp.concatenate([y_chunks[r] for r in order], axis=0)

    def reduce_ffn(parts, axis):
        own = None
        for s in range(groups):
            piece = halves_scatter(parts[s], axis)
            if s == 0:
                own = piece.astype(F32)
            else:
                pairs = [(t, (t + s * GROUP) % n_tensor) for t in range(n_tensor)]
                own = own + lax.ppermute(piece, "tensor", pairs).astype(F32)
        return halves_gather(own.astype(BF16), axis).astype(F32)

    def cat(parts, s):
        return jnp.concatenate([parts[r][s] for r in order], axis=0)

    grad_w_down = reduce_ffn(
        [dot_tn(cat(hidden, s), y_cat).astype(BF16) for s in range(groups)], 1
    )
    grad_w_gate = reduce_ffn(
        [dot_tn(h_cat, cat(g_gate, s)).astype(BF16) for s in range(groups)], 0
    )
    grad_w_up = reduce_ffn(
        [dot_tn(h_cat, cat(g_up, s)).astype(BF16) for s in range(groups)], 0
    )

    out_parts = dot_tn(my_heads, grad_mid_low).astype(BF16).reshape(n_tensor, head_cols, feats)
    out_parts = halves_scatter(out_parts, 1)

    def out_part(rel):
        return lax.dynamic_index_in_dim(
            out_parts, owner_of(ring, rel), 0, keepdims=False
        ).astype(F32)

    grad_w_out = halves_gather(ring_scatter(out_part, ring).astype(BF16), 0).astype(F32)

    joint_local = dot_tn(x_all, d_joint)
    grad_attn_gain = jnp.sum(joint_local * w_joint.astype(F32), axis=1) / attn_gain
    grad_joint = halves_gather(halves_scatter(joint_local.astype(BF16), 0), 0).astype(F32)

    slots = 2 * n_dp + 1
    own_seg = lax.dynamic_slice_in_dim(segments, t_idx * rows, rows)
    one_hot = (own_seg[:, None] == jnp.arange(slots, dtype=jnp.int32)[None, :]).astype(F32)
    per_row = jnp.stack(
        [
            jnp.sum(result * result, axis=1),
            jnp.sum(attn_branch * attn_branch, axis=1),
            jnp.sum(ffn_branch * ffn_branch, axis=1),
            jnp.ones((rows,), F32),
        ],
        axis=1,
    )
    table = jnp.dot(per_row.T, one_hot, precision=lax.Precision.HIGHEST, preferred_element_type=F32)
    packed = jnp.concatenate([grad_attn_gain, grad_ffn_gain, table.reshape(-1)])
    packed = jnp.pad(packed, (0, -packed.shape[0] % 1024)).reshape(-1, 128)
    packed = sum_all(packed).reshape(-1)
    sums = packed[2 * feats : 2 * feats + 4 * slots].reshape(4, slots)
    doc_rms = jnp.sqrt(sums[:3] / (jnp.maximum(sums[3:], 1.0) * feats))

    return (
        result.astype(BF16),
        input_grad,
        packed[:feats],
        packed[feats : 2 * feats],
        grad_joint[:, 2 * head_cols :],
        grad_joint[:, :head_cols],
        grad_joint[:, head_cols : 2 * head_cols],
        grad_w_out,
        grad_w_gate,
        grad_w_up,
        grad_w_down,
        doc_rms,
    )


def solution(mesh):
    both = P(("dp", "tensor"), None)
    col, row = P(None, "tensor"), P("tensor", None)
    return jax.shard_map(
        shards,
        mesh=mesh,
        in_specs=(both, P("dp"), P(), P(), col, col, col, row, col, col, row, both),
        out_specs=(both, both, P(), P(), col, col, col, row, col, col, row, P()),
        check_vma=False,
    )
```

time: 1730 us -> 935 us (0.54)
  waiting for transfers between devices: 1210 us -> 318 us
  starting transfers between devices: 11.9 us -> 123 us
  Pallas kernels: 0 us -> 99.2 us
  blocking collectives: 39.3 us -> 0 us
  matrix products: 195 us -> 156 us
  local copies, waits for them, and re-layouts: 115 us -> 88.8 us
    reduce_scatter x4 -> x0, waiting for transfers between devices: 556 us -> none  [the longest x1 152 us: shards(): lax.psum_scatter((gate_part + contract_cols(grad_up_pre, w_up)).astype(jn...]
    all_gather x4 -> x0, waiting for transfers between devices: 441 us -> none  [the longest x1 123 us: shards(): lax.all_gather(h_normed.astype(jnp.bfloat16), 'tensor', axis=0, tiled=True)]
    ppermute x5 -> x98, waiting for transfers between devices: 0.01 us -> 313 us  [the longest x39 91.7 us: swap(): return lax.ppermute(value, axis, [(d, d ^ bit) for d in range(count)])]
    psum x1 -> x0, waiting for transfers between devices: 213 us -> none  [shards(): lax.psum(grad_joint_w.astype(jnp.bfloat16), 'dp').astype(jnp.float32)]
    ppermute x5 -> x98, starting transfers between devices: 10.9 us -> 114 us  [the longest x8 31.5 us: ring_gather(): f = lax.ppermute(f, 'tensor', ahead)]
    pallas_call x0 -> x14, Pallas kernels: none -> 99.2 us  [the longest x8 36.3 us: qkv_chunk(): pl.pallas_call(qkv_body, grid_spec=pltpu.PrefetchScalarGridSpec(num_scala...]
    dot_general x43 -> x66, matrix products: 195 us -> 156 us  [the longest x33 57.3 us: dot_nt(): lax.dot_general(a, b, (((1,), (1,)), ((), ())), preferred_element_type=F32)]
    psum x1 -> x0, blocking collectives: 39.3 us -> none  [shards(): lax.psum((grad_attn_part, grad_ffn_part, doc_table, doc_count), ('dp', 't...]
  transfers between devices with their start and end apart: 14 -> 100, of which waited for: 9 -> 34; matrix products, arithmetic and copies ran while one was open for 11% -> 33% of each run, Pallas kernels for 0% -> 11%
where the time goes in v1:
time: 935 us; the launch traced here: 924 us
  waiting for transfers between devices  318 us (34%)
  matrix products  156 us (17%)
  starting transfers between devices  123 us (13%)
  other arithmetic  118 us (13%)
  Pallas kernels  99.2 us (11%)
  local copies, waits for them, and re-layouts  88.8 us (9%)
  between operations  21.7 us (2%)
    ppermute x39, waiting for transfers between devices, swap(): return lax.ppermute(value, axis, [(d, d ^ bit) for d in range(count)])  91.7 us
    ppermute x3, waiting for transfers between devices, reduce_ffn(): own = own + lax.ppermute(piece, 'tensor', pairs).astype(F32)  66.8 us
    ppermute x8, waiting for transfers between devices, ring_scatter(): f = lax.ppermute(pf.astype(BF16), 'tensor', ahead)  58.4 us
    dot_general x33, matrix products, dot_nt(): lax.dot_general(a, b, (((1,), (1,)), ((), ())), preferred_element_type=F32)  57.3 us
    dot_general x25, matrix products, dot_nn(): return jnp.dot(a, b, preferred_element_type=F32)  51 us
    dot_general x8, matrix products, dot_tn(): lax.dot_general(a, b, (((0,), (0,)), ((), ())), preferred_element_type=F32)  47.3 us
    ppermute x8, waiting for transfers between devices, ring_gather(): b = lax.ppermute(b, 'tensor', back)  44.5 us
    pallas_call x8, Pallas kernels, qkv_chunk(): pl.pallas_call(qkv_body, grid_spec=pltpu.PrefetchScalarGridSpec(num_scala...  36.3 us
  transfers between devices with their start and end apart: 100, of which 34 were waited for; matrix products, arithmetic and copies ran while one was open for 33% of the time, Pallas kernels for 11%

profile of v1, /device:TPU:0, one launch (start us, length us, event | category | flops | bytes accessed | tf_op | source)
XLA Modules:
  0.0 924.4 jit_solution(4520244828694856453)
XLA Ops:
  63.9 15.8 %collective-permute-done.13 = bf16[64,2048]{1,0:T(8,128)(2,1)S(1)} collective-permute-done((bf16[64,2048]{1,0:T(8,128)(2,1)}, bf16[64,2048]{1,0:T(8,128)(2,1)S(1)}, u32[]{:S(2)}, u32[]{:S(2)}) %collective-permute-start.13) | collective-permute-done | bytes 262176 | tf_op jit(solution)/shard_map/ppermute | solution.py:65
  79.6 22.3 %collective-permute-start.15 = (bf16[64,2048]{1,0:T(8,128)(2,1)S(1)}, bf16[64,2048]{1,0:T(8,128)(2,1)S(1)}, u32[]{:S(2)}, u32[]{:S(2)}) collective-permute-start(bf16[64,2048]{1,0:T(8,128)(2,1)S(1)} %collective-permute-done.13), channel_id=1, source_target_pairs={{0,2},{2,4},{4,6},{6,7},{7,5},{5,3},{3,1},{1,0},{8,10},{10,12},{12... | collective-permute-start | bytes 786440 | tf_op jit(solution)/shard_map/ppermute | solution.py:65
  128.2 26.0 %collective-permute-done.4.x_ref = bf16[256,2048]{1,0:T(8,128)(2,1)} collective-permute-done((bf16[256,2048]{1,0:T(8,128)(2,1)}, bf16[256,2048]{1,0:T(8,128)(2,1)}, u32[]{:S(2)}, u32[]{:S(2)}) %collective-permute-start.4) | collective-permute-done | bytes 1048608 | tf_op jit(solution)/shard_map/ppermute | solution.py:66
  156.3 18.2 %collective-permute-done.38 = bf16[256,2048]{1,0:T(8,128)(2,1)} collective-permute-done((bf16[256,2048]{1,0:T(8,128)(2,1)}, bf16[256,2048]{1,0:T(8,128)(2,1)}, u32[]{:S(2)}, u32[]{:S(2)}) %collective-permute-start.38) | collective-permute-done | bytes 1048608 | tf_op jit(solution)/shard_map/ppermute | solution.py:66
  206.2 6.9 collective-permute-done.22
  213.1 11.4 %collective-permute-done.25 = bf16[512,688]{0,1:T(8,128)(2,1)S(1)} collective-permute-done((bf16[512,688]{0,1:T(8,128)(2,1)S(1)}, bf16[512,688]{0,1:T(8,128)(2,1)S(1)}, u32[]{:S(2)}, u32[]{:S(2)}) %collective-permute-start.25) | collective-permute-done | bytes 704544 | tf_op jit(solution)/shard_map/ppermute | solution.py:107
  274.5 10.2 %attend.2.rest_0_ = bf16[2048,256]{1,0:T(8,128)(2,1)} custom-call(bf16[2048,256]{1,0:T(8,128)(2,1)} %get-tuple-element.78.q_ref, bf16[2048,256]{1,0:T(8,128)(2,1)} %get-tuple-element.79.k0.k1, bf16[2048,256]{1,0:T(8,128)(2,1)} %get-tuple-element.79.k0.k1, bf16[2048,256]{1,0:T(8,128)(2,1)} %get-tuple-element.80.v0.v1, ...), custom_call_target="tpu_custom_call" | custom-call | flops 1342177280 | bytes 3145728 | tf_op jit(solution)/shard_map/attend/pallas_call | solution.py:302
  286.3 10.2 %attend.3 = bf16[2048,256]{1,0:T(8,128)(2,1)} custom-call(bf16[2048,256]{1,0:T(8,128)(2,1)} %get-tuple-element.78.q_ref, bf16[1024,256]{1,0:T(8,128)(2,1)} %copy-done.80, bf16[2048,256]{1,0:T(8,128)(2,1)} %get-tuple-element.79.k0.k1, bf16[1024,256]{1,0:T(8,128)(2,1)} %copy-done.81, ...), custom_call_target="tpu_custom_call", output_to_operand_aliasing={{}: (6, {})} | custom-call | flops 1342177280 | bytes 3145728 | tf_op jit(solution)/shard_map/attend/pallas_call | solution.py:302
  322.0 5.4 all-to-all-done
  334.5 5.3 multiply_reduce_fusion.6
  364.5 8.4 pad_maximum_fusion
  431.6 5.6 convolution_convert_fusion.1
  437.3 5.5 convolution_convert_fusion.4
  447.8 5.5 convolution_convert_fusion.2
  458.3 5.7 convolution_convert_fusion.6
  465.3 5.5 convolution_convert_fusion.5
  472.1 5.5 convolution_convert_fusion.3
  500.1 32.7 %collective-permute-done.43 = bf16[256,2048]{1,0:T(8,128)(2,1)S(1)} collective-permute-done((bf16[256,2048]{1,0:T(8,128)(2,1)S(1)}, bf16[256,2048]{1,0:T(8,128)(2,1)S(1)}, u32[]{:S(2)}, u32[]{:S(2)}) %collective-permute-start.43) | collective-permute-done | bytes 1048608 | tf_op jit(solution)/shard_map/ppermute | solution.py:92
  564.9 17.2 %collective-permute-done.87 = bf16[512,688]{0,1:T(8,128)(2,1)} collective-permute-done((bf16[512,688]{0,1:T(8,128)(2,1)}, bf16[512,688]{0,1:T(8,128)(2,1)}, u32[]{:S(2)}, u32[]{:S(2)}) %collective-permute-start.87) | collective-permute-done | bytes 704544 | tf_op jit(solution)/shard_map/ppermute | solution.py:107
  584.7 12.3 %collective-permute-done.80 = bf16[512,688]{0,1:T(8,128)(2,1)S(1)} collective-permute-done((bf16[512,688]{0,1:T(8,128)(2,1)}, bf16[512,688]{0,1:T(8,128)(2,1)S(1)}, u32[]{:S(2)}, u32[]{:S(2)}) %collective-permute-start.80) | collective-permute-done | bytes 704544 | tf_op jit(solution)/shard_map/ppermute | solution.py:107
  601.4 42.6 %collective-permute-done.95 = bf16[688,512]{1,0:T(8,128)(2,1)} collective-permute-done((bf16[688,512]{1,0:T(8,128)(2,1)}, bf16[688,512]{1,0:T(8,128)(2,1)}, u32[]{:S(2)}, u32[]{:S(2)}) %collective-permute-start.95) | collective-permute-done | bytes 704544 | tf_op jit(solution)/shard_map/ppermute | solution.py:577
  646.4 12.6 %collective-permute-done.88 = bf16[512,688]{0,1:T(8,128)(2,1)} collective-permute-done((bf16[512,688]{0,1:T(8,128)(2,1)}, bf16[512,688]{0,1:T(8,128)(2,1)}, u32[]{:S(2)}, u32[]{:S(2)}) %collective-permute-start.88) | collective-permute-done | bytes 704544 | tf_op jit(solution)/shard_map/ppermute | solution.py:577
  662.3 11.7 %collective-permute-done.81 = bf16[512,688]{0,1:T(8,128)(2,1)} collective-permute-done((bf16[512,688]{0,1:T(8,128)(2,1)}, bf16[512,688]{0,1:T(8,128)(2,1)}, u32[]{:S(2)}, u32[]{:S(2)}) %collective-permute-start.81) | collective-permute-done | bytes 704544 | tf_op jit(solution)/shard_map/ppermute | solution.py:577
  677.1 17.6 %attend_back.2 = (bf16[2048,768]{1,0:T(8,128)(2,1)}, f32[2048,256]{1,0:T(8,128)}, f32[2048,256]{1,0:T(8,128)}) custom-call(bf16[2048,256]{1,0:T(8,128)(2,1)} %get-tuple-element.78.q_ref, bf16[2048,256]{1,0:T(8,128)(2,1)} %bitcast.25.g_ref, bf16[1024,256]{1,0:T(8,128)(2,1)} %copy-done.80, bf16[2048,256]{1,0:T(8,128)(2,1)} %get-tuple-element.79.k0.k1, ...), custom_call_target="tpu_custom_call" | custom-call | flops 3355443200 | bytes 7340032 | tf_op jit(solution)/shard_map/attend_back/pallas_call | solution.py:383
  698.5 17.8 %attend_back.3 = (bf16[2048,768]{1,0:T(8,128)(2,1)}, f32[2048,256]{1,0:T(8,128)}, f32[2048,256]{1,0:T(8,128)}) custom-call(bf16[2048,256]{1,0:T(8,128)(2,1)} %get-tuple-element.78.q_ref, bf16[2048,256]{1,0:T(8,128)(2,1)} %bitcast.25.g_ref, bf16[2048,256]{1,0:T(8,128)(2,1)} %get-tuple-element.79.k0.k1, ...), custom_call_target="tpu_custom_call", output_to_operand_aliasing={{0}: (9, {})} | custom-call | flops 3355443200 | bytes 7340032 | tf_op jit(solution)/shard_map/attend_back/pallas_call | solution.py:383
  735.7 10.4 %fusion.142 = (bf16[2048,768]{1,0:T(8,128)(2,1)S(1)}, f32[2048]{0:T(1024)S(1)}) fusion(bf16[2048,768]{1,0:T(8,128)(2,1)S(1)} %copy-done.15, bf16[2048,2048]{1,0:T(8,128)(2,1)} %get-tuple-element.87, bf16[2048,768]{1,0:T(8,128)(2,1)} %finish_keys.3), kind=kOutput, calls=%fused_computation.397 | convolution fusion | flops 6448740352 | bytes 17833984 | tf_op jit(solution)/shard_map/dot_general | solution.py:171
  767.2 9.2 collective-permute-done.48
  781.2 5.2 collective-permute-done.52
  828.3 12.3 %collective-permute-done.50 = bf16[256,2048]{1,0:T(8,128)(2,1)S(1)} collective-permute-done((bf16[256,2048]{1,0:T(8,128)(2,1)S(1)}, bf16[256,2048]{1,0:T(8,128)(2,1)S(1)}, u32[]{:S(2)}, u32[]{:S(2)}) %collective-permute-start.50) | collective-permute-done | bytes 1048608 | tf_op jit(solution)/shard_map/ppermute | solution.py:92
  845.7 22.1 %collective-permute-done.66 = bf16[8,64,2048]{2,1,0:T(8,128)(2,1)S(1)} collective-permute-done((bf16[8,64,2048]{2,1,0:T(8,128)(2,1)S(1)}, bf16[8,64,2048]{2,1,0:T(8,128)(2,1)S(1)}, u32[]{:S(2)}, u32[]{:S(2)}) %collective-permute-start.66) | collective-permute-done | bytes 2097184 | tf_op jit(solution)/shard_map/ppermute | solution.py:107
  870.9 12.8 %collective-permute-done.63 = bf16[512,768]{1,0:T(8,128)(2,1)S(1)} collective-permute-done((bf16[512,768]{1,0:T(8,128)(2,1)S(1)}, bf16[512,768]{1,0:T(8,128)(2,1)S(1)}, u32[]{:S(2)}, u32[]{:S(2)}) %collective-permute-start.63) | collective-permute-done | bytes 786464 | tf_op jit(solution)/shard_map/ppermute | solution.py:107
  886.2 5.0 collective-permute-done.68
  (708 shorter events, 488.0 us)
Async XLA Ops:
  2.9 55.5 %collective-permute-start.11 = (bf16[64,2048]{1,0:T(8,128)(2,1)}, bf16[64,2048]{1,0:T(8,128)(2,1)}, u32[]{:S(2)}, u32[]{:S(2)}) collective-permute-start(bf16[64,2048]{1,0:T(8,128)(2,1)} %get-tuple-element.97), channel_id=1, source_target_pairs={{0,2},{2,4},{4,6},{6,7},{7,5},{5,3},{3,1},{1,0},{8,10},{10,12},{12... | collective-permute-start | bytes 786440 | tf_op jit(solution)/shard_map/ppermute | solution.py:65
  6.0 54.1 %collective-permute-start.12 = (bf16[64,2048]{1,0:T(8,128)(2,1)}, bf16[64,2048]{1,0:T(8,128)(2,1)}, u32[]{:S(2)}, u32[]{:S(2)}) collective-permute-start(bf16[64,2048]{1,0:T(8,128)(2,1)} %get-tuple-element.97), channel_id=1, source_target_pairs={{0,1},{2,0},{4,2},{6,4},{7,6},{5,7},{3,5},{1,3},{8,9},{10,8},{12,1... | collective-permute-start | bytes 786440 | tf_op jit(solution)/shard_map/ppermute | solution.py:66
  7.6 119.2 %collective-permute-start = (bf16[256,2048]{1,0:T(8,128)(2,1)}, bf16[256,2048]{1,0:T(8,128)(2,1)}, u32[]{:S(2)}, u32[]{:S(2)}) collective-permute-start(bf16[256,2048]{1,0:T(8,128)(2,1)} %fusion.19.x_ref), channel_id=1, source_target_pairs={{0,2},{2,4},{4,6},{6,7},{7,5},{5,3},{3,1},{1,0},{8,10},{10,12},{12... | collective-permute-start | bytes 3145736 | tf_op jit(solution)/shard_map/ppermute | solution.py:65
  13.2 103.9 %collective-permute-start.21 = (bf16[512,688]{0,1:T(8,128)(2,1)}, bf16[512,688]{0,1:T(8,128)(2,1)}, u32[]{:S(2)}, u32[]{:S(2)}) collective-permute-start(bf16[512,688]{0,1:T(8,128)(2,1)} %constant_dynamic-slice_fusion.18), channel_id=1, source_target_pairs={{4,0},{5,1},{6,2},{7,3},{0,4},{1,5},{2,6},{3,7},{12,8},{13,9},{14,... | collective-permute-start | bytes 2113544 | tf_op jit(solution)/shard_map/ppermute | solution.py:504
  58.1 60.8 %collective-permute-start.27 = (bf16[688,512]{1,0:T(8,128)(2,1)}, bf16[688,512]{1,0:T(8,128)(2,1)}, u32[]{:S(2)}, u32[]{:S(2)}) collective-permute-start(bf16[688,512]{1,0:T(8,128)(2,1)} %constant_dynamic-slice_fusion.16), channel_id=1, source_target_pairs={{4,0},{5,1},{6,2},{7,3},{0,4},{1,5},{2,6},{3,7},{12,8},{13,9},{14,... | collective-permute-start | bytes 2113544 | tf_op jit(solution)/shard_map/ppermute | solution.py:504
  115.9 58.6 %collective-permute-start.38 = (bf16[256,2048]{1,0:T(8,128)(2,1)}, bf16[256,2048]{1,0:T(8,128)(2,1)}, u32[]{:S(2)}, u32[]{:S(2)}) collective-permute-start(bf16[256,2048]{1,0:T(8,128)(2,1)} %param.55), channel_id=1, source_target_pairs={{0,1},{2,0},{3,2},{1,3},{4,5},{6,4},{7,6},{5,7},{8,9},{10,8},{11,1... | collective-permute-start | bytes 3145736 | tf_op jit(solution)/shard_map/ppermute | solution.py:66
  117.2 57.3 %collective-permute-start.39 = (bf16[256,2048]{1,0:T(8,128)(2,1)}, bf16[256,2048]{1,0:T(8,128)(2,1)}, u32[]{:S(2)}, u32[]{:S(2)}) collective-permute-start(bf16[256,2048]{1,0:T(8,128)(2,1)} %param.55), channel_id=1, source_target_pairs={{0,2},{2,3},{3,1},{1,0},{4,6},{6,7},{7,5},{5,4},{8,10},{10,11},{11... | collective-permute-start | bytes 3145736 | tf_op jit(solution)/shard_map/ppermute | solution.py:65
  118.9 80.0 %collective-permute-start.19 = (bf16[8,64,2048]{2,1,0:T(8,128)(2,1)}, bf16[8,64,2048]{2,1,0:T(8,128)(2,1)}, u32[]{:S(2)}, u32[]{:S(2)}) collective-permute-start(bf16[8,64,2048]{2,1,0:T(8,128)(2,1)} %fusion.95), channel_id=1, source_target_pairs={{0,16},{8,24},{16,0},{24,8},{1,17},{9,25},{17,1},{25,9},{2,18},{10... | collective-permute-start | bytes 6291464 | tf_op jit(solution)/shard_map/ppermute | solution.py:107
  126.7 67.4 %collective-permute-start.24 = (bf16[512,688]{0,1:T(8,128)(2,1)S(1)}, bf16[512,688]{0,1:T(8,128)(2,1)S(1)}, u32[]{:S(2)}, u32[]{:S(2)}) collective-permute-start(bf16[512,688]{0,1:T(8,128)(2,1)S(1)} %constant_dynamic-slice_fusion.17), channel_id=1, source_target_pairs={{4,0},{5,1},{6,2},{7,3},{0,4},{1,5},{2,6},{3,7},{12,8},{13,9},{14,... | collective-permute-start | bytes 2113544 | tf_op jit(solution)/shard_map/ppermute | solution.py:504
  213.1 53.3 %collective-permute-start.29 = (bf16[688,1024]{1,0:T(8,128)(2,1)}, bf16[688,1024]{1,0:T(8,128)(2,1)}, u32[]{:S(2)}, u32[]{:S(2)}) collective-permute-start(bf16[688,1024]{1,0:T(8,128)(2,1)} %pad_maximum_fusion.8), channel_id=1, source_target_pairs={{0,8},{8,0},{16,24},{24,16},{1,9},{9,1},{17,25},{25,17},{2,10},{10... | collective-permute-start | bytes 4227080 | tf_op jit(solution)/shard_map/ppermute | solution.py:107
  224.6 105.2 %collective-permute-start.20 = (bf16[8,128,2048]{2,1,0:T(8,128)(2,1)}, bf16[8,128,2048]{2,1,0:T(8,128)(2,1)}, u32[]{:S(2)}, u32[]{:S(2)}) collective-permute-start(bf16[8,128,2048]{2,1,0:T(8,128)(2,1)} %pad_maximum_fusion.1), channel_id=1, source_target_pairs={{0,8},{8,0},{16,24},{24,16},{1,9},{9,1},{17,25},{25,17},{2,10},{10... | collective-permute-start | bytes 12582920 | tf_op jit(solution)/shard_map/ppermute | solution.py:107
  255.0 50.2 %collective-permute-start.26 = (bf16[1024,688]{0,1:T(8,128)(2,1)}, bf16[1024,688]{0,1:T(8,128)(2,1)}, u32[]{:S(2)}, u32[]{:S(2)}) collective-permute-start(bf16[1024,688]{0,1:T(8,128)(2,1)} %pad_maximum_fusion.7), channel_id=1, source_target_pairs={{0,8},{8,0},{16,24},{24,16},{1,9},{9,1},{17,25},{25,17},{2,10},{10... | collective-permute-start | bytes 4227080 | tf_op jit(solution)/shard_map/ppermute | solution.py:107
  255.0 53.9 %collective-permute-start.23 = (bf16[1024,688]{0,1:T(8,128)(2,1)}, bf16[1024,688]{0,1:T(8,128)(2,1)}, u32[]{:S(2)}, u32[]{:S(2)}) collective-permute-start(bf16[1024,688]{0,1:T(8,128)(2,1)} %pad_maximum_fusion.6), channel_id=1, source_target_pairs={{0,8},{8,0},{16,24},{24,16},{1,9},{9,1},{17,25},{25,17},{2,10},{10... | collective-permute-start | bytes 4227080 | tf_op jit(solution)/shard_map/ppermute | solution.py:107
  484.5 51.5 %collective-permute-start.35 = (bf16[256,2048]{1,0:T(8,128)(2,1)}, bf16[256,2048]{1,0:T(8,128)(2,1)S(1)}, u32[]{:S(2)}, u32[]{:S(2)}) collective-permute-start(bf16[256,2048]{1,0:T(8,128)(2,1)} %pad_maximum_fusion.15), channel_id=1, source_target_pairs={{0,2},{2,3},{3,1},{1,0},{4,6},{6,7},{7,5},{5,4},{8,10},{10,11},{11... | collective-permute-start | bytes 3145736 | tf_op jit(solution)/shard_map/ppermute | solution.py:92
  498.4 100.2 %collective-permute-start.92 = (bf16[688,512]{1,0:T(8,128)(2,1)}, bf16[688,512]{1,0:T(8,128)(2,1)}, u32[]{:S(2)}, u32[]{:S(2)}) collective-permute-start(bf16[688,512]{1,0:T(8,128)(2,1)} %constant_dynamic-slice_fusion.9), channel_id=1, source_target_pairs={{0,16},{8,24},{16,0},{24,8},{1,17},{9,25},{17,1},{25,9},{2,18},{10... | collective-permute-start | bytes 2113544 | tf_op jit(solution)/shard_map/ppermute | solution.py:107
  532.8 112.9 %collective-permute-start.85 = (bf16[512,688]{0,1:T(8,128)(2,1)}, bf16[512,688]{0,1:T(8,128)(2,1)}, u32[]{:S(2)}, u32[]{:S(2)}) collective-permute-start(bf16[512,688]{0,1:T(8,128)(2,1)} %constant_dynamic-slice_fusion.2), channel_id=1, source_target_pairs={{0,16},{8,24},{16,0},{24,8},{1,17},{9,25},{17,1},{25,9},{2,18},{10... | collective-permute-start | bytes 2113544 | tf_op jit(solution)/shard_map/ppermute | solution.py:107
  538.3 58.7 %collective-permute-start.80 = (bf16[512,688]{0,1:T(8,128)(2,1)}, bf16[512,688]{0,1:T(8,128)(2,1)S(1)}, u32[]{:S(2)}, u32[]{:S(2)}) collective-permute-start(bf16[512,688]{0,1:T(8,128)(2,1)} %constant_dynamic-slice_fusion.4), channel_id=1, source_target_pairs={{0,16},{8,24},{16,0},{24,8},{1,17},{9,25},{17,1},{25,9},{2,18},{10... | collective-permute-start | bytes 2113544 | tf_op jit(solution)/shard_map/ppermute | solution.py:107
  547.4 129.7 %all-to-all-start.1 = ((bf16[256,8,256]{2,0,1:T(8,128)(2,1)}), bf16[256,8,256]{2,0,1:T(8,128)(2,1)}, u32[]{:S(2)}, u32[]{:S(2)}) async-start(bf16[256,8,256]{2,0,1:T(8,128)(2,1)} %bitcast.207), calls=%async_computation.1 | async-start | bytes 2097152 | tf_op jit(solution)/shard_map/all_to_all | solution.py:541
  560.6 101.7 %collective-permute-start.78 = (bf16[512,688]{0,1:T(8,128)(2,1)S(1)}, bf16[512,688]{0,1:T(8,128)(2,1)}, u32[]{:S(2)}, u32[]{:S(2)}) collective-permute-start(bf16[512,688]{0,1:T(8,128)(2,1)S(1)} %copy-done.77), channel_id=1, source_target_pairs={{0,16},{8,24},{16,0},{24,8},{1,17},{9,25},{17,1},{25,9},{2,18},{10... | collective-permute-start | bytes 2113544 | tf_op jit(solution)/shard_map/ppermute | solution.py:107
  582.0 61.9 %collective-permute-start.95 = (bf16[688,512]{1,0:T(8,128)(2,1)}, bf16[688,512]{1,0:T(8,128)(2,1)}, u32[]{:S(2)}, u32[]{:S(2)}) collective-permute-start(bf16[688,512]{1,0:T(8,128)(2,1)} %add_convert_fusion.11), channel_id=1, source_target_pairs={{0,4},{1,5},{2,6},{3,7},{4,0},{5,1},{6,2},{7,3},{8,12},{9,13},{10,... | collective-permute-start | bytes 2113544 | tf_op jit(solution)/shard_map/ppermute | solution.py:577
  597.0 62.0 %collective-permute-start.88 = (bf16[512,688]{0,1:T(8,128)(2,1)}, bf16[512,688]{0,1:T(8,128)(2,1)}, u32[]{:S(2)}, u32[]{:S(2)}) collective-permute-start(bf16[512,688]{0,1:T(8,128)(2,1)} %add_convert_fusion.14), channel_id=1, source_target_pairs={{0,4},{1,5},{2,6},{3,7},{4,0},{5,1},{6,2},{7,3},{8,12},{9,13},{10,... | collective-permute-start | bytes 2113544 | tf_op jit(solution)/shard_map/ppermute | solution.py:577
  598.6 75.3 %collective-permute-start.81 = (bf16[512,688]{0,1:T(8,128)(2,1)}, bf16[512,688]{0,1:T(8,128)(2,1)}, u32[]{:S(2)}, u32[]{:S(2)}) collective-permute-start(bf16[512,688]{0,1:T(8,128)(2,1)} %add_convert_fusion.17), channel_id=1, source_target_pairs={{0,4},{1,5},{2,6},{3,7},{4,0},{5,1},{6,2},{7,3},{8,12},{9,13},{10,... | collective-permute-start | bytes 2113544 | tf_op jit(solution)/shard_map/ppermute | solution.py:577
  643.9 159.8 %collective-permute-start.65 = (bf16[8,128,2048]{2,1,0:T(8,128)(2,1)}, bf16[8,128,2048]{2,1,0:T(8,128)(2,1)}, u32[]{:S(2)}, u32[]{:S(2)}) collective-permute-start(bf16[8,128,2048]{2,1,0:T(8,128)(2,1)} %constant_dynamic-slice_fusion.13), channel_id=1, source_target_pairs={{0,8},{8,0},{16,24},{24,16},{1,9},{9,1},{17,25},{25,17},{2,10},{10... | collective-permute-start | bytes 12582920 | tf_op jit(solution)/shard_map/ppermute | solution.py:107
  645.7 74.2 %collective-permute-start.96 = (bf16[688,512]{1,0:T(8,128)(2,1)S(1)}, bf16[688,512]{1,0:T(8,128)(2,1)}, u32[]{:S(2)}, u32[]{:S(2)}) collective-permute-start(bf16[688,512]{1,0:T(8,128)(2,1)S(1)} %add_convert_fusion.10), channel_id=1, source_target_pairs={{0,16},{8,24},{16,0},{24,8},{1,17},{9,25},{17,1},{25,9},{2,18},{10... | collective-permute-start | bytes 2113544 | tf_op jit(solution)/shard_map/ppermute | solution.py:107
  661.7 62.3 %collective-permute-start.89 = (bf16[512,688]{0,1:T(8,128)(2,1)}, bf16[512,688]{0,1:T(8,128)(2,1)}, u32[]{:S(2)}, u32[]{:S(2)}) collective-permute-start(bf16[512,688]{0,1:T(8,128)(2,1)} %add_convert_fusion.13), channel_id=1, source_target_pairs={{0,16},{8,24},{16,0},{24,8},{1,17},{9,25},{17,1},{25,9},{2,18},{10... | collective-permute-start | bytes 2113544 | tf_op jit(solution)/shard_map/ppermute | solution.py:107
  676.5 52.1 %collective-permute-start.82 = (bf16[512,688]{0,1:T(8,128)(2,1)}, bf16[512,688]{0,1:T(8,128)(2,1)}, u32[]{:S(2)}, u32[]{:S(2)}) collective-permute-start(bf16[512,688]{0,1:T(8,128)(2,1)} %add_convert_fusion.16), channel_id=1, source_target_pairs={{0,16},{8,24},{16,0},{24,8},{1,17},{9,25},{17,1},{25,9},{2,18},{10... | collective-permute-start | bytes 2113544 | tf_op jit(solution)/shard_map/ppermute | solution.py:107
  723.9 63.7 %collective-permute-start.97 = (bf16[688,1024]{1,0:T(8,128)(2,1)}, bf16[688,1024]{1,0:T(8,128)(2,1)}, u32[]{:S(2)}, u32[]{:S(2)}) collective-permute-start(bf16[688,1024]{1,0:T(8,128)(2,1)} %pad_maximum_fusion.11), channel_id=1, source_target_pairs={{0,8},{8,0},{16,24},{24,16},{1,9},{9,1},{17,25},{25,17},{2,10},{10... | collective-permute-start | bytes 4227080 | tf_op jit(solution)/shard_map/ppermute | solution.py:107
  728.6 62.3 %collective-permute-start.90 = (bf16[1024,688]{0,1:T(8,128)(2,1)}, bf16[1024,688]{0,1:T(8,128)(2,1)}, u32[]{:S(2)}, u32[]{:S(2)}) collective-permute-start(bf16[1024,688]{0,1:T(8,128)(2,1)} %pad_maximum_fusion.10), channel_id=1, source_target_pairs={{0,8},{8,0},{16,24},{24,16},{1,9},{9,1},{17,25},{25,17},{2,10},{10... | collective-permute-start | bytes 4227080 | tf_op jit(solution)/shard_map/ppermute | solution.py:107
  731.4 88.7 %collective-permute-start.83 = (bf16[1024,688]{0,1:T(8,128)(2,1)}, bf16[1024,688]{0,1:T(8,128)(2,1)}, u32[]{:S(2)}, u32[]{:S(2)}) collective-permute-start(bf16[1024,688]{0,1:T(8,128)(2,1)} %pad_maximum_fusion.9), channel_id=1, source_target_pairs={{0,8},{8,0},{16,24},{24,16},{1,9},{9,1},{17,25},{25,17},{2,10},{10... | collective-permute-start | bytes 4227080 | tf_op jit(solution)/shard_map/ppermute | solution.py:107
  808.2 59.6 %collective-permute-start.66 = (bf16[8,64,2048]{2,1,0:T(8,128)(2,1)S(1)}, bf16[8,64,2048]{2,1,0:T(8,128)(2,1)S(1)}, u32[]{:S(2)}, u32[]{:S(2)}) collective-permute-start(bf16[8,64,2048]{2,1,0:T(8,128)(2,1)S(1)} %constant_dynamic-slice_fusion.12), channel_id=1, source_target_pairs={{0,16},{8,24},{16,0},{24,8},{1,17},{9,25},{17,1},{25,9},{2,18},{10... | collective-permute-start | bytes 6291464 | tf_op jit(solution)/shard_map/ppermute | solution.py:107
  826.7 56.9 %collective-permute-start.63 = (bf16[512,768]{1,0:T(8,128)(2,1)S(1)}, bf16[512,768]{1,0:T(8,128)(2,1)S(1)}, u32[]{:S(2)}, u32[]{:S(2)}) collective-permute-start(bf16[512,768]{1,0:T(8,128)(2,1)S(1)} %add_convert_fusion.9), channel_id=1, source_target_pairs={{0,16},{8,24},{16,0},{24,8},{1,17},{9,25},{17,1},{25,9},{2,18},{10... | collective-permute-start | bytes 2359304 | tf_op jit(solution)/shard_map/ppermute | solution.py:107
  841.6 51.3 %collective-permute-start.51 = (bf16[256,2048]{1,0:T(8,128)(2,1)S(1)}, bf16[256,2048]{1,0:T(8,128)(2,1)S(1)}, u32[]{:S(2)}, u32[]{:S(2)}) collective-permute-start(bf16[256,2048]{1,0:T(8,128)(2,1)S(1)} %fusion.15), channel_id=1, source_target_pairs={{0,2},{2,4},{4,6},{6,7},{7,5},{5,3},{3,1},{1,0},{8,10},{10,12},{12... | collective-permute-start | bytes 3145736 | tf_op jit(solution)/shard_map/ppermute | solution.py:92
  (209 other events, 2874.6 us)

commit v2 on v1

v2 whole, which is shorter than its diff:
```python
import functools
import math

import jax
import jax.numpy as jnp
from jax import lax
from jax.experimental import pallas as pl
from jax.experimental.pallas import tpu as pltpu
from jax.sharding import PartitionSpec as P

HEAD_DIM = 128
WINDOW = 1024
EPS = 1e-06
NEG = -1e30
F32 = jnp.float32
BF16 = jnp.bfloat16
Q_BLK = 256
COST_PART = 16
GROUP = 4


def ring_cycle(count):
    if count == 8:
        return [0, 2, 4, 6, 7, 5, 3, 1]
    width = 4 if count % 4 == 0 else count
    order = []
    for row in range(count // width):
        part = list(range(row * width, (row + 1) * width))
        order += part if row % 2 == 0 else part[::-1]
    return order


def group_cycles(count):
    base = [0, 2, 3, 1] if count == 8 else list(range(GROUP))
    return [[g * GROUP + b for b in base] for g in range(count // GROUP)]


def step_pairs(cycles, step):
    return [
        (cyc[i], cyc[(i + step) % len(cyc)]) for cyc in cycles for i in range(len(cyc))
    ]


def owners(cycles):
    table = {}
    for cyc in cycles:
        for i, dev in enumerate(cyc):
            table[dev] = [cyc[(i + rel) % len(cyc)] for rel in range(len(cyc))]
    rows = jnp.array([table[t] for t in range(len(table))], jnp.int32)
    return rows[lax.axis_index("tensor")]


def rel_order(size):
    order = [0]
    for k in range(1, size // 2):
        order += [-k, k]
    return order + [size // 2]


def after(value, *deps):
    return lax.optimization_barrier((value,) + deps)[0]


def together(*values):
    return lax.optimization_barrier(values)


class Gather:
    def __init__(self, own, cycles):
        self.size = len(cycles[0])
        self.ahead, self.back = step_pairs(cycles, 1), step_pairs(cycles, -1)
        self.f = self.b = own
        self.chunks = {0: [own]}
        self.k = 0

    def step(self, *deps):
        self.k += 1
        f, b = lax.optimization_barrier((self.f, self.b) + deps)[:2]
        if self.k < self.size // 2:
            self.f = lax.ppermute(f, "tensor", self.ahead)
            self.b = lax.ppermute(b, "tensor", self.back)
            self.chunks[-self.k], self.chunks[self.k] = [self.f], [self.b]
        else:
            half = self.f.shape[0] // 2
            self.f = lax.ppermute(f[:half], "tensor", self.ahead)
            self.b = lax.ppermute(b[half:], "tensor", self.back)
            self.chunks[self.k] = [self.f, self.b]

    def all(self):
        while self.k < self.size // 2:
            self.step()
        return self.chunks


class Scatter:
    def __init__(self, far, cycles):
        self.size = len(cycles[0])
        self.ahead, self.back = step_pairs(cycles, 1), step_pairs(cycles, -1)
        self.k = self.size // 2
        half = far.shape[0] // 2
        self.sent = lax.optimization_barrier((far[:half], far[half:]))
        self.send()

    def send(self):
        self.f = lax.ppermute(self.sent[0], "tensor", self.ahead)
        self.b = lax.ppermute(self.sent[1], "tensor", self.back)

    def step(self, near, first, *deps):
        f, b, near = lax.optimization_barrier((self.f, self.b, near) + deps)[:3]
        self.k -= 1
        self.sent = ring_add(near, f, b, first)
        self.send()


def bits_of(count):
    bit, out = 1, []
    while bit < count:
        out.append(bit)
        bit *= 2
    return out


def swap(value, axis, bit):
    count = lax.axis_size(axis)
    return lax.ppermute(value, axis, [(d, d ^ bit) for d in range(count)])


class Halves:
    def __init__(self, send, keep, axis):
        self.sent, self.keep, self.axis = send, keep, axis
        self.bits = bits_of(lax.axis_size("dp"))

    def send(self, *deps):
        self.sent = after(self.sent, *deps)
        self.got = swap(self.sent, "dp", self.bits[0])

    def add(self, *deps):
        got = after(self.got, *deps)
        self.bits = self.bits[1:]
        if self.bits:
            pair = half_add(self.keep, got, self.axis, dp_side(self.bits[0]))
            self.sent, self.keep = pair
            return self.keep
        self.value = plain_add(self.keep, got)
        return self.value

    def finish(self, *deps):
        self.add(*deps)
        while self.bits:
            self.send()
            self.add()
        return self.value


def dp_side(bit):
    side = (lax.axis_index("dp") // bit) % 2
    return jnp.stack([1 - side, side]).astype(jnp.int32)


def place_of(device, count):
    place = 0
    for bit in bits_of(count):
        place = place * 2 + (device // bit) % 2
    return place


def part_of(place, count):
    device = 0
    for bit in bits_of(count):
        device = device * 2 + place % 2
        place = place // 2
    return device


def all_dp(value):
    return lax.all_gather(value, "dp", axis=0, tiled=False)


def spread_parts(out, bits, *deps):
    for bit in bits:
        out = out + [(x ^ bit, swap(after(v, *deps), "dp", bit)) for x, v in out]
    return out


def sum_all(value):
    for axis in ("tensor", "dp"):
        for bit in bits_of(lax.axis_size(axis)):
            value = value + swap(value, axis, bit)
    return value


def shifted(value, axis, steps):
    count = lax.axis_size(axis)
    leading, last = max(0, -steps), min(count, count - steps)
    return lax.ppermute(value, axis, [(s, s + steps) for s in range(leading, last)])


def norm_forward(values, gain):
    inverse = lax.rsqrt(jnp.mean(values * values, axis=-1, keepdims=True) + EPS)
    unit = values * inverse
    return unit * gain, unit, inverse


def norm_backward(grad, unit, inverse, gain):
    scaled = grad * gain
    inner = jnp.mean(scaled * unit, axis=-1, keepdims=True)
    return inverse * (scaled - unit * inner)


def dot_nn(a, b):
    return jnp.dot(a, b, preferred_element_type=F32)


def dot_tn(a, b):
    return lax.dot_general(a, b, (((0,), (0,)), ((), ())), preferred_element_type=F32)


def dot_nt(a, b):
    return lax.dot_general(a, b, (((1,), (1,)), ((), ())), preferred_element_type=F32)


def rope_tables(positions):
    half = HEAD_DIM // 2
    freq = jnp.exp(jnp.arange(half, dtype=F32) * (-2.0 * math.log(10000.0) / HEAD_DIM))
    angles = positions.astype(F32)[:, None] * freq[None, :]
    cos, sin = jnp.cos(angles), jnp.sin(angles)
    return jnp.concatenate([cos, cos], axis=1), jnp.concatenate([-sin, sin], axis=1)


def cost(flops, bytes_accessed, transcendentals):
    return pl.CostEstimate(
        flops=flops // COST_PART,
        bytes_accessed=bytes_accessed // COST_PART,
        transcendentals=transcendentals // COST_PART,
    )


def params(*sem):
    return pltpu.CompilerParams(
        dimension_semantics=sem or None, vmem_limit_bytes=56 * 1024 * 1024
    )


ANY = pl.BlockSpec(memory_space=pl.ANY)


def qkv_body(n_in, idx, *refs):
    xs, refs = refs[:n_in], refs[n_in:]
    wq, wk, wv, cos_ref, sin_ref = refs[:5]
    q_out, kv_out, x_out = refs[-3:]
    at = 0
    for x in xs:
        x_out[at : at + x.shape[0], :] = x[...]
        at += x.shape[0]
    x = x_out[...]
    cos, sin = cos_ref[...], sin_ref[...]
    cols = wq.shape[1]
    for w, out in ((wq, q_out), (wk, kv_out)):
        p = dot_nn(x, w[...])
        for h in range(cols // HEAD_DIM):
            c = slice(h * HEAD_DIM, (h + 1) * HEAD_DIM)
            seg = p[:, c]
            out[:, c] = (seg * cos + pltpu.roll(seg, HEAD_DIM // 2, 1) * sin).astype(BF16)
    kv_out[:, cols:] = dot_nn(x, wv[...]).astype(BF16)


def qkv_chunk(places, rel, xs, wq, wk, wv, cos, sin, bufs):
    rows = sum(x.shape[0] for x in xs)
    feats, cols = wq.shape
    total = cos.shape[0]
    n_in = len(xs)
    full = lambda a: pl.BlockSpec(a.shape, lambda i, idx: (0, 0))
    at = lambda width: pl.BlockSpec((rows, width), lambda i, idx: (idx[rel], 0))
    args = list(xs) + [wq, wk, wv, cos, sin]
    in_specs = [full(a) for a in args[:-2]] + [at(HEAD_DIM)] * 2
    aliases = {}
    if bufs is not None:
        aliases = {1 + len(args) + i: i for i in range(3)}
        in_specs += [ANY] * 3
        args += list(bufs)
    widths = (cols, 2 * cols, feats)
    return pl.pallas_call(
        functools.partial(qkv_body, n_in),
        grid_spec=pltpu.PrefetchScalarGridSpec(
            num_scalar_prefetch=1,
            grid=(1,),
            in_specs=in_specs,
            out_specs=[at(w) for w in widths],
        ),
        out_shape=[jax.ShapeDtypeStruct((total, w), BF16) for w in widths],
        input_output_aliases=aliases,
        compiler_params=params("arbitrary"),
        cost_estimate=cost(
            flops=2 * rows * feats * cols * 3,
            bytes_accessed=2 * (feats * cols * 3 + rows * (2 * feats + 3 * cols)),
            transcendentals=0,
        ),
        name="qkv_chunk",
    )(places, *args)


def place_body(rels, idx, *refs):
    at = 0
    for rel, src in zip(rels, refs):
        rows = src.shape[0]
        refs[-1][idx[rel], at : at + rows, :] = src[...]
        at = (at + rows) % refs[-1].shape[1]


def place_chunks(places, chunks, count):
    rels = [rel % count for rel in rel_order(count) for _ in chunks[rel]]
    pieces = [c for rel in rel_order(count) for c in chunks[rel]]
    shape = (count,) + pieces[0].shape
    return pl.pallas_call(
        functools.partial(place_body, rels),
        grid_spec=pltpu.PrefetchScalarGridSpec(
            num_scalar_prefetch=1,
            grid=(1,),
            in_specs=[pl.BlockSpec(c.shape, lambda i, idx: (0, 0)) for c in pieces],
            out_specs=pl.BlockSpec(shape, lambda i, idx: (0, 0, 0)),
        ),
        out_shape=jax.ShapeDtypeStruct(shape, BF16),
        compiler_params=params("arbitrary"),
        name="place_chunks",
    )(places, *pieces)


def tn_cols_body(n, idx, a, b, send, keep):
    j = pl.program_id(0)
    out = dot_tn(a[...], b[...]).astype(BF16)

    @pl.when(j < n)
    def _():
        send[...] = out

    @pl.when(j >= n)
    def _():
        keep[...] = out


def half_place(n):
    return lambda j, idx: jnp.where(j < n, idx[0] * n + j, idx[1] * n + j - n)


def tn_cols(a, b):
    k, m = a.shape
    cols = b.shape[1]
    n = 2
    w = cols // (2 * n)
    at = half_place(n)
    return pl.pallas_call(
        functools.partial(tn_cols_body, n),
        grid_spec=pltpu.PrefetchScalarGridSpec(
            num_scalar_prefetch=1,
            grid=(2 * n,),
            in_specs=[
                pl.BlockSpec((k, m), lambda j, idx: (0, 0)),
                pl.BlockSpec((k, w), lambda j, idx: (0, at(j, idx))),
            ],
            out_specs=[
                pl.BlockSpec((m, w), lambda j, idx: (0, jnp.minimum(j, n - 1))),
                pl.BlockSpec((m, w), lambda j, idx: (0, jnp.maximum(j - n, 0))),
            ],
        ),
        out_shape=[jax.ShapeDtypeStruct((m, cols // 2), BF16)] * 2,
        compiler_params=params("arbitrary"),
        cost_estimate=cost(
            flops=2 * k * m * cols, bytes_accessed=2 * (k * m + k * cols + m * cols), transcendentals=0
        ),
        name="tn_cols",
    )(dp_side(1), a, b)


def tn_rows_body(n, idx, a, b, w, send, keep, sums):
    j = pl.program_id(0)
    out = dot_tn(a[...], b[...])
    sums[...] = jnp.sum(out * w[...].astype(F32), axis=1, keepdims=True)

    @pl.when(j < n)
    def _():
        send[...] = out.astype(BF16)

    @pl.when(j >= n)
    def _():
        keep[...] = out.astype(BF16)


def tn_rows(a, b, w):
    k, m = a.shape
    cols = b.shape[1]
    n = 2
    blk = m // (2 * n)
    at = half_place(n)
    return pl.pallas_call(
        functools.partial(tn_rows_body, n),
        grid_spec=pltpu.PrefetchScalarGridSpec(
            num_scalar_prefetch=1,
            grid=(2 * n,),
            in_specs=[
                pl.BlockSpec((k, blk), lambda j, idx: (0, at(j, idx))),
                pl.BlockSpec((k, cols), lambda j, idx: (0, 0)),
                pl.BlockSpec((blk, cols), lambda j, idx: (at(j, idx), 0)),
            ],
            out_specs=[
                pl.BlockSpec((blk, cols), lambda j, idx: (jnp.minimum(j, n - 1), 0)),
                pl.BlockSpec((blk, cols), lambda j, idx: (jnp.maximum(j - n, 0), 0)),
                pl.BlockSpec((blk, 1), lambda j, idx: (at(j, idx), 0)),
            ],
        ),
        out_shape=[jax.ShapeDtypeStruct((m // 2, cols), BF16)] * 2
        + [jax.ShapeDtypeStruct((m, 1), F32)],
        compiler_params=params("arbitrary"),
        cost_estimate=cost(
            flops=2 * k * m * cols, bytes_accessed=2 * (k * m + k * cols + m * cols), transcendentals=0
        ),
        name="tn_rows",
    )(dp_side(1), a, b, w)


def half_add_body(idx, keep, got, send_out, keep_out):
    j = pl.program_id(0)
    out = (keep[...].astype(F32) + got[...].astype(F32)).astype(BF16)

    @pl.when(j == 0)
    def _():
        send_out[...] = out

    @pl.when(j == 1)
    def _():
        keep_out[...] = out


def half_add(keep, got, axis, side):
    shape = list(keep.shape)
    shape[axis] //= 2
    place = lambda j, idx: (0, idx[j]) if axis == 1 else (idx[j], 0)
    one = pl.BlockSpec(tuple(shape), lambda j, idx: (0, 0))
    src = pl.BlockSpec(tuple(shape), place)
    return pl.pallas_call(
        half_add_body,
        grid_spec=pltpu.PrefetchScalarGridSpec(
            num_scalar_prefetch=1, grid=(2,), in_specs=[src, src], out_specs=[one, one]
        ),
        out_shape=[jax.ShapeDtypeStruct(tuple(shape), BF16)] * 2,
        compiler_params=params("arbitrary"),
        cost_estimate=cost(flops=keep.size, bytes_accessed=6 * keep.size, transcendentals=0),
        name="half_add",
    )(side, keep, got)


def plain_add_body(a, b, out):
    out[...] = (a[...].astype(F32) + b[...].astype(F32)).astype(BF16)


def plain_add(a, b):
    rows, cols = a.shape
    blk = pl.BlockSpec((rows // 2, cols), lambda j: (j, 0))
    return pl.pallas_call(
        plain_add_body,
        grid=(2,),
        in_specs=[blk, blk],
        out_specs=blk,
        out_shape=jax.ShapeDtypeStruct(a.shape, BF16),
        compiler_params=params("arbitrary"),
        cost_estimate=cost(flops=a.size, bytes_accessed=6 * a.size, transcendentals=0),
        name="plain_add",
    )(a, b)


def ring_add_body(first, near, f, b, f_out, b_out):
    rows = f_out.shape[0]
    at = 0 if first else rows
    ahead, behind = near[at : at + rows, :].astype(F32), near[rows - at : 2 * rows - at, :].astype(F32)
    n = f.shape[0]
    f_out[:n, :] = (ahead[:n] + f[...].astype(F32)).astype(BF16)
    b_out[rows - n :, :] = (behind[rows - n :] + b[...].astype(F32)).astype(BF16)
    if n < rows:
        f_out[n:, :] = ahead[n:].astype(BF16)
        b_out[: rows - n, :] = behind[: rows - n].astype(BF16)


def ring_add(near, f, b, first):
    rows, cols = near.shape[0] // 2, near.shape[1]
    whole = lambda a: pl.BlockSpec(a.shape, lambda i: (0, 0))
    return pl.pallas_call(
        functools.partial(ring_add_body, first),
        grid=(1,),
        in_specs=[whole(near), whole(f), whole(b)],
        out_specs=[pl.BlockSpec((rows, cols), lambda i: (0, 0))] * 2,
        out_shape=[jax.ShapeDtypeStruct((rows, cols), BF16)] * 2,
        compiler_params=params("arbitrary"),
        cost_estimate=cost(flops=near.size, bytes_accessed=8 * near.size, transcendentals=0),
        name="ring_add",
    )(near, f, b)


def grad_x_body(idx, rows, w, out):
    out[...] = dot_nt(rows[...], w[...]).astype(out.dtype)


def grad_x_terms(places, rels, d_joint, w_joint, rows, kind):
    feats, cols = w_joint.shape
    step = rels[-1] - rels[0]
    return pl.pallas_call(
        grad_x_body,
        grid_spec=pltpu.PrefetchScalarGridSpec(
            num_scalar_prefetch=1,
            grid=(len(rels),),
            in_specs=[
                pl.BlockSpec((rows, cols), lambda j, idx: (idx[rels[0] + j * step], 0)),
                pl.BlockSpec((feats, cols), lambda j, idx: (0, 0)),
            ],
            out_specs=pl.BlockSpec((rows, feats), lambda j, idx: (j, 0)),
        ),
        out_shape=jax.ShapeDtypeStruct((len(rels) * rows, feats), kind),
        compiler_params=params("arbitrary"),
        cost_estimate=cost(
            flops=2 * rows * feats * cols * len(rels), bytes_accessed=2 * feats * cols, transcendentals=0
        ),
        name="grad_x_terms",
    )(places, d_joint, w_joint)


def input_grad_body(own, f, b, mid, x_ref, gain, out):
    grad = own[...] + f[...].astype(F32) + b[...].astype(F32)
    x = x_ref[...].astype(F32)
    inverse = lax.rsqrt(jnp.mean(x * x, axis=-1, keepdims=True) + EPS)
    unit = x * inverse
    scaled = grad * gain[...]
    inner = jnp.mean(scaled * unit, axis=-1, keepdims=True)
    out[...] = (mid[...] + inverse * (scaled - unit * inner)).astype(BF16)


def input_grad_of(own, f, b, mid, tokens, gain):
    rows, feats = tokens.shape
    blk = pl.BlockSpec((rows // 2, feats), lambda i: (i, 0))
    return pl.pallas_call(
        input_grad_body,
        grid=(2,),
        in_specs=[blk] * 5 + [pl.BlockSpec((1, feats), lambda i: (0, 0))],
        out_specs=blk,
        out_shape=jax.ShapeDtypeStruct((rows, feats), BF16),
        compiler_params=params("arbitrary"),
        cost_estimate=cost(flops=9 * rows * feats, bytes_accessed=14 * rows * feats, transcendentals=0),
        name="input_grad",
    )(own, f, b, mid, tokens, gain.reshape(1, -1))


def shard_sum_body(n_back, units, pad, value, *refs):
    out = refs[-1]
    total = value[:units, :].astype(F32)
    for back in refs[:n_back]:
        total = total + back[...].astype(F32)
    out[...] = total.astype(BF16)


def shard_sum(value, backs, units):
    whole = lambda a: pl.BlockSpec(a.shape, lambda i: (0, 0))
    return pl.pallas_call(
        functools.partial(shard_sum_body, len(backs), units, 0),
        grid=(1,),
        in_specs=[whole(a) for a in (value, *backs)],
        out_specs=pl.BlockSpec((units, value.shape[1]), lambda i: (0, 0)),
        out_shape=jax.ShapeDtypeStruct((units, value.shape[1]), BF16),
        compiler_params=params("arbitrary"),
        cost_estimate=cost(flops=value.size, bytes_accessed=4 * value.size, transcendentals=0),
        name="shard_sum",
    )(value, *backs)


def widen_body(src, *outs):
    at = 0
    for out in outs:
        out[...] = src[0, :, at : at + out.shape[1]].astype(F32)
        at += out.shape[1]


def widen_pieces_body(n, idx, *refs):
    p = pl.program_id(0)
    outs = refs[n:]
    for i, src in enumerate(refs[:n]):

        @pl.when(p == i)
        def _():
            at = 0
            for out in outs:
                out[...] = src[:, at : at + out.shape[1]].astype(F32)
                at += out.shape[1]


def widen_pieces(places, pieces, widths):
    n = len(pieces)
    rows, cols = pieces[0].shape
    return pl.pallas_call(
        functools.partial(widen_pieces_body, n),
        grid_spec=pltpu.PrefetchScalarGridSpec(
            num_scalar_prefetch=1,
            grid=(n,),
            in_specs=[pl.BlockSpec((rows, cols), lambda p, idx: (0, 0))] * n,
            out_specs=[pl.BlockSpec((rows, w), lambda p, idx: (idx[p], 0)) for w in widths],
        ),
        out_shape=[jax.ShapeDtypeStruct((n * rows, w), F32) for w in widths],
        compiler_params=params("arbitrary"),
        name="widen_pieces",
    )(places, *pieces)


def widen_cols(got):
    n_dp, rows, cols = got.shape
    return pl.pallas_call(
        widen_body,
        grid=(n_dp,),
        in_specs=[pl.BlockSpec((1, rows, cols), lambda p: (part_of(p, n_dp), 0, 0))],
        out_specs=[pl.BlockSpec((rows, cols), lambda p: (0, p))],
        out_shape=[jax.ShapeDtypeStruct((rows, n_dp * cols), F32)],
        compiler_params=params("arbitrary"),
        name="widen_cols",
    )(got)[0]


def parts_ready(p, srcs, parts, sems):
    copies = [pltpu.make_async_copy(w, parts.at[i], sems.at[i]) for i, w in enumerate(srcs)]

    @pl.when(p == 0)
    def _():
        for c in copies:
            c.start()

    for i, c in enumerate(copies):

        @pl.when(p == i)
        def _():
            c.wait()


def out_body(n_dp, idx, heads, x_ref, gain, *refs):
    srcs, (branch_out, mid_out, h_out, heads_out, parts, sems) = refs[:n_dp], refs[n_dp:]
    p = pl.program_id(0)
    n_t, rows, cols = heads.shape
    width = parts.shape[2]
    parts_ready(p, srcs, parts, sems)

    @pl.when(p == 0)
    def _():
        for t in range(n_t):
            heads_out[:, t * cols : (t + 1) * cols] = heads[t]

    part = pl.ds(pl.multiple_of(idx[p] * width, width), width)
    branch_out[:, part] = dot_nn(heads_out[...], parts[p])

    @pl.when(p == n_dp - 1)
    def _():
        mid = x_ref[...].astype(F32) + branch_out[...]
        mid_out[...] = mid
        inverse = lax.rsqrt(jnp.mean(mid * mid, axis=-1, keepdims=True) + EPS)
        h_out[...] = (mid * inverse * gain[...]).astype(BF16)


def out_project(heads, w_places, w_parts, tokens, gain):
    n_dp = len(w_parts)
    feats_in, width = w_parts[0].shape
    rows, feats = tokens.shape
    full = lambda shape: pl.BlockSpec(shape, lambda p, idx: (0,) * len(shape))
    sq = (rows, feats)
    return pl.pallas_call(
        functools.partial(out_body, n_dp),
        grid_spec=pltpu.PrefetchScalarGridSpec(
            num_scalar_prefetch=1,
            grid=(n_dp,),
            in_specs=[full(heads.shape), full(sq), full((1, feats))] + [ANY] * n_dp,
            out_specs=[full(sq)] * 4,
            scratch_shapes=[
                pltpu.VMEM((n_dp, feats_in, width), BF16),
                pltpu.SemaphoreType.DMA((n_dp,)),
            ],
        ),
        out_shape=[
            jax.ShapeDtypeStruct(sq, F32),
            jax.ShapeDtypeStruct(sq, F32),
            jax.ShapeDtypeStruct(sq, BF16),
            jax.ShapeDtypeStruct((rows, feats_in), BF16),
        ],
        compiler_params=params("arbitrary"),
        cost_estimate=cost(
            flops=2 * rows * feats * feats_in,
            bytes_accessed=2 * feats * feats_in + 16 * rows * feats,
            transcendentals=0,
        ),
        name="out_project",
    )(w_places, heads, tokens, gain.reshape(1, -1), *w_parts)


def out_back_body(n_dp, idx, own, f, b, mid_ref, dy, gain, *refs):
    srcs, (mid_out, low_out, gain_out, heads_out, acc, parts, sems) = refs[:n_dp], refs[n_dp:]
    p = pl.program_id(0)
    n_t, rows, cols = heads_out.shape
    width = parts.shape[2]
    parts_ready(p, srcs, parts, sems)

    @pl.when(p == 0)
    def _():
        grad = own[...] + f[...].astype(F32) + b[...].astype(F32)
        mid = mid_ref[...]
        inverse = lax.rsqrt(jnp.mean(mid * mid, axis=-1, keepdims=True) + EPS)
        unit = mid * inverse
        gain_out[...] = jnp.sum(grad * unit, axis=0, keepdims=True)
        scaled = grad * gain[...]
        inner = jnp.mean(scaled * unit, axis=-1, keepdims=True)
        total = dy[...].astype(F32) + inverse * (scaled - unit * inner)
        mid_out[...] = total
        low_out[...] = total.astype(BF16)
        acc[...] = jnp.zeros_like(acc)

    part = pl.ds(pl.multiple_of(idx[p] * width, width), width)
    acc[...] += dot_nt(low_out[:, part], parts[p])

    @pl.when(p == n_dp - 1)
    def _():
        for t in range(n_t):
            heads_out[t] = acc[:, t * cols : (t + 1) * cols].astype(BF16)


def out_back(own, f, b, mid, dy, gain, w_places, w_parts, n_t):
    n_dp = len(w_parts)
    feats_in, width = w_parts[0].shape
    rows, feats = mid.shape
    full = lambda shape: pl.BlockSpec(shape, lambda p, idx: (0,) * len(shape))
    sq = (rows, feats)
    heads = (n_t, rows, feats_in // n_t)
    return pl.pallas_call(
        functools.partial(out_back_body, n_dp),
        grid_spec=pltpu.PrefetchScalarGridSpec(
            num_scalar_prefetch=1,
            grid=(n_dp,),
            in_specs=[full(sq)] * 5 + [full((1, feats))] + [ANY] * n_dp,
            out_specs=[full(sq), full(sq), full((1, feats)), full(heads)],
            scratch_shapes=[
                pltpu.VMEM((rows, feats_in), F32),
                pltpu.VMEM((n_dp, feats_in, width), BF16),
                pltpu.SemaphoreType.DMA((n_dp,)),
            ],
        ),
        out_shape=[
            jax.ShapeDtypeStruct(sq, F32),
            jax.ShapeDtypeStruct(sq, BF16),
            jax.ShapeDtypeStruct((1, feats), F32),
            jax.ShapeDtypeStruct(heads, BF16),
        ],
        compiler_params=params("arbitrary"),
        cost_estimate=cost(
            flops=2 * rows * feats * feats_in,
            bytes_accessed=2 * feats * feats_in + 20 * rows * feats,
            transcendentals=0,
        ),
        name="out_back",
    )(w_places, own, f, b, mid, dy, gain.reshape(1, -1), *w_parts)


def ffn_body(n_in, n_w, first, units, n_buf, *refs):
    hs, refs = refs[:n_in], refs[n_in:]
    ys, refs = refs[:n_in], refs[n_in:]
    srcs, refs = refs[:n_w], refs[n_w:]
    if first:
        refs = refs[n_buf:]
        h_out, y_out, refs = refs[0], refs[1], refs[2:]
    else:
        dh_in, refs = refs[0], refs[1 + n_buf :]
    hid_out, gg_out, gu_out, dh_ref, weights, sems = refs[:6]
    waits = []
    for j in range(3):
        if first:
            waits.append([pltpu.make_async_copy(srcs[j], weights.at[j], sems.at[j])])
            continue
        src = srcs[j]
        n_dp, _, width = src.shape
        waits.append(
            [
                pltpu.make_async_copy(
                    src.at[p], weights.at[j, :, pl.ds(p * width, width)], sems.at[j]
                )
                for p in range(n_dp)
            ]
        )
    for group in waits:
        for c in group:
            c.start()

    def ready(j):
        for c in waits[j]:
            c.wait()
        return weights[j]

    if not first:
        h_out, y_out = refs[6:]
    at = 0
    for h, y in zip(hs, ys):
        h_out[at : at + h.shape[0], :] = h[...]
        y_out[at : at + h.shape[0], :] = y[...]
        at += h.shape[0]
    gate = dot_nt(h_out[...], ready(0))
    up = dot_nt(h_out[...], ready(1))
    gh = dot_nt(y_out[...], ready(2))
    sig = jax.nn.sigmoid(gate)
    act = gate * sig
    hid_out[:, :units] = (act * up).astype(BF16)
    gg = (gh * up * (sig + act * (1.0 - sig))).astype(BF16)
    gu = (gh * act).astype(BF16)
    gg_out[:, :units] = gg
    gu_out[:, :units] = gu
    pad = hid_out.shape[1] - units
    if pad > 0:
        for o in (hid_out, gg_out, gu_out):
            o[:, units:] = jnp.zeros((o.shape[0], pad), BF16)
    part = dot_nn(gg, weights[0]) + dot_nn(gu, weights[1])
    if not first:
        part = part + dh_in[...]
    dh_ref[...] = part


def ffn_set(hs, ys, srcs, units, shard, shards, total, place, dh, bufs):
    n_in, n_w, first = len(hs), len(srcs), shard == 0
    feats = hs[0].shape[1]
    m = sum(h.shape[0] for h in hs)
    pad = -(-units // 128) * 128
    whole = lambda a: pl.BlockSpec(a.shape, lambda i: (0, 0))
    args = list(hs) + list(ys) + list(srcs)
    in_specs = [whole(a) for a in args[: 2 * n_in]] + [ANY] * n_w
    if not first:
        args.append(dh)
        in_specs.append(whole(dh))
    out_specs = [pl.BlockSpec((m, pad), lambda i: (place, shard))] * 3
    out_shape = [jax.ShapeDtypeStruct((total, pad * shards), BF16)] * 3
    held = list(bufs[2:])
    if first:
        out_specs = [pl.BlockSpec((m, feats), lambda i: (place, 0))] * 2 + out_specs
        out_shape = [jax.ShapeDtypeStruct((total, feats), BF16)] * 2 + out_shape
        held = list(bufs)
    aliases = {len(args) + i: i for i in range(len(held))}
    args += held
    in_specs += [ANY] * len(held)
    scratch = [pltpu.VMEM((3, units, feats), BF16), pltpu.SemaphoreType.DMA((3,))]
    if not first:
        scratch += [pltpu.VMEM((m, feats), BF16)] * 2
    out = pl.pallas_call(
        functools.partial(ffn_body, n_in, n_w, first, units, len(held)),
        grid=(1,),
        in_specs=in_specs,
        out_specs=out_specs + [pl.BlockSpec((m, feats), lambda i: (0, 0))],
        out_shape=out_shape + [jax.ShapeDtypeStruct((m, feats), F32)],
        scratch_shapes=scratch,
        input_output_aliases=aliases,
        compiler_params=params("arbitrary"),
        cost_estimate=cost(
            flops=10 * m * feats * units,
            bytes_accessed=6 * feats * units + 16 * m * feats,
            transcendentals=m * units,
        ),
        name="ffn_set",
    )(*args)
    new, dh = list(out[:-1]), out[-1]
    return (new if first else list(bufs[:2]) + new), dh


def down_body(n_got, units, hid, own, *refs):
    got, (out, weights, sems) = refs[:n_got], refs[n_got:]
    waits = [[pltpu.make_async_copy(own, weights.at[0], sems.at[0])]]
    for s, src in enumerate(got):
        n_dp, _, width = src.shape
        waits.append(
            [
                pltpu.make_async_copy(
                    src.at[p], weights.at[s + 1, :, pl.ds(p * width, width)], sems.at[s + 1]
                )
                for p in range(n_dp)
            ]
        )
    for group in waits:
        for c in group:
            c.start()
    pad = hid.shape[1] // (n_got + 1)
    total = None
    for s, group in enumerate(waits):
        for c in group:
            c.wait()
        part = dot_nn(hid[:, s * pad : s * pad + units], weights[s])
        total = part if total is None else total + part
    out[...] = total.astype(BF16)


def down_rows(hid, own, got):
    m = hid.shape[0]
    units, feats = own.shape
    n_w = len(got) + 1
    return pl.pallas_call(
        functools.partial(down_body, len(got), units),
        grid=(1,),
        in_specs=[pl.BlockSpec(hid.shape, lambda i: (0, 0))] + [ANY] * n_w,
        out_specs=pl.BlockSpec((m, feats), lambda i: (0, 0)),
        out_shape=jax.ShapeDtypeStruct((m, feats), BF16),
        scratch_shapes=[
            pltpu.VMEM((n_w, units, feats), BF16),
            pltpu.SemaphoreType.DMA((n_w,)),
        ],
        compiler_params=params("arbitrary"),
        cost_estimate=cost(
            flops=2 * m * units * feats * n_w,
            bytes_accessed=2 * units * feats * n_w + 6 * m * feats,
            transcendentals=0,
        ),
        name="down_rows",
    )(hid, own, *got)


LOG2E = 1.4426950408889634
SCALE = HEAD_DIM ** (-0.5)


def attend_body(q_ref, k0, k1, v0, v1, lo_ref, *rest):
    o_ref, ks, vs = rest[-3:]
    i = pl.program_id(1)
    span = Q_BLK + WINDOW

    @pl.when(i == 0)
    def _():
        ks[:WINDOW] = k0[...]
        ks[WINDOW:] = k1[...]
        vs[:WINDOW] = v0[...]
        vs[WINDOW:] = v1[...]

    start = pl.multiple_of(i * Q_BLK, Q_BLK)
    kb = ks[pl.ds(start, span), :]
    vb = vs[pl.ds(start, span), :]
    s = dot_nt(q_ref[...], kb) * (SCALE * LOG2E)
    col = lax.broadcasted_iota(jnp.int32, s.shape, 1)
    row = lax.broadcasted_iota(jnp.int32, s.shape, 0)
    lo = lo_ref[...] - start
    s = jnp.where((col >= lo) & (col <= row + WINDOW), s, NEG)
    p = jnp.exp2(s - jnp.max(s, axis=1, keepdims=True))
    total = jnp.sum(p, axis=1, keepdims=True)
    o = dot_nn(p.astype(BF16), vb) * (1.0 / total)
    o_ref[...] = o.astype(BF16)


def attend(half, q, pair, lo, buf):
    total, cols = q.shape
    heads = cols // HEAD_DIM
    rows = total // 2
    blocks = rows // Q_BLK
    base = half * blocks
    q_spec = pl.BlockSpec((Q_BLK, HEAD_DIM), lambda h, i: (base + i, h))
    key_spec = lambda b, c: pl.BlockSpec((WINDOW, HEAD_DIM), lambda h, i: (b, c + h))
    lo_spec = pl.BlockSpec((Q_BLK, 1), lambda h, i: (base + i, 0))
    in_specs = [
        q_spec,
        key_spec(pair[0][1], 0),
        key_spec(pair[1][1], 0),
        key_spec(pair[0][1], heads),
        key_spec(pair[1][1], heads),
        lo_spec,
    ]
    args = [q, pair[0][0], pair[1][0], pair[0][0], pair[1][0], lo]
    aliases = {}
    if buf is not None:
        in_specs.append(pl.BlockSpec(memory_space=pl.ANY))
        args.append(buf)
        aliases = {6: 0}
    return pl.pallas_call(
        attend_body,
        grid=(heads, blocks),
        in_specs=in_specs,
        out_specs=q_spec,
        out_shape=jax.ShapeDtypeStruct((total, cols), BF16),
        scratch_shapes=[pltpu.VMEM((2 * WINDOW, HEAD_DIM), BF16)] * 2,
        input_output_aliases=aliases,
        compiler_params=params("arbitrary", "arbitrary"),
        cost_estimate=cost(
            flops=4 * rows * (Q_BLK + WINDOW) * cols,
            bytes_accessed=2 * cols * 6 * WINDOW,
            transcendentals=rows * (Q_BLK + WINDOW) * heads,
        ),
        name="attend",
    )(*args)


def attend_back_body(q_ref, g_ref, k0, k1, v0, v1, lo_ref, cos_ref, sin_ref, *rest):
    dq_ref, dk_ref, dv_ref, ks, vs = rest[-5:]
    i = pl.program_id(1)
    span = Q_BLK + WINDOW

    @pl.when(i == 0)
    def _():
        ks[:WINDOW] = k0[...]
        ks[WINDOW:] = k1[...]
        vs[:WINDOW] = v0[...]
        vs[WINDOW:] = v1[...]
        dk_ref[...] = jnp.zeros_like(dk_ref)
        dv_ref[...] = jnp.zeros_like(dv_ref)

    start = pl.multiple_of(i * Q_BLK, Q_BLK)
    kb = ks[pl.ds(start, span), :]
    vb = vs[pl.ds(start, span), :]
    q, g = q_ref[...], g_ref[...]
    s = dot_nt(kb, q) * (SCALE * LOG2E)
    key = lax.broadcasted_iota(jnp.int32, s.shape, 0)
    row = lax.broadcasted_iota(jnp.int32, s.shape, 1)
    lo = lo_ref[...] - start
    s = jnp.where((key >= lo) & (key <= row + WINDOW), s, NEG)
    p = jnp.exp2(s - jnp.max(s, axis=0, keepdims=True))
    p = p * (1.0 / jnp.sum(p, axis=0, keepdims=True))
    dp = dot_nt(vb, g)
    inner = jnp.sum(p * dp, axis=0, keepdims=True)
    ds = (p * (dp - inner)).astype(BF16)
    dq = dot_tn(ds, kb) * SCALE
    dq = dq * cos_ref[...] - pltpu.roll(dq, HEAD_DIM // 2, 1) * sin_ref[...]
    dq_ref[...] = dq.astype(BF16)
    dk_ref[pl.ds(start, span), :] += dot_nn(ds, q) * SCALE
    dv_ref[pl.ds(start, span), :] += dot_nn(p.astype(BF16), g)


def attend_back(half, q, g, pair, lo_row, cos, sin, buf):
    total, cols = q.shape
    heads = cols // HEAD_DIM
    rows = total // 2
    blocks = rows // Q_BLK
    base = half * blocks
    q_spec = pl.BlockSpec((Q_BLK, HEAD_DIM), lambda h, i: (base + i, h))
    key_spec = lambda b, c: pl.BlockSpec((WINDOW, HEAD_DIM), lambda h, i: (b, c + h))
    rope_spec = pl.BlockSpec((Q_BLK, HEAD_DIM), lambda h, i: (base + i, 0))
    lo_spec = pl.BlockSpec((1, Q_BLK), lambda h, i: (0, base + i))
    grad_spec = pl.BlockSpec((2 * WINDOW, HEAD_DIM), lambda h, i: (0, h))
    in_specs = [
        q_spec,
        q_spec,
        key_spec(pair[0][1], 0),
        key_spec(pair[1][1], 0),
        key_spec(pair[0][1], heads),
        key_spec(pair[1][1], heads),
        lo_spec,
        rope_spec,
        rope_spec,
    ]
    args = [q, g, pair[0][0], pair[1][0], pair[0][0], pair[1][0], lo_row, cos, sin]
    aliases = {}
    if buf is not None:
        in_specs.append(pl.BlockSpec(memory_space=pl.ANY))
        args.append(buf)
        aliases = {9: 0}
    return pl.pallas_call(
        attend_back_body,
        grid=(heads, blocks),
        in_specs=in_specs,
        out_specs=[
            pl.BlockSpec((Q_BLK, HEAD_DIM), lambda h, i: (base + i, 2 * heads + h)),
            grad_spec,
            grad_spec,
        ],
        out_shape=[
            jax.ShapeDtypeStruct((total, 3 * cols), BF16),
            jax.ShapeDtypeStruct((2 * WINDOW, cols), F32),
            jax.ShapeDtypeStruct((2 * WINDOW, cols), F32),
        ],
        scratch_shapes=[pltpu.VMEM((2 * WINDOW, HEAD_DIM), BF16)] * 2,
        input_output_aliases=aliases,
        compiler_params=params("arbitrary", "arbitrary"),
        cost_estimate=cost(
            flops=10 * rows * (Q_BLK + WINDOW) * cols,
            bytes_accessed=2 * cols * 14 * WINDOW,
            transcendentals=rows * (Q_BLK + WINDOW) * heads,
        ),
        name="attend_back",
    )(*args)


def finish_body(half, ak, av, ok, ov, cos_ref, sin_ref, _, out_ref):
    cols = ak.shape[1]

    def write(gk, gv):
        for h in range(cols // HEAD_DIM):
            c = slice(h * HEAD_DIM, (h + 1) * HEAD_DIM)
            seg = gk[:, c]
            seg = seg * cos_ref[...] - pltpu.roll(seg, HEAD_DIM // 2, 1) * sin_ref[...]
            out_ref[:, c] = seg.astype(BF16)
        out_ref[:, cols:] = gv.astype(BF16)

    write(ak[...] + ok[...].astype(F32), av[...] + ov[...].astype(F32))


def finish_keys(half, ak, av, other_k, other_v, cos, sin, buf):
    cols = ak.shape[1]
    blk = 512
    n = WINDOW // blk
    base = half * n
    own = pl.BlockSpec((blk, cols), lambda i: (base + i, 0))
    oth = lambda o: pl.BlockSpec((blk, cols), lambda i: (o[1] * n + i, o[2]))
    rope = pl.BlockSpec((blk, HEAD_DIM), lambda i: (base + i, 0))
    return pl.pallas_call(
        functools.partial(finish_body, half),
        grid=(n,),
        in_specs=[own, own, oth(other_k), oth(other_v), rope, rope, ANY],
        out_specs=pl.BlockSpec((blk, 2 * cols), lambda i: (base + i, 0)),
        out_shape=jax.ShapeDtypeStruct(buf.shape, BF16),
        input_output_aliases={6: 0},
        compiler_params=params("arbitrary"),
        name="finish_keys",
    )(ak, av, other_k[0], other_v[0], cos, sin, buf)


def shards(
    tokens, segments, attn_gain, ffn_gain, w_query, w_key, w_value, w_out, w_gate, w_up, w_down, cotangent
):
    rows, feats = tokens.shape
    n_tensor = lax.axis_size("tensor")
    n_dp = lax.axis_size("dp")
    block_len = rows * n_tensor
    head_cols = w_query.shape[1]
    units = w_gate.shape[1]
    unit_pad = -(-units // 128) * 128
    dp_idx, t_idx = lax.axis_index("dp"), lax.axis_index("tensor")
    first_pos = dp_idx * block_len
    ring = [ring_cycle(n_tensor)]
    square = group_cycles(n_tensor)
    groups = n_tensor // GROUP
    far = n_tensor // 2
    part_cols = feats // n_dp
    own_w = (w_gate.T, w_up.T, w_down)

    def to_group(piece, s):
        pairs = [(t, (t + s * GROUP) % n_tensor) for t in range(n_tensor)]
        return lax.ppermute(piece, "tensor", pairs)

    def dp_cols(value):
        return lax.dynamic_slice_in_dim(value, dp_idx * part_cols, part_cols, 1)

    ring_owners = owners(ring)
    x_f = tokens.astype(F32)
    x_normed, x_unit, x_inv = norm_forward(x_f, attn_gain)
    x_low = x_normed.astype(BF16)
    go = Gather(dp_cols(w_out), ring)
    go.all()
    w_joint = jnp.concatenate([w_key, w_value, w_query], axis=1)
    gx = Gather(after(x_low, go.f, go.b), ring)
    gx.step()
    w_out_part = place_chunks(ring_owners, go.chunks, n_tensor)
    cos, sin = rope_tables(first_pos + jnp.arange(block_len, dtype=jnp.int32))
    cos, sin = after(cos, w_joint, w_out_part), after(sin, w_joint)

    def qkv(rel, bufs):
        return qkv_chunk(
            ring_owners, rel % n_tensor, gx.chunks[rel], w_query, w_key, w_value, cos, sin, bufs
        )

    bufs = qkv(0, None)
    for k in range(1, far):
        came = (gx.f, gx.b)
        gx.step(bufs[0])
        if k == 1:
            seg_tail = after(segments[block_len - WINDOW :].astype(F32), *came)
            prev_seg = shifted(seg_tail, "dp", 1).astype(jnp.int32)
            w_out_part = w_out_part.reshape(n_tensor * head_cols, part_cols)
            low_bits = bits_of(n_dp)
            w_spread = spread_parts([(0, w_out_part)], low_bits[-1:])
        if k == far - 1:
            w_spread = spread_parts(w_spread, low_bits[:-1], *came)
        bufs = qkv(k, qkv(-k, bufs))
    w_places = jnp.stack([dp_idx ^ x for x, _ in w_spread]).astype(jnp.int32)
    w_out_parts = [w for _, w in w_spread]

    seg_all = jnp.concatenate([prev_seg, segments], axis=0)
    low_key = jnp.sum((seg_all[None, :] < segments[:, None]).astype(jnp.int32), axis=1)
    low_key = jnp.where(dp_idx == 0, jnp.maximum(low_key, WINDOW), low_key)
    spot = jnp.arange(block_len, dtype=jnp.int32)
    low_key = jnp.maximum(low_key, spot + 1)
    low_key = low_key - jnp.where(spot >= block_len // 2, block_len // 2, 0)
    low_col, low_row = low_key[:, None], low_key[None, :]

    came = (gx.f, gx.b)
    mine, low_col, low_row, *w_out_parts = lax.optimization_barrier(
        (tuple(dp_cols(w) for w in own_w), low_col, low_row, *w_out_parts)
    )
    first = after(mine[0], *came)
    gate_got = [to_group(first, s) for s in range(1, groups)]
    bufs = list(bufs)
    bufs[0] = after(bufs[0], low_col, low_row, first, *w_out_parts)
    bufs = qkv(far, bufs)
    query, key_value, x_all = bufs
    tail_kv = after(key_value[block_len - WINDOW :])
    prev = shifted(tail_kv, "dp", 1)
    gy = Gather(after(cotangent, *came), square)
    gy.step()

    late, early = ((key_value, 0), (key_value, 1)), ((prev, 0), (key_value, 0))
    heads_late = attend(1, query, late, low_col, None)
    gy_came = (gy.f, gy.b)
    heads_late = after(heads_late, *gy_came)
    heads_low = attend(0, query, early, low_col, heads_late)
    heads_low = heads_low.reshape(n_tensor, rows, head_cols)
    heads_low = after(heads_low, *gate_got)

    heads_got = lax.all_to_all(heads_low, "tensor", split_axis=0, concat_axis=0, tiled=True)
    gate_all_got = [all_dp(after(g, heads_low)) for g in gate_got]
    second = after(mine[1], heads_got)
    up_got = [to_group(second, s) for s in range(1, groups)]
    gy.step(heads_got)
    y_chunks = gy.chunks
    attn_branch, mid, h_low, my_heads = out_project(
        heads_got, w_places, w_out_parts, tokens, ffn_gain
    )

    gh = Gather(h_low, square)
    sets = {0: ([0], 2), 1: ([-1, 1], 0), 2: ([2], 3)}
    ffn_bufs, dhs = [], {}

    def ffn(i, shard, *deps):
        rels, place = sets[i]
        hs = [c for r in rels for c in gh.chunks[r]]
        ys = [c for r in rels for c in y_chunks[r]]
        srcs = own_w if shard == 0 else got[shard - 1]
        hs[0] = after(hs[0], *deps)
        return ffn_set(
            hs, ys, srcs, units, shard, groups, GROUP * rows, place, dhs.get(i), ffn_bufs
        )

    gh.step()
    ffn_bufs, dhs[0] = ffn(0, 0)
    third = after(mine[2], h_low, *up_got)
    down_got = [to_group(third, s) for s in range(1, groups)]
    came = (*gh.chunks[1], *gh.chunks[-1], *gate_all_got)
    up_all_got = [all_dp(after(g, dhs[0], *came)) for g in up_got]
    gh.step(dhs[0])
    ffn_bufs, dhs[1] = ffn(1, 0)
    came = (*gh.chunks[2], *y_chunks[2], *up_all_got)
    down_all_got = [all_dp(after(d, dhs[1], *came)) for d in down_got]
    got = list(zip(gate_all_got, up_all_got, down_all_got))
    ffn_bufs, dhs[2] = ffn(2, 0)
    for s in range(1, groups):
        ffn_bufs, dhs[2] = ffn(2, s)
    sh = Scatter(dhs[2].astype(BF16), square)
    for s in range(1, groups):
        ffn_bufs, dhs[1] = ffn(1, s, *sh.sent)
    sh.step(dhs[1], False)
    for s in range(1, groups):
        ffn_bufs, dhs[0] = ffn(0, s, *sh.sent)
    h_all, y_all, hid_all, gate_all, up_all = ffn_bufs

    def send_back(red, *deps):
        cut = lambda s: red.value[s * unit_pad : s * unit_pad + units]
        return [to_group(after(cut(s), *deps), groups - s) for s in range(1, groups)]

    red_down = Halves(*tn_cols(hid_all, y_all), 1)
    red_down.send()
    red_gate = Halves(*tn_cols(after(gate_all, red_down.sent), h_all), 1)
    sh.f, sh.b, dhs[0], red_down.got, red_gate.sent = together(
        sh.f, sh.b, dhs[0], red_down.got, red_gate.sent
    )
    grad_mid, grad_mid_low, grad_ffn_gain, my_grad_heads = out_back(
        dhs[0], sh.f, sh.b, mid, cotangent, ffn_gain, w_places, w_out_parts, n_tensor
    )
    grad_heads = lax.all_to_all(
        my_grad_heads, "tensor", split_axis=0, concat_axis=0, tiled=True
    ).reshape(block_len, head_cols)

    red_down.add()
    red_down.send(my_grad_heads)
    red_gate.send(red_down.sent)
    sf_all = down_rows(after(hid_all, red_down.sent), own_w[2], [g[2] for g in got])
    red_up = Halves(*tn_cols(after(up_all, red_down.sent), h_all), 1)
    grad_heads, red_down.got, red_gate.got, sf_all, red_up.sent = together(
        grad_heads, red_down.got, red_gate.got, sf_all, red_up.sent
    )
    red_down.finish()
    down_back = send_back(red_down)
    red_gate.add()
    red_gate.send()
    red_up.send()
    sf = Scatter(sf_all[3 * rows :], square)

    grad_heads = after(grad_heads, red_down.value, *sf.sent, red_gate.sent)
    d_joint, bk, bv = attend_back(0, query, grad_heads, early, low_row, cos, sin, None)
    d_joint, bk, bv, sf.f, sf.b, red_up.got = together(d_joint, bk, bv, sf.f, sf.b, red_up.got)
    back = after(jnp.concatenate([bk[:WINDOW], bv[:WINDOW]], axis=1).astype(BF16))
    got_back = shifted(back, "dp", -1)
    sf.step(after(sf_all[: 2 * rows], back), False)
    red_up.add()
    out_local = dot_tn(my_heads, after(grad_mid_low, back)).astype(BF16)
    out_dp = lax.psum_scatter(out_local, "dp", scatter_dimension=1, tiled=True)
    d_joint, ak, av = attend_back(
        1, query, after(grad_heads, back, *sf.sent, red_up.sent, out_local),
        late, low_row, cos, sin, d_joint,
    )
    d_joint, ak, av, got_back, sf.f, sf.b, red_gate.got, *down_back = together(
        d_joint, ak, av, got_back, sf.f, sf.b, red_gate.got, *down_back
    )
    red_gate.finish()
    gate_back = send_back(red_gate)
    red_up.send(red_gate.value)
    d_joint = finish_keys(0, after(ak, red_gate.value), av, (bk, 1, 0), (bv, 1, 0), cos, sin, d_joint)
    d_joint = finish_keys(1, ak, av, (got_back, 0, 0), (got_back, 0, 1), cos, sin, d_joint)

    def terms(rels, kind, *deps):
        rels = [r % n_tensor for r in rels]
        return grad_x_terms(after(ring_owners, *deps), rels, d_joint, w_joint, rows, kind)

    sx = Scatter(terms([far], BF16), ring)
    near = terms([far - 1, 1 - far], F32, *sx.sent)
    down_own = shard_sum(after(red_down.value, *sx.sent), down_back, units)
    down_dp = all_dp(down_own)
    joint = tn_rows(after(x_all, *sx.sent), d_joint, w_joint)
    grad_attn_gain = joint[2][:, 0] / attn_gain
    sx.f, sx.b, near, down_own, joint, out_dp, *gate_back = together(
        sx.f, sx.b, near, down_own, tuple(joint), out_dp, *gate_back
    )
    out_own = lax.psum_scatter(out_dp, "tensor", scatter_dimension=0, tiled=True)
    red_joint = Halves(*joint[:2], 0)
    red_joint.send()
    sx.step(near, True)
    gate_own = shard_sum(after(red_gate.value, *sx.sent), gate_back, units)
    gate_dp = all_dp(gate_own)
    near = terms([far - 2, 2 - far], F32, gate_own)
    sx.f, sx.b, near, red_up.got, red_joint.got, gate_own = together(
        sx.f, sx.b, near, red_up.got, red_joint.got, gate_own
    )
    red_up.finish()
    red_joint.add()
    up_back = send_back(red_up)
    red_joint.send()
    sx.step(near, True, red_up.value, red_joint.sent)
    ffn_branch = after(sf_all[2 * rows : 3 * rows], *sx.sent).astype(F32)
    ffn_branch = ffn_branch + sf.f.astype(F32) + sf.b.astype(F32)
    result = mid + ffn_branch
    slots = 2 * n_dp + 1
    own_seg = lax.dynamic_slice_in_dim(segments, t_idx * rows, rows)
    one_hot = (own_seg[:, None] == jnp.arange(slots, dtype=jnp.int32)[None, :]).astype(F32)
    per_row = jnp.stack(
        [
            jnp.sum(result * result, axis=1),
            jnp.sum(attn_branch * attn_branch, axis=1),
            jnp.sum(ffn_branch * ffn_branch, axis=1),
            jnp.ones((rows,), F32),
        ],
        axis=1,
    )
    table = jnp.dot(per_row.T, one_hot, precision=lax.Precision.HIGHEST, preferred_element_type=F32)
    packed = jnp.concatenate([grad_attn_gain, grad_ffn_gain[0], table.reshape(-1)])
    packed = jnp.pad(packed, (0, -packed.shape[0] % 1024)).reshape(-1, 128)
    near = terms([far - 3, 3 - far], F32, packed)
    grad_w_down = widen_cols(after(down_dp, near))
    sx.f, sx.b, near, red_joint.got, grad_w_down, out_own, *up_back = together(
        sx.f, sx.b, near, red_joint.got, grad_w_down, out_own, *up_back
    )
    out_all = all_dp(out_own)
    sx.step(near, True)
    for k in range(far - 4, 0, -1):
        sx.step(terms([k, -k], F32, *sx.sent), True)
    up_own = shard_sum(after(red_up.value, *sx.sent), up_back, units)
    up_dp = all_dp(up_own)
    red_joint.finish(*sx.sent)
    joint_parts = spread_parts([(0, red_joint.value)], bits_of(n_dp)[::-1])
    joint_places = jnp.stack([place_of(dp_idx ^ x, n_dp) for x, _ in joint_parts])
    grad_w_gate = widen_cols(after(gate_dp, up_own, red_joint.value)).T
    own = terms([0], F32, grad_w_gate)
    packed = sum_all(after(packed, *sx.sent))
    sx.f, sx.b, own, packed = together(sx.f, sx.b, own, packed)
    input_grad = input_grad_of(own, sx.f, sx.b, grad_mid, tokens, attn_gain)
    grad_w_out = jnp.concatenate(list(out_all), axis=1).astype(F32)
    grad_w_key, grad_w_value, grad_w_query = widen_pieces(
        joint_places.astype(jnp.int32), [v for _, v in joint_parts], [head_cols] * 3
    )
    grad_w_up = widen_cols(up_dp).T

    packed = packed.reshape(-1)
    sums = packed[2 * feats : 2 * feats + 4 * slots].reshape(4, slots)
    doc_rms = jnp.sqrt(sums[:3] / (jnp.maximum(sums[3:], 1.0) * feats))

    return (
        result.astype(BF16),
        input_grad,
        packed[:feats],
        packed[feats : 2 * feats],
        grad_w_query,
        grad_w_key,
        grad_w_value,
        grad_w_out,
        grad_w_gate,
        grad_w_up,
        grad_w_down,
        doc_rms,
    )


def solution(mesh):
    both = P(("dp", "tensor"), None)
    col, row = P(None, "tensor"), P("tensor", None)
    return jax.shard_map(
        shards,
        mesh=mesh,
        in_specs=(both, P("dp"), P(), P(), col, col, col, row, col, col, row, both),
        out_specs=(both, both, P(), P(), col, col, col, row, col, col, row, P()),
        check_vma=False,
    )
```

time: 935 us -> 882 us (0.943)
  Pallas kernels: 99.2 us -> 392 us
  matrix products: 156 us -> 6.01 us
  other arithmetic: 118 us -> 29.9 us
  local copies, waits for them, and re-layouts: 88.8 us -> 39.3 us
  waiting for transfers between devices: 318 us -> 274 us
    pallas_call x8 -> x48, Pallas kernels: 36.3 us -> 329 us  [the longest x6 82 us: ffn_set(): pl.pallas_call(functools.partial(ffn_body, n_in, n_w, first, units, len(h...]
    dot_general x58 -> x0, matrix products: 108 us -> none  [the longest x33 57.3 us: dot_nt(): lax.dot_general(a, b, (((1,), (1,)), ((), ())), preferred_element_type=F32)]
    ppermute x54 -> x46, waiting for transfers between devices: 221 us -> 154 us  [the longest x6 73.6 us: to_group(): return lax.ppermute(piece, 'tensor', pairs)]
    dot_general x8 -> x1, matrix products: 47.3 us -> 5.79 us  [dot_tn(): lax.dot_general(a, b, (((0,), (0,)), ((), ())), preferred_element_type=F32)]
    convert_element_type x29 -> x5, other arithmetic: 40 us -> 5.8 us  [the longest x1 2.5 us: shards(): x_low = x_normed.astype(BF16)]
    select_n x17 -> x0, other arithmetic: 31.7 us -> none  [halves_gather(): low = jnp.where(side == 0, value, other)]
    concatenate x19 -> x2, other arithmetic: 26.3 us -> 1.4 us  [the longest x1 1.32 us: rope_tables(): jnp.concatenate([-sin, sin], axis=1)]
    unnamed x291 -> x132, local copies, waits for them, and re-layouts: 29.9 us -> 9.54 us
  transfers between devices with their start and end apart: 100 -> 79, of which waited for: 34 -> 35; matrix products, arithmetic and copies ran while one was open for 33% -> 6% of each run, Pallas kernels for 11% -> 38%
where the time goes in v2:
time: 882 us; the launch traced here: 872 us
  Pallas kernels  392 us (44%)
  waiting for transfers between devices  274 us (31%)
  starting transfers between devices  116 us (13%)
  local copies, waits for them, and re-layouts  39.3 us (4%)
  other arithmetic  29.9 us (3%)
  between operations  15.1 us (2%)
    pallas_call x6, Pallas kernels, ffn_set(): pl.pallas_call(functools.partial(ffn_body, n_in, n_w, first, units, len(h...  82 us
    ppermute x19, waiting for transfers between devices, swap(): return lax.ppermute(value, axis, [(d, d ^ bit) for d in range(count)])  79.4 us
    ppermute x6, waiting for transfers between devices, to_group(): return lax.ppermute(piece, 'tensor', pairs)  73.6 us
    pallas_call x8, Pallas kernels, qkv_chunk(): pl.pallas_call(functools.partial(qkv_body, n_in), grid_spec=pltpu.Prefetc...  40.6 us
    pallas_call x3, Pallas kernels, tn_cols(): pl.pallas_call(functools.partial(tn_cols_body, n), grid_spec=pltpu.Prefet...  38.2 us
    ppermute x19, starting transfers between devices, swap(): return lax.ppermute(value, axis, [(d, d ^ bit) for d in range(count)])  37.8 us
    pallas_call x2, Pallas kernels, attend_back(): pl.pallas_call(attend_back_body, grid=(heads, blocks), in_specs=in_specs,...  35.6 us
    pallas_call x5, Pallas kernels, grad_x_terms(): pl.pallas_call(grad_x_body, grid_spec=pltpu.PrefetchScalarGridSpec(num_sc...  27.8 us
  transfers between devices with their start and end apart: 79, of which 35 were waited for; matrix products, arithmetic and copies ran while one was open for 6% of the time, Pallas kernels for 38%

profile of v2, /device:TPU:0, one launch (start us, length us, event | category | flops | bytes accessed | tf_op | source)
XLA Modules:
  0.0 871.8 jit_solution(16827091803346964976)
XLA Ops:
  93.4 14.6 %collective-permute-done.17.refs_1_ = bf16[2048,512]{1,0:T(8,128)(2,1)} collective-permute-done((bf16[2048,512]{1,0:T(8,128)(2,1)S(1)}, bf16[2048,512]{1,0:T(8,128)(2,1)}, u32[]{:S(2)}, u32[]{:S(2)}) %collective-permute-start.17) | collective-permute-done | bytes 2097184 | tf_op jit(solution)/shard_map/ppermute | solution.py:125
  158.2 10.3 %attend.2.rest_0_ = bf16[2048,256]{1,0:T(8,128)(2,1)} custom-call(bf16[2048,256]{1,0:T(8,128)(2,1)} %get-tuple-element.305.q_ref, bf16[2048,512]{1,0:T(8,128)(2,1)} %get-tuple-element.306.k0.k1.v0.v1, bf16[2048,512]{1,0:T(8,128)(2,1)} %get-tuple-element.306.k0.k1.v0.v1, bf16[2048,512]{1,0:T(8,128)(2,1)} %get-tuple-element.306.k0.k1.v0.v1, ...), custom_call_target="tpu_custom_call" | custom-call | flops 83886080 | bytes 196608 | tf_op jit(solution)/shard_map/attend/pallas_call | solution.py:967
  172.5 11.5 %collective-permute-done.22.refs_3_ = bf16[256,2048]{1,0:T(8,128)(2,1)S(1)} collective-permute-done((bf16[256,2048]{1,0:T(8,128)(2,1)S(1)}, bf16[256,2048]{1,0:T(8,128)(2,1)S(1)}, u32[]{:S(2)}, u32[]{:S(2)}) %collective-permute-start.22) | collective-permute-done | bytes 1048608 | tf_op jit(solution)/shard_map/ppermute | solution.py:81
  185.1 10.3 %attend.3 = bf16[2048,256]{1,0:T(8,128)(2,1)} custom-call(bf16[2048,256]{1,0:T(8,128)(2,1)} %get-tuple-element.305.q_ref, bf16[1024,512]{1,0:T(8,128)(2,1)} %copy-done.7, bf16[2048,512]{1,0:T(8,128)(2,1)} %get-tuple-element.306.k0.k1.v0.v1, bf16[1024,512]{1,0:T(8,128)(2,1)} %copy-done.7, ...), custom_call_target="tpu_custom_call", output_to_operand_aliasing={{}: (6, {})} | custom-call | flops 83886080 | bytes 196608 | tf_op jit(solution)/shard_map/attend/pallas_call | solution.py:967
  202.0 24.5 %all-to-all-done.heads = bf16[8,256,256]{2,1,0:T(8,128)(2,1)S(1)} async-done(((bf16[8,256,256]{2,1,0:T(8,128)(2,1)}), bf16[8,256,256]{2,1,0:T(8,128)(2,1)S(1)}, u32[]{:S(2)}, u32[]{:S(2)}) %all-to-all-start) | async-done | bytes 1048608 | tf_op jit(solution)/shard_map/all_to_all | solution.py:1199
  227.5 10.3 %out_project.1 = (f32[256,2048]{1,0:T(8,128)}, f32[256,2048]{1,0:T(8,128)}, bf16[256,2048]{1,0:T(8,128)(2,1)}, bf16[256,2048]{1,0:T(8,128)(2,1)}) custom-call(s32[4]{0:T(128)} %pad_add_fusion.1.idx, bf16[8,256,256]{2,1,0:T(8,128)(2,1)} %copy-done.17, bf16[256,2048]{1,0:T(8,128)(2,1)} %x_ref.3, f32[1,2048]{1,0:T(1,128)} %bitcast.80, ...), custom_call_target="tpu_custom_call" | custom-call | flops 134217728 | bytes 1048576 | tf_op jit(solution)/shard_map/out_project/pallas_call | solution.py:665
  239.9 11.0 %ffn_set.6 = (bf16[1024,2048]{1,0:T(8,128)(2,1)}, bf16[1024,2048]{1,0:T(8,128)(2,1)}, bf16[1024,1536]{1,0:T(8,128)(2,1)}, bf16[1024,1536]{1,0:T(8,128)(2,1)}, bf...) custom-call(bf16[256,2048]{1,0:T(8,128)(2,1)} %get-tuple-element.356.refs_0_, bf16[256,2048]{1,0:T(8,128)(2,1)} %dy.1, ...), custom_call_target="tpu_custom_call" | custom-call | flops 225443840 | bytes 1052672 | tf_op jit(solution)/shard_map/ffn_set/pallas_call | solution.py:844
  251.0 25.1 %collective-permute-done.30 = bf16[688,512]{1,0:T(8,128)(2,1)} collective-permute-done((bf16[688,512]{1,0:T(8,128)(2,1)S(1)}, bf16[688,512]{1,0:T(8,128)(2,1)}, u32[]{:S(2)}, u32[]{:S(2)}) %collective-permute-start.30) | collective-permute-done | bytes 704544 | tf_op jit(solution)/shard_map/ppermute | solution.py:1129
  285.0 10.3 %collective-permute-start.26 = (bf16[128,2048]{1,0:T(8,128)(2,1)}, bf16[128,2048]{1,0:T(8,128)(2,1)S(1)}, u32[]{:S(2)}, u32[]{:S(2)}) collective-permute-start(bf16[128,2048]{1,0:T(8,128)(2,1)} %slice.107), channel_id=1, source_target_pairs={{0,2},{2,3},{3,1},{1,0},{4,6},{6,7},{7,5},{5,4},{8,10},{10,11},{11... | collective-permute-start | bytes 1572872 | tf_op jit(solution)/shard_map/ppermute | solution.py:85
  295.2 17.8 %ffn_set.7 = (bf16[1024,2048]{1,0:T(8,128)(2,1)}, bf16[1024,2048]{1,0:T(8,128)(2,1)}, bf16[1024,1536]{1,0:T(8,128)(2,1)}, bf16[1024,1536]{1,0:T(8,128)(2,1)}, bf...) custom-call(bf16[256,2048]{1,0:T(8,128)(2,1)} %collective-permute-do, ...), custom_call_target="tpu_custom_call", output_to_operand_aliasing={{0}: (7, {}), {1}: (8, {}), {2}: (9, {}), {3}: (10, {}), {4... | custom-call | flops 450887680 | bytes 1576960 | tf_op jit(solution)/shard_map/ffn_set/pallas_call | solution.py:844
  318.8 11.3 %ffn_set.8 = (bf16[1024,2048]{1,0:T(8,128)(2,1)}, bf16[1024,2048]{1,0:T(8,128)(2,1)}, bf16[1024,1536]{1,0:T(8,128)(2,1)}, bf16[1024,1536]{1,0:T(8,128)(2,1)}, bf...) custom-call(bf16[128,2048]{1,0:T(8,128)(2,1)} %copy-done.25, ...), custom_call_target="tpu_custom_call", output_to_operand_aliasing={{0}: (7, {}), {1}: (8, {}), {2}: (9, {}), {3}: (10, {}), {4... | custom-call | flops 225443840 | bytes 1052672 | tf_op jit(solution)/shard_map/ffn_set/pallas_call | solution.py:844
  330.2 14.6 %all-gather.19.cloned.1.call-done = bf16[2752,512]{1,0:T(8,128)(2,1)} async-done(((bf16[688,512]{1,0:T(8,128)(2,1)}), bf16[2752,512]{1,0:T(8,128)(2,1)}) %all-gather.19.cloned.1.call-update) | async-done | bytes 2818064 | tf_op jit(solution)/shard_map/all_gather | solution.py:176
  344.8 11.4 %ffn_set.9 = (bf16[1024,1536]{1,0:T(8,128)(2,1)}, bf16[1024,1536]{1,0:T(8,128)(2,1)}, bf16[1024,1536]{1,0:T(8,128)(2,1)}, f32[256,2048]{1,0:T(8,128)}) custom-call(bf16[128,2048]{1,0:T(8,128)(2,1)} %copy-done.25, bf16[128,2048]{1,0:T(8,128)(2,1)} %copy-done.24, ...), custom_call_target="tpu_custom_call", output_to_operand_aliasing={{0}: (8, {}), {1}: (9, {}), {2}: (10, {})} | custom-call | flops 225443840 | bytes 1052672 | tf_op jit(solution)/shard_map/ffn_set/pallas_call | solution.py:844
  360.8 18.7 %ffn_set.10 = (bf16[1024,1536]{1,0:T(8,128)(2,1)}, bf16[1024,1536]{1,0:T(8,128)(2,1)}, bf16[1024,1536]{1,0:T(8,128)(2,1)}, f32[512,2048]{1,0:T(8,128)}) custom-call(bf16[256,2048]{1,0:T(8,128)(2,1)} %collective-permute-done.24.refs_0_, bf16[256,2048]{1,0:T(8,128)(2,1)} %copy-done.15, ...), custom_call_target="tpu_custom_call", output_to_operand_aliasing={{0}: (8, {}), {1}: (9, {}), {2}: (10, {})} | custom-call | flops 450887680 | bytes 1576960 | tf_op jit(solution)/shard_map/ffn_set/pallas_call | solution.py:844
  384.6 11.6 %ffn_set.11 = (bf16[1024,1536]{1,0:T(8,128)(2,1)}, bf16[1024,1536]{1,0:T(8,128)(2,1)}, bf16[1024,1536]{1,0:T(8,128)(2,1)}, f32[256,2048]{1,0:T(8,128)}) custom-call(bf16[256,2048]{1,0:T(8,128)(2,1)} %get-tuple-element.356.refs_0_, bf16[256,2048]{1,0:T(8,128)(2,1)} %dy.1, ...), custom_call_target="tpu_custom_call", output_to_operand_aliasing={{0}: (6, {}), {1}: (7, {}), {2}: (8, {})} | custom-call | flops 225443840 | bytes 1052672 | tf_op jit(solution)/shard_map/ffn_set/pallas_call | solution.py:844
  396.2 12.8 %tn_cols.3 = (bf16[1536,1024]{1,0:T(8,128)(2,1)}, bf16[1536,1024]{1,0:T(8,128)(2,1)}) custom-call(s32[2]{0:T(128)} %pad_add_fusion.2.idx, bf16[1024,1536]{1,0:T(8,128)(2,1)} %get-tuple-element.378.a.hid, bf16[1024,2048]{1,0:T(8,128)(2,1)} %get-tuple-element.362.b), custom_call_target="tpu_custom_call" | custom-call | flops 402653184 | bytes 851968 | tf_op jit(solution)/shard_map/tn_cols/pallas_call | solution.py:351
  411.7 12.7 %tn_cols.4 = (bf16[1536,1024]{1,0:T(8,128)(2,1)}, bf16[1536,1024]{1,0:T(8,128)(2,1)}) custom-call(s32[2]{0:T(128)} %pad_add_fusion.2.idx, bf16[1024,1536]{1,0:T(8,128)(2,1)} %get-tuple-element.365.a, bf16[1024,2048]{1,0:T(8,128)(2,1)} %get-tuple-element.366.b), custom_call_target="tpu_custom_call" | custom-call | flops 402653184 | bytes 851968 | tf_op jit(solution)/shard_map/tn_cols/pallas_call | solution.py:351
  424.4 10.5 %collective-permute-done.34.f = bf16[256,2048]{1,0:T(8,128)(2,1)} collective-permute-done((bf16[256,2048]{1,0:T(8,128)(2,1)}, bf16[256,2048]{1,0:T(8,128)(2,1)}, u32[]{:S(2)}, u32[]{:S(2)}) %collective-permute-start.34) | collective-permute-done | bytes 1048608 | tf_op jit(solution)/shard_map/ppermute | solution.py:105
  443.8 12.6 %out_back.1 = (f32[256,2048]{1,0:T(8,128)}, bf16[256,2048]{1,0:T(8,128)(2,1)}, f32[1,2048]{1,0:T(1,128)}, bf16[8,256,256]{2,1,0:T(8,128)(2,1)}) custom-call(s32[4]{0:T(128)} %pad_add_fusion.1.idx, f32[256,2048]{1,0:T(8,128)} %get-tuple-element.368.own, bf16[256,2048]{1,0:T(8,128)(2,1)} %collective-permute-done.34.f, ...), custom_call_target="tpu_custom_call" | custom-call | flops 134217728 | bytes 1179648 | tf_op jit(solution)/shard_map/out_back/pallas_call | solution.py:730
  461.7 13.2 %down_rows.1 = bf16[1024,2048]{1,0:T(8,128)(2,1)} custom-call(bf16[1024,1536]{1,0:T(8,128)(2,1)} %get-tuple-element.378.a.hid, bf16[688,2048]{1,0:T(8,128)(2,1)} %own.1, bf16[4,688,512]{2,1,0:T(8,128)(2,1)} %bitcast.52), custom_call_target="tpu_custom_call" | custom-call | flops 360710144 | bytes 1138688 | tf_op jit(solution)/shard_map/down_rows/pallas_call | solution.py:894
  474.9 12.7 %tn_cols.5 = (bf16[1536,1024]{1,0:T(8,128)(2,1)}, bf16[1536,1024]{1,0:T(8,128)(2,1)}) custom-call(s32[2]{0:T(128)} %pad_add_fusion.2.idx, bf16[1024,1536]{1,0:T(8,128)(2,1)} %get-tuple-element.380.a, bf16[1024,2048]{1,0:T(8,128)(2,1)} %get-tuple-element.366.b), custom_call_target="tpu_custom_call" | custom-call | flops 402653184 | bytes 851968 | tf_op jit(solution)/shard_map/tn_cols/pallas_call | solution.py:351
  487.6 10.3 %collective-permute-done.37.b = bf16[1536,512]{1,0:T(8,128)(2,1)S(1)} collective-permute-done((bf16[1536,512]{1,0:T(8,128)(2,1)}, bf16[1536,512]{1,0:T(8,128)(2,1)S(1)}, u32[]{:S(2)}, u32[]{:S(2)}) %collective-permute-start.37) | collective-permute-done | bytes 1572896 | tf_op jit(solution)/shard_map/ppermute | solution.py:125
  511.5 17.8 %attend_back.2 = (bf16[2048,768]{1,0:T(8,128)(2,1)}, f32[2048,256]{1,0:T(8,128)}, f32[2048,256]{1,0:T(8,128)}) custom-call(bf16[2048,256]{1,0:T(8,128)(2,1)} %get-tuple-element.305.q_ref, bf16[2048,256]{1,0:T(8,128)(2,1)} %bitcast.69, bf16[1024,512]{1,0:T(8,128)(2,1)} %copy-done.7, bf16[2048,512]{1,0:T(8,128)(2,1)} %get-tuple-element.306.k0.k1.v0.v1, ...), custom_call_target="tpu_custom_call" | custom-call | flops 209715200 | bytes 458752 | tf_op jit(solution)/shard_map/attend_back/pallas_call | solution.py:1048
  552.7 6.3 half_add.6
  559.0 17.8 %attend_back.3 = (bf16[2048,768]{1,0:T(8,128)(2,1)}, f32[2048,256]{1,0:T(8,128)}, f32[2048,256]{1,0:T(8,128)}) custom-call(bf16[2048,256]{1,0:T(8,128)(2,1)} %get-tuple-element.305.q_ref, bf16[2048,256]{1,0:T(8,128)(2,1)} %bitcast.70, bf16[2048,512]{1,0:T(8,128)(2,1)} %get-tuple-element.306.k0.k1.v0.v1, ...), custom_call_target="tpu_custom_call", output_to_operand_aliasing={{0}: (9, {})} | custom-call | flops 209715200 | bytes 458752 | tf_op jit(solution)/shard_map/attend_back/pallas_call | solution.py:1048
  576.8 7.1 collective-permute-done.46.refs_0_
  617.3 13.0 %tn_rows.1 = (bf16[1024,768]{1,0:T(8,128)(2,1)}, bf16[1024,768]{1,0:T(8,128)(2,1)}, f32[2048,1]{1,0:T(8,128)}) custom-call(s32[2]{0:T(128)} %pad_add_fusion.2.idx, bf16[2048,2048]{1,0:T(8,128)(2,1)} %get-tuple-element.430.a, bf16[2048,768]{1,0:T(8,128)(2,1)} %finish_keys.3.rows.b, bf16[2048,768]{1,0:T(8,128)(2,1)} %copy-done.2), custom_call_target="tpu_custom_call" | custom-call | flops 402653184 | bytes 917504 | tf_op jit(solution)/shard_map/tn_rows/pallas_call | solution.py:394
  638.5 31.3 %collective-permute-start.52 = (bf16[1536,512]{1,0:T(8,128)(2,1)}, bf16[1536,512]{1,0:T(8,128)(2,1)S(1)}, u32[]{:S(2)}, u32[]{:S(2)}) collective-permute-start(bf16[1536,512]{1,0:T(8,128)(2,1)} %get-tuple-element.445), channel_id=1, source_target_pairs={{0,16},{8,24},{16,0},{24,8},{1,17},{9,25},{17,1},{25,9},{2,18},{10... | collective-permute-start | bytes 4718600 | tf_op jit(solution)/shard_map/ppermute | solution.py:125
  678.1 26.2 %collective-permute-done.52.b = bf16[1536,512]{1,0:T(8,128)(2,1)S(1)} collective-permute-done((bf16[1536,512]{1,0:T(8,128)(2,1)}, bf16[1536,512]{1,0:T(8,128)(2,1)S(1)}, u32[]{:S(2)}, u32[]{:S(2)}) %collective-permute-start.52) | collective-permute-done | bytes 1572896 | tf_op jit(solution)/shard_map/ppermute | solution.py:125
  704.3 7.8 collective-permute-done.50.f
  751.2 41.4 %collective-permute-done.57.refs_0_ = bf16[688,512]{1,0:T(8,128)(2,1)} collective-permute-done((bf16[688,512]{1,0:T(8,128)(2,1)}, bf16[688,512]{1,0:T(8,128)(2,1)}, u32[]{:S(2)}, u32[]{:S(2)}) %collective-permute-start.57) | collective-permute-done | bytes 704544 | tf_op jit(solution)/shard_map/ppermute | solution.py:1129
  804.4 19.5 %collective-permute-done.60 = f32[40,128]{1,0:T(8,128)S(1)} collective-permute-done((f32[40,128]{1,0:T(8,128)S(1)}, f32[40,128]{1,0:T(8,128)S(1)}, u32[]{:S(2)}, u32[]{:S(2)}) %collective-permute-start.60) | collective-permute-done | bytes 20512 | tf_op jit(solution)/shard_map/ppermute | solution.py:125
  (389 shorter events, 370.2 us)
Async XLA Ops:
  7.2 268.9 %all-gather.15.cloned.1.call-start = ((), (), s32[]{:S(2)}) async-start(), calls=%async_computation.6 | async-start | bytes 3522560 | tf_op jit(solution)/shard_map/all_gather | solution.py:176
  69.8 38.2 %collective-permute-start.17 = (bf16[2048,512]{1,0:T(8,128)(2,1)S(1)}, bf16[2048,512]{1,0:T(8,128)(2,1)}, u32[]{:S(2)}, u32[]{:S(2)}) collective-permute-start(bf16[2048,512]{1,0:T(8,128)(2,1)S(1)} %bitcast.67), channel_id=1, source_target_pairs={{0,16},{8,24},{16,0},{24,8},{1,17},{9,25},{17,1},{25,9},{2,18},{10... | collective-permute-start | bytes 6291464 | tf_op jit(solution)/shard_map/ppermute | solution.py:125
  110.0 39.4 %collective-permute-start.19 = (bf16[2048,512]{1,0:T(8,128)(2,1)}, bf16[2048,512]{1,0:T(8,128)(2,1)}, u32[]{:S(2)}, u32[]{:S(2)}) collective-permute-start(bf16[2048,512]{1,0:T(8,128)(2,1)} %collective-permute-done.17.refs_1_), channel_id=1, source_target_pairs={{0,8},{8,0},{16,24},{24,16},{1,9},{9,1},{17,25},{25,17},{2,10},{10... | collective-permute-start | bytes 6291464 | tf_op jit(solution)/shard_map/ppermute | solution.py:125
  110.0 39.4 %collective-permute-start.18 = (bf16[2048,512]{1,0:T(8,128)(2,1)S(1)}, bf16[2048,512]{1,0:T(8,128)(2,1)}, u32[]{:S(2)}, u32[]{:S(2)}) collective-permute-start(bf16[2048,512]{1,0:T(8,128)(2,1)S(1)} %bitcast.68), channel_id=1, source_target_pairs={{0,8},{8,0},{16,24},{24,16},{1,9},{9,1},{17,25},{25,17},{2,10},{10... | collective-permute-start | bytes 6291464 | tf_op jit(solution)/shard_map/ppermute | solution.py:125
  157.4 38.1 %collective-permute-start.23 = (bf16[688,512]{1,0:T(8,128)(2,1)S(1)}, bf16[688,512]{1,0:T(8,128)(2,1)}, u32[]{:S(2)}, u32[]{:S(2)}) collective-permute-start(bf16[688,512]{1,0:T(8,128)(2,1)S(1)} %copy-done.44), channel_id=1, source_target_pairs={{0,4},{1,5},{2,6},{3,7},{4,0},{5,1},{6,2},{7,3},{8,12},{9,13},{10,... | collective-permute-start | bytes 2113544 | tf_op jit(solution)/shard_map/ppermute | solution.py:1129
  201.3 116.5 %all-gather.17.cloned.1.call-start = ((), (), s32[]{:S(2)}) async-start(), calls=%async_computation.7 | async-start | bytes 3522560 | tf_op jit(solution)/shard_map/all_gather | solution.py:176
  237.8 38.3 %collective-permute-start.25 = (bf16[256,2048]{1,0:T(8,128)(2,1)}, bf16[256,2048]{1,0:T(8,128)(2,1)S(1)}, u32[]{:S(2)}, u32[]{:S(2)}) collective-permute-start(bf16[256,2048]{1,0:T(8,128)(2,1)} %get-tuple-element.356.refs_0_), channel_id=1, source_target_pairs={{0,1},{2,0},{3,2},{1,3},{4,5},{6,4},{7,6},{5,7},{8,9},{10,8},{11,1... | collective-permute-start | bytes 3145736 | tf_op jit(solution)/shard_map/ppermute | solution.py:81
  239.1 37.0 %collective-permute-start.24 = (bf16[256,2048]{1,0:T(8,128)(2,1)}, bf16[256,2048]{1,0:T(8,128)(2,1)}, u32[]{:S(2)}, u32[]{:S(2)}) collective-permute-start(bf16[256,2048]{1,0:T(8,128)(2,1)} %get-tuple-element.356.refs_0_), channel_id=1, source_target_pairs={{0,2},{2,3},{3,1},{1,0},{4,6},{6,7},{7,5},{5,4},{8,10},{10,11},{11... | collective-permute-start | bytes 3145736 | tf_op jit(solution)/shard_map/ppermute | solution.py:80
  276.1 68.7 %all-gather.19.cloned.1.call-start = ((), (), s32[]{:S(2)}) async-start(), calls=%async_computation.8 | async-start | bytes 3522560 | tf_op jit(solution)/shard_map/all_gather | solution.py:176
  276.2 36.9 %collective-permute-start.31 = (bf16[688,512]{1,0:T(8,128)(2,1)}, bf16[688,512]{1,0:T(8,128)(2,1)}, u32[]{:S(2)}, u32[]{:S(2)}) collective-permute-start(bf16[688,512]{1,0:T(8,128)(2,1)} %constant_dynamic-slice_fusion), channel_id=1, source_target_pairs={{0,4},{1,5},{2,6},{3,7},{4,0},{5,1},{6,2},{7,3},{8,12},{9,13},{10,... | collective-permute-start | bytes 2113544 | tf_op jit(solution)/shard_map/ppermute | solution.py:1129
  456.4 41.5 %collective-permute-start.38 = (bf16[1536,1024]{1,0:T(8,128)(2,1)}, bf16[1536,1024]{1,0:T(8,128)(2,1)}, u32[]{:S(2)}, u32[]{:S(2)}) collective-permute-start(bf16[1536,1024]{1,0:T(8,128)(2,1)} %get-tuple-element.377), channel_id=1, source_target_pairs={{0,8},{8,0},{16,24},{24,16},{1,9},{9,1},{17,25},{25,17},{2,10},{10... | collective-permute-start | bytes 9437192 | tf_op jit(solution)/shard_map/ppermute | solution.py:125
  456.4 41.4 %all-to-all-start.1 = ((bf16[8,256,256]{2,1,0:T(8,128)(2,1)}), bf16[8,256,256]{2,1,0:T(8,128)(2,1)S(1)}, u32[]{:S(2)}, u32[]{:S(2)}) async-start(bf16[8,256,256]{2,1,0:T(8,128)(2,1)} %get-tuple-element.371), calls=%async_computation.1 | async-start | bytes 2097152 | tf_op jit(solution)/shard_map/all_to_all | solution.py:1258
  461.1 170.6 %reduce-scatter.3.cloned.1.call-start = ((), (), s32[]{:S(2)}) async-start(), calls=%async_computation.4 | async-start | bytes 10485760 | tf_op jit(solution)/shard_map/reduce_scatter | solution.py:1285
  538.3 208.1 %all-gather.21.cloned.1.call-start = ((), (), s32[]{:S(2)}) async-start(), calls=%async_computation.9 | async-start | bytes 3522560 | tf_op jit(solution)/shard_map/all_gather | solution.py:176
  538.3 46.4 %collective-permute-start.45 = (bf16[1536,512]{1,0:T(8,128)(2,1)}, bf16[1536,512]{1,0:T(8,128)(2,1)S(1)}, u32[]{:S(2)}, u32[]{:S(2)}) collective-permute-start(bf16[1536,512]{1,0:T(8,128)(2,1)} %get-tuple-element.390), channel_id=1, source_target_pairs={{0,16},{8,24},{16,0},{24,8},{1,17},{9,25},{17,1},{25,9},{2,18},{10... | collective-permute-start | bytes 4718600 | tf_op jit(solution)/shard_map/ppermute | solution.py:125
  545.6 39.1 %collective-permute-start.43 = (bf16[256,2048]{1,0:T(8,128)(2,1)}, bf16[256,2048]{1,0:T(8,128)(2,1)S(1)}, u32[]{:S(2)}, u32[]{:S(2)}) collective-permute-start(bf16[256,2048]{1,0:T(8,128)(2,1)} %get-tuple-element.404), channel_id=1, source_target_pairs={{0,2},{2,3},{3,1},{1,0},{4,6},{6,7},{7,5},{5,4},{8,10},{10,11},{11... | collective-permute-start | bytes 3145736 | tf_op jit(solution)/shard_map/ppermute | solution.py:105
  547.1 38.9 %collective-permute-start.44 = (bf16[256,2048]{1,0:T(8,128)(2,1)}, bf16[256,2048]{1,0:T(8,128)(2,1)S(1)}, u32[]{:S(2)}, u32[]{:S(2)}) collective-permute-start(bf16[256,2048]{1,0:T(8,128)(2,1)} %get-tuple-element.405), channel_id=1, source_target_pairs={{0,1},{2,0},{3,2},{1,3},{4,5},{6,4},{7,6},{5,7},{8,9},{10,8},{11,1... | collective-permute-start | bytes 3145736 | tf_op jit(solution)/shard_map/ppermute | solution.py:106
  547.6 38.4 %collective-permute-start.42 = (bf16[1024,512]{1,0:T(8,128)(2,1)S(1)}, bf16[1024,512]{1,0:T(8,128)(2,1)S(1)}, u32[]{:S(2)}, u32[]{:S(2)}) collective-permute-start(bf16[1024,512]{1,0:T(8,128)(2,1)S(1)} %pad_maximum_fusion.2), channel_id=1, source_target_pairs={{8,0},{16,8},{24,16},{9,1},{17,9},{25,17},{10,2},{18,10},{26,18},{... | collective-permute-start | bytes 3145736 | tf_op jit(solution)/shard_map/ppermute | solution.py:195
  605.5 187.2 %reduce-scatter.5.cloned.1.call-start = ((), (), s32[]{:S(2)}) async-start(), calls=%async_computation.5 | async-start | bytes 2359296 | tf_op jit(solution)/shard_map/reduce_scatter | solution.py:1312
  631.7 202.8 %all-gather.23.cloned.1.call-start = ((), (), s32[]{:S(2)}) async-start(), calls=%async_computation.10 | async-start | bytes 3522560 | tf_op jit(solution)/shard_map/all_gather | solution.py:176
  638.4 219.0 %all-gather.25.cloned.1.call-start = ((), (), s32[]{:S(2)}) async-start(), calls=%async_computation.11 | async-start | bytes 1310720 | tf_op jit(solution)/shard_map/all_gather | solution.py:176
  638.5 65.8 %collective-permute-start.52 = (bf16[1536,512]{1,0:T(8,128)(2,1)}, bf16[1536,512]{1,0:T(8,128)(2,1)S(1)}, u32[]{:S(2)}, u32[]{:S(2)}) collective-permute-start(bf16[1536,512]{1,0:T(8,128)(2,1)} %get-tuple-element.445), channel_id=1, source_target_pairs={{0,16},{8,24},{16,0},{24,8},{1,17},{9,25},{17,1},{25,9},{2,18},{10... | collective-permute-start | bytes 4718600 | tf_op jit(solution)/shard_map/ppermute | solution.py:125
  669.8 44.9 %collective-permute-start.53 = (bf16[1024,768]{1,0:T(8,128)(2,1)}, bf16[1024,768]{1,0:T(8,128)(2,1)S(1)}, u32[]{:S(2)}, u32[]{:S(2)}) collective-permute-start(bf16[1024,768]{1,0:T(8,128)(2,1)} %get-tuple-element.446), channel_id=1, source_target_pairs={{0,8},{8,0},{16,24},{24,16},{1,9},{9,1},{17,25},{25,17},{2,10},{10... | collective-permute-start | bytes 4718600 | tf_op jit(solution)/shard_map/ppermute | solution.py:125
  670.0 42.2 %collective-permute-start.50 = (bf16[256,2048]{1,0:T(8,128)(2,1)}, bf16[256,2048]{1,0:T(8,128)(2,1)S(1)}, u32[]{:S(2)}, u32[]{:S(2)}) collective-permute-start(bf16[256,2048]{1,0:T(8,128)(2,1)} %get-tuple-element.440), channel_id=1, source_target_pairs={{0,2},{2,4},{4,6},{6,7},{7,5},{5,3},{3,1},{1,0},{8,10},{10,12},{12... | collective-permute-start | bytes 3145736 | tf_op jit(solution)/shard_map/ppermute | solution.py:105
  671.9 42.9 %collective-permute-start.51 = (bf16[256,2048]{1,0:T(8,128)(2,1)S(1)}, bf16[256,2048]{1,0:T(8,128)(2,1)S(1)}, u32[]{:S(2)}, u32[]{:S(2)}) collective-permute-start(bf16[256,2048]{1,0:T(8,128)(2,1)S(1)} %copy-done.64), channel_id=1, source_target_pairs={{0,1},{2,0},{4,2},{6,4},{7,6},{5,7},{3,5},{1,3},{8,9},{10,8},{12,1... | collective-permute-start | bytes 3145736 | tf_op jit(solution)/shard_map/ppermute | solution.py:106
  727.4 65.2 %collective-permute-start.54 = (bf16[256,2048]{1,0:T(8,128)(2,1)}, bf16[256,2048]{1,0:T(8,128)(2,1)}, u32[]{:S(2)}, u32[]{:S(2)}) collective-permute-start(bf16[256,2048]{1,0:T(8,128)(2,1)} %get-tuple-element.458), channel_id=1, source_target_pairs={{0,2},{2,4},{4,6},{6,7},{7,5},{5,3},{3,1},{1,0},{8,10},{10,12},{12... | collective-permute-start | bytes 3145736 | tf_op jit(solution)/shard_map/ppermute | solution.py:105
  729.2 63.4 %collective-permute-start.55 = (bf16[256,2048]{1,0:T(8,128)(2,1)}, bf16[256,2048]{1,0:T(8,128)(2,1)}, u32[]{:S(2)}, u32[]{:S(2)}) collective-permute-start(bf16[256,2048]{1,0:T(8,128)(2,1)} %get-tuple-element.459), channel_id=1, source_target_pairs={{0,1},{2,0},{4,2},{6,4},{7,6},{5,7},{3,5},{1,3},{8,9},{10,8},{12,1... | collective-permute-start | bytes 3145736 | tf_op jit(solution)/shard_map/ppermute | solution.py:106
  730.3 62.3 %collective-permute-start.56 = (bf16[512,768]{1,0:T(8,128)(2,1)}, bf16[512,768]{1,0:T(8,128)(2,1)}, u32[]{:S(2)}, u32[]{:S(2)}) collective-permute-start(bf16[512,768]{1,0:T(8,128)(2,1)} %get-tuple-element.454), channel_id=1, source_target_pairs={{0,16},{8,24},{16,0},{24,8},{1,17},{9,25},{17,1},{25,9},{2,18},{10... | collective-permute-start | bytes 2359304 | tf_op jit(solution)/shard_map/ppermute | solution.py:125
  735.3 57.3 %collective-permute-start.57 = (bf16[688,512]{1,0:T(8,128)(2,1)}, bf16[688,512]{1,0:T(8,128)(2,1)}, u32[]{:S(2)}, u32[]{:S(2)}) collective-permute-start(bf16[688,512]{1,0:T(8,128)(2,1)} %slice.143), channel_id=1, source_target_pairs={{0,4},{1,5},{2,6},{3,7},{4,0},{5,1},{6,2},{7,3},{8,12},{9,13},{10,... | collective-permute-start | bytes 2113544 | tf_op jit(solution)/shard_map/ppermute | solution.py:1129
  792.7 67.6 %all-gather.27.cloned.1.call-start = ((), (), s32[]{:S(2)}) async-start(), calls=%async_computation.12 | async-start | bytes 3522560 | tf_op jit(solution)/shard_map/all_gather | solution.py:176
  799.8 44.4 %collective-permute-start.58 = (bf16[256,2048]{1,0:T(8,128)(2,1)}, bf16[256,2048]{1,0:T(8,128)(2,1)S(1)}, u32[]{:S(2)}, u32[]{:S(2)}) collective-permute-start(bf16[256,2048]{1,0:T(8,128)(2,1)} %get-tuple-element.474), channel_id=1, source_target_pairs={{0,2},{2,4},{4,6},{6,7},{7,5},{5,3},{3,1},{1,0},{8,10},{10,12},{12... | collective-permute-start | bytes 3145736 | tf_op jit(solution)/shard_map/ppermute | solution.py:105
  799.9 44.4 %collective-permute-start.59 = (bf16[256,2048]{1,0:T(8,128)(2,1)}, bf16[256,2048]{1,0:T(8,128)(2,1)S(1)}, u32[]{:S(2)}, u32[]{:S(2)}) collective-permute-start(bf16[256,2048]{1,0:T(8,128)(2,1)} %get-tuple-element.475), channel_id=1, source_target_pairs={{0,1},{2,0},{4,2},{6,4},{7,6},{5,7},{3,5},{1,3},{8,9},{10,8},{12,1... | collective-permute-start | bytes 3145736 | tf_op jit(solution)/shard_map/ppermute | solution.py:106
  (113 other events, 1597.3 us)
Sparse Core Ops, SparseCore 0:
  195.6 27.1 all-gather.14
  276.3 27.1 all-gather.16
  318.0 26.7 all-gather.18
  538.4 93.1 reduce-scatter.2
  633.1 30.9 all-gather.20
  667.9 83.5 reduce-scatter.4
  753.1 27.6 all-gather.22
  792.8 15.0 all-gather.24
  809.6 30.1 all-gather.26

commit v3 on v2

--- a/solution.py
+++ b/solution.py
@@ -41,11 +41,12 @@
     ]
 
 
-def owners(cycles):
+def owners(cycles, rels=None):
     table = {}
     for cyc in cycles:
         for i, dev in enumerate(cyc):
-            table[dev] = [cyc[(i + rel) % len(cyc)] for rel in range(len(cyc))]
+            steps = range(len(cyc)) if rels is None else rels
+            table[dev] = [cyc[(i + rel) % len(cyc)] for rel in steps]
     rows = jnp.array([table[t] for t in range(len(table))], jnp.int32)
     return rows[lax.axis_index("tensor")]
 
@@ -97,7 +98,7 @@
         self.size = len(cycles[0])
         self.ahead, self.back = step_pairs(cycles, 1), step_pairs(cycles, -1)
         self.k = self.size // 2
-        half = far.shape[0] // 2
+        half = self.half = far.shape[0] // 2
         self.sent = lax.optimization_barrier((far[:half], far[half:]))
         self.send()
 
@@ -105,10 +106,10 @@
         self.f = lax.ppermute(self.sent[0], "tensor", self.ahead)
         self.b = lax.ppermute(self.sent[1], "tensor", self.back)
 
-    def step(self, near, first, *deps):
+    def step(self, near, first, *deps, at=0):
         f, b, near = lax.optimization_barrier((self.f, self.b, near) + deps)[:3]
         self.k -= 1
-        self.sent = ring_add(near, f, b, first)
+        self.sent = ring_add(near, f, b, first, 2 * self.half, at)
         self.send()
 
 
@@ -182,11 +183,8 @@
     return out
 
 
-def sum_all(value):
-    for axis in ("tensor", "dp"):
-        for bit in bits_of(lax.axis_size(axis)):
-            value = value + swap(value, axis, bit)
-    return value
+def hops():
+    return [(a, bit) for a in ("tensor", "dp") for bit in bits_of(lax.axis_size(a))]
 
 
 def shifted(value, axis, steps):
@@ -371,6 +369,53 @@
     )(dp_side(1), a, b)
 
 
+def pick_body(idx, src, out):
+    out[...] = src[...]
+
+
+def pick_rows(places, src):
+    n = places.shape[0]
+    rows, cols = src.shape[0] // n, src.shape[1]
+    return pl.pallas_call(
+        pick_body,
+        grid_spec=pltpu.PrefetchScalarGridSpec(
+            num_scalar_prefetch=1,
+            grid=(n,),
+            in_specs=[pl.BlockSpec((rows, cols), lambda j, idx: (idx[j], 0))],
+            out_specs=pl.BlockSpec((rows, cols), lambda j, idx: (j, 0)),
+        ),
+        out_shape=jax.ShapeDtypeStruct(src.shape, src.dtype),
+        compiler_params=params("arbitrary"),
+        cost_estimate=cost(flops=0, bytes_accessed=4 * src.size, transcendentals=0),
+        name="pick_rows",
+    )(places, src)
+
+
+def tn_whole_body(a, b, out):
+    out[...] = dot_tn(a[...], b[...]).astype(BF16)
+
+
+def tn_whole(a, b):
+    k, m = a.shape
+    cols = b.shape[1]
+    w = cols // 4
+    return pl.pallas_call(
+        tn_whole_body,
+        grid=(4,),
+        in_specs=[
+            pl.BlockSpec((k, m), lambda j: (0, 0)),
+            pl.BlockSpec((k, w), lambda j: (0, j)),
+        ],
+        out_specs=pl.BlockSpec((m, w), lambda j: (0, j)),
+        out_shape=jax.ShapeDtypeStruct((m, cols), BF16),
+        compiler_params=params("arbitrary"),
+        cost_estimate=cost(
+            flops=2 * k * m * cols, bytes_accessed=2 * (k * m + k * cols + m * cols), transcendentals=0
+        ),
+        name="tn_whole",
+    )(a, b)
+
+
 def tn_rows_body(n, idx, a, b, w, send, keep, sums):
     j = pl.program_id(0)
     out = dot_tn(a[...], b[...])
@@ -479,13 +524,13 @@
         b_out[: rows - n, :] = behind[: rows - n].astype(BF16)
 
 
-def ring_add(near, f, b, first):
-    rows, cols = near.shape[0] // 2, near.shape[1]
+def ring_add(near, f, b, first, rows, at):
+    cols = near.shape[1]
     whole = lambda a: pl.BlockSpec(a.shape, lambda i: (0, 0))
     return pl.pallas_call(
         functools.partial(ring_add_body, first),
         grid=(1,),
-        in_specs=[whole(near), whole(f), whole(b)],
+        in_specs=[pl.BlockSpec((2 * rows, cols), lambda i: (at, 0)), whole(f), whole(b)],
         out_specs=[pl.BlockSpec((rows, cols), lambda i: (0, 0))] * 2,
         out_shape=[jax.ShapeDtypeStruct((rows, cols), BF16)] * 2,
         compiler_params=params("arbitrary"),
@@ -1132,17 +1177,17 @@
         return lax.dynamic_slice_in_dim(value, dp_idx * part_cols, part_cols, 1)
 
     ring_owners = owners(ring)
+    ring_pairs = owners(ring, [r for k in range(far - 1, 0, -1) for r in (k, -k)] + [far, 0])
     x_f = tokens.astype(F32)
     x_normed, x_unit, x_inv = norm_forward(x_f, attn_gain)
     x_low = x_normed.astype(BF16)
     go = Gather(dp_cols(w_out), ring)
-    go.all()
     w_joint = jnp.concatenate([w_key, w_value, w_query], axis=1)
-    gx = Gather(after(x_low, go.f, go.b), ring)
+    gx = Gather(x_low, ring)
     gx.step()
-    w_out_part = place_chunks(ring_owners, go.chunks, n_tensor)
+    go.step(x_low)
     cos, sin = rope_tables(first_pos + jnp.arange(block_len, dtype=jnp.int32))
-    cos, sin = after(cos, w_joint, w_out_part), after(sin, w_joint)
+    cos, sin = after(cos, w_joint, x_low), after(sin, w_joint)
 
     def qkv(rel, bufs):
         return qkv_chunk(
@@ -1150,20 +1195,20 @@
         )
 
     bufs = qkv(0, None)
-    for k in range(1, far):
-        came = (gx.f, gx.b)
-        gx.step(bufs[0])
+    for k in range(1, far + 1):
+        gx.f, gx.b, go.f, go.b, bufs = together(gx.f, gx.b, go.f, go.b, tuple(bufs))
+        if k == far:
+            break
         if k == 1:
-            seg_tail = after(segments[block_len - WINDOW :].astype(F32), *came)
+            seg_tail = after(segments[block_len - WINDOW :].astype(F32), gx.f, gx.b)
             prev_seg = shifted(seg_tail, "dp", 1).astype(jnp.int32)
-            w_out_part = w_out_part.reshape(n_tensor * head_cols, part_cols)
-            low_bits = bits_of(n_dp)
-            w_spread = spread_parts([(0, w_out_part)], low_bits[-1:])
-        if k == far - 1:
-            w_spread = spread_parts(w_spread, low_bits[:-1], *came)
+        gx.step()
+        go.step()
         bufs = qkv(k, qkv(-k, bufs))
-    w_places = jnp.stack([dp_idx ^ x for x, _ in w_spread]).astype(jnp.int32)
-    w_out_parts = [w for _, w in w_spread]
+    w_out_part = place_chunks(after(ring_owners, go.f, go.b), go.chunks, n_tensor)
+    w_out_part = w_out_part.reshape(n_tensor * head_cols, part_cols)
+    low_bits = bits_of(n_dp)
+    w_spread = spread_parts([(0, w_out_part)], low_bits[-1:])
 
     seg_all = jnp.concatenate([prev_seg, segments], axis=0)
     low_key = jnp.sum((seg_all[None, :] < segments[:, None]).astype(jnp.int32), axis=1)
@@ -1174,13 +1219,11 @@
     low_col, low_row = low_key[:, None], low_key[None, :]
 
     came = (gx.f, gx.b)
-    mine, low_col, low_row, *w_out_parts = lax.optimization_barrier(
-        (tuple(dp_cols(w) for w in own_w), low_col, low_row, *w_out_parts)
-    )
+    mine, low_col, low_row = together(tuple(dp_cols(w) for w in own_w), low_col, low_row)
     first = after(mine[0], *came)
     gate_got = [to_group(first, s) for s in range(1, groups)]
     bufs = list(bufs)
-    bufs[0] = after(bufs[0], low_col, low_row, first, *w_out_parts)
+    bufs[0] = after(bufs[0], low_col, low_row, first, w_out_part)
     bufs = qkv(far, bufs)
     query, key_value, x_all = bufs
     tail_kv = after(key_value[block_len - WINDOW :])
@@ -1188,18 +1231,23 @@
     gy = Gather(after(cotangent, *came), square)
     gy.step()
 
-    late, early = ((key_value, 0), (key_value, 1)), ((prev, 0), (key_value, 0))
+    late = ((key_value, 0), (key_value, 1))
     heads_late = attend(1, query, late, low_col, None)
-    gy_came = (gy.f, gy.b)
-    heads_late = after(heads_late, *gy_came)
+    heads_late, prev, gy.f, gy.b = together(heads_late, prev, gy.f, gy.b)
+    early = ((prev, 0), (key_value, 0))
     heads_low = attend(0, query, early, low_col, heads_late)
     heads_low = heads_low.reshape(n_tensor, rows, head_cols)
-    heads_low = after(heads_low, *gate_got)
+    w_first = w_spread[-1][1]
+    heads_low, w_first, *gate_got = together(heads_low, w_first, *gate_got)
+    w_spread[-1] = (w_spread[-1][0], w_first)
 
     heads_got = lax.all_to_all(heads_low, "tensor", split_axis=0, concat_axis=0, tiled=True)
-    gate_all_got = [all_dp(after(g, heads_low)) for g in gate_got]
+    w_spread = spread_parts(w_spread, low_bits[:-1], heads_low)
+    w_places = jnp.stack([dp_idx ^ x for x, _ in w_spread]).astype(jnp.int32)
+    heads_got, *w_out_parts = together(heads_got, *[w for _, w in w_spread])
     second = after(mine[1], heads_got)
     up_got = [to_group(second, s) for s in range(1, groups)]
+    gate_all_got = [all_dp(after(g, heads_low)) for g in gate_got]
     gy.step(heads_got)
     y_chunks = gy.chunks
     attn_branch, mid, h_low, my_heads = out_project(
@@ -1276,54 +1324,43 @@
 
     grad_heads = after(grad_heads, red_down.value, *sf.sent, red_gate.sent)
     d_joint, bk, bv = attend_back(0, query, grad_heads, early, low_row, cos, sin, None)
-    d_joint, bk, bv, sf.f, sf.b, red_up.got = together(d_joint, bk, bv, sf.f, sf.b, red_up.got)
+    d_joint, bk, bv, sf.f, sf.b, red_up.got, red_gate.got, *down_back = together(
+        d_joint, bk, bv, sf.f, sf.b, red_up.got, red_gate.got, *down_back
+    )
+    red_gate.finish()
+    gate_back = send_back(red_gate)
     back = after(jnp.concatenate([bk[:WINDOW], bv[:WINDOW]], axis=1).astype(BF16))
     got_back = shifted(back, "dp", -1)
-    sf.step(after(sf_all[: 2 * rows], back), False)
+    sf.step(after(sf_all, back), False)
     red_up.add()
-    out_local = dot_tn(my_heads, after(grad_mid_low, back)).astype(BF16)
+    red_up.send(back)
+    d_joint, ak, av = attend_back(
+        1, query, after(grad_heads, back, *sf.sent, red_up.sent, red_gate.value),
+        late, low_row, cos, sin, d_joint,
+    )
+    d_joint, ak, av, got_back, sf.f, sf.b, red_up.got, *gate_back = together(
+        d_joint, ak, av, got_back, sf.f, sf.b, red_up.got, *gate_back
+    )
+    out_local = tn_whole(my_heads, after(grad_mid_low, ak))
     out_dp = lax.psum_scatter(out_local, "dp", scatter_dimension=1, tiled=True)
-    d_joint, ak, av = attend_back(
-        1, query, after(grad_heads, back, *sf.sent, red_up.sent, out_local),
-        late, low_row, cos, sin, d_joint,
-    )
-    d_joint, ak, av, got_back, sf.f, sf.b, red_gate.got, *down_back = together(
-        d_joint, ak, av, got_back, sf.f, sf.b, red_gate.got, *down_back
-    )
-    red_gate.finish()
-    gate_back = send_back(red_gate)
-    red_up.send(red_gate.value)
-    d_joint = finish_keys(0, after(ak, red_gate.value), av, (bk, 1, 0), (bv, 1, 0), cos, sin, d_joint)
+    ak = after(ak, out_local)
+    d_joint = finish_keys(0, ak, av, (bk, 1, 0), (bv, 1, 0), cos, sin, d_joint)
     d_joint = finish_keys(1, ak, av, (got_back, 0, 0), (got_back, 0, 1), cos, sin, d_joint)
 
     def terms(rels, kind, *deps):
         rels = [r % n_tensor for r in rels]
         return grad_x_terms(after(ring_owners, *deps), rels, d_joint, w_joint, rows, kind)
 
-    sx = Scatter(terms([far], BF16), ring)
-    near = terms([far - 1, 1 - far], F32, *sx.sent)
-    down_own = shard_sum(after(red_down.value, *sx.sent), down_back, units)
+    red_up.finish(out_local)
+    up_back = send_back(red_up)
+    sx = Scatter(after(terms([far], BF16), red_up.value), ring)
+    near = terms([far - 1, 1 - far], F32, red_up.value)
+    down_own = shard_sum(after(red_down.value, red_up.value), down_back, units)
     down_dp = all_dp(down_own)
+    gate_own = shard_sum(after(red_gate.value, down_own), gate_back, units)
+    gate_dp = all_dp(gate_own)
     joint = tn_rows(after(x_all, *sx.sent), d_joint, w_joint)
     grad_attn_gain = joint[2][:, 0] / attn_gain
-    sx.f, sx.b, near, down_own, joint, out_dp, *gate_back = together(
-        sx.f, sx.b, near, down_own, tuple(joint), out_dp, *gate_back
-    )
-    out_own = lax.psum_scatter(out_dp, "tensor", scatter_dimension=0, tiled=True)
-    red_joint = Halves(*joint[:2], 0)
-    red_joint.send()
-    sx.step(near, True)
-    gate_own = shard_sum(after(red_gate.value, *sx.sent), gate_back, units)
-    gate_dp = all_dp(gate_own)
-    near = terms([far - 2, 2 - far], F32, gate_own)
-    sx.f, sx.b, near, red_up.got, red_joint.got, gate_own = together(
-        sx.f, sx.b, near, red_up.got, red_joint.got, gate_own
-    )
-    red_up.finish()
-    red_joint.add()
-    up_back = send_back(red_up)
-    red_joint.send()
-    sx.step(near, True, red_up.value, red_joint.sent)
     ffn_branch = after(sf_all[2 * rows : 3 * rows], *sx.sent).astype(F32)
     ffn_branch = ffn_branch + sf.f.astype(F32) + sf.b.astype(F32)
     result = mid + ffn_branch
@@ -1342,24 +1379,53 @@
     table = jnp.dot(per_row.T, one_hot, precision=lax.Precision.HIGHEST, preferred_element_type=F32)
     packed = jnp.concatenate([grad_attn_gain, grad_ffn_gain[0], table.reshape(-1)])
     packed = jnp.pad(packed, (0, -packed.shape[0] % 1024)).reshape(-1, 128)
-    near = terms([far - 3, 3 - far], F32, packed)
+    sx.f, sx.b, near, down_own, gate_own, joint, packed, out_dp, *up_back = together(
+        sx.f, sx.b, near, down_own, gate_own, tuple(joint), packed, out_dp, *up_back
+    )
+    red_joint = Halves(*joint[:2], 0)
+    red_joint.send()
+    far_out = lax.dynamic_slice_in_dim(out_dp, ring_owners[far] * head_cols, head_cols)
+    so = Scatter(far_out, ring)
+    todo = hops()
+    hop = swap(after(packed, red_joint.got), *todo[0])
+    sx.step(near, True)
+    up_own = shard_sum(after(red_up.value, *sx.sent), up_back, units)
+    up_dp = all_dp(up_own)
+    near = terms([far - 2, 2 - far], F32, up_own)
+    picked = pick_rows(after(ring_pairs, near), out_dp)
+    sx.f, sx.b, near, red_joint.got, up_own, picked, hop, so.f, so.b = together(
+        sx.f, sx.b, near, red_joint.got, up_own, picked, hop, so.f, so.b
+    )
+    packed = packed + hop
+    so.step(picked, True, at=0)
+    red_joint.add()
+    red_joint.send()
+    sx.step(near, True, red_joint.sent)
+    near = terms([far - 3, 3 - far], F32, *sx.sent)
     grad_w_down = widen_cols(after(down_dp, near))
-    sx.f, sx.b, near, red_joint.got, grad_w_down, out_own, *up_back = together(
-        sx.f, sx.b, near, red_joint.got, grad_w_down, out_own, *up_back
-    )
-    out_all = all_dp(out_own)
+    sx.f, sx.b, near, red_joint.got, grad_w_down, so.f, so.b = together(
+        sx.f, sx.b, near, red_joint.got, grad_w_down, so.f, so.b
+    )
+    so.step(picked, True, at=1)
     sx.step(near, True)
     for k in range(far - 4, 0, -1):
         sx.step(terms([k, -k], F32, *sx.sent), True)
-    up_own = shard_sum(after(red_up.value, *sx.sent), up_back, units)
-    up_dp = all_dp(up_own)
-    red_joint.finish(*sx.sent)
-    joint_parts = spread_parts([(0, red_joint.value)], bits_of(n_dp)[::-1])
+    red_joint.finish()
+    joint_parts = spread_parts([(0, red_joint.value)], low_bits[-1:])
+    grad_w_gate = widen_cols(after(gate_dp, red_joint.value)).T
+    own = terms([0], F32, grad_w_gate)
+    sx.f, sx.b, own, so.f, so.b, joint_first = together(
+        sx.f, sx.b, own, so.f, so.b, joint_parts[-1][1]
+    )
+    joint_parts[-1] = (joint_parts[-1][0], joint_first)
+    joint_parts = spread_parts(joint_parts, low_bits[:-1][::-1])
     joint_places = jnp.stack([place_of(dp_idx ^ x, n_dp) for x, _ in joint_parts])
-    grad_w_gate = widen_cols(after(gate_dp, up_own, red_joint.value)).T
-    own = terms([0], F32, grad_w_gate)
-    packed = sum_all(after(packed, *sx.sent))
-    sx.f, sx.b, own, packed = together(sx.f, sx.b, own, packed)
+    for i in range(2, far - 1):
+        so.step(picked, True, at=i)
+    for axis, bit in todo[1:]:
+        packed = packed + swap(after(packed, sx.f, sx.b), axis, bit)
+    out_own = picked[-head_cols:].astype(F32) + so.f.astype(F32) + so.b.astype(F32)
+    out_all = all_dp(out_own.astype(BF16))
     input_grad = input_grad_of(own, sx.f, sx.b, grad_mid, tokens, attn_gain)
     grad_w_out = jnp.concatenate(list(out_all), axis=1).astype(F32)
     grad_w_key, grad_w_value, grad_w_query = widen_pieces(

time: 882 us -> 848 us (0.961)
  starting transfers between devices: 116 us -> 86.8 us
  waiting for transfers between devices: 274 us -> 250 us
  Pallas kernels: 392 us -> 413 us
    ppermute x19, waiting for transfers between devices: 79.4 us -> 17.7 us  [swap(): return lax.ppermute(value, axis, [(d, d ^ bit) for d in range(count)])]
    ppermute x8 -> x12, waiting for transfers between devices: 18.4 us -> 51.5 us  [send(): self.f = lax.ppermute(self.sent[0], 'tensor', self.ahead)]
    ppermute x19, starting transfers between devices: 37.8 us -> 9.18 us  [swap(): return lax.ppermute(value, axis, [(d, d ^ bit) for d in range(count)])]
    ppermute x8, waiting for transfers between devices: 21.3 us -> 39.3 us  [step(): self.f = lax.ppermute(f, 'tensor', self.ahead)]
    ppermute x8, waiting for transfers between devices: 23.6 us -> 7.49 us  [step(): self.b = lax.ppermute(b, 'tensor', self.back)]
    pallas_call x0 -> x2, Pallas kernels: none -> 13.2 us  [the longest x1 6.91 us: tn_whole(): pl.pallas_call(tn_whole_body, grid=(4,), in_specs=[pl.BlockSpec((k, m), l...]
    ppermute x8 -> x12, starting transfers between devices: 11.5 us -> 18.8 us  [send(): self.f = lax.ppermute(self.sent[0], 'tensor', self.ahead)]
    pallas_call x5 -> x8, Pallas kernels: 20.3 us -> 26.7 us  [ring_add(): pl.pallas_call(functools.partial(ring_add_body, first), grid=(1,), in_spe...]
  transfers between devices with their start and end apart: 79 -> 86, of which waited for: 35 -> 37; matrix products, arithmetic and copies ran while one was open for 6% -> 5% of each run, Pallas kernels for 38% -> 41%
where the time goes in v3:
time: 848 us; the launch traced here: 831 us
  Pallas kernels  413 us (49%)
  waiting for transfers between devices  250 us (29%)
  starting transfers between devices  86.8 us (10%)
  local copies, waits for them, and re-layouts  39.2 us (5%)
  other arithmetic  25.9 us (3%)
  between operations  16 us (2%)
    pallas_call x6, Pallas kernels, ffn_set(): pl.pallas_call(functools.partial(ffn_body, n_in, n_w, first, units, len(h...  81.6 us
    ppermute x6, waiting for transfers between devices, to_group(): return lax.ppermute(piece, 'tensor', pairs)  69.4 us
    ppermute x12, waiting for transfers between devices, send(): self.f = lax.ppermute(self.sent[0], 'tensor', self.ahead)  51.5 us
    pallas_call x8, Pallas kernels, qkv_chunk(): pl.pallas_call(functools.partial(qkv_body, n_in), grid_spec=pltpu.Prefetc...  40.3 us
    ppermute x8, waiting for transfers between devices, step(): self.f = lax.ppermute(f, 'tensor', self.ahead)  39.3 us
    pallas_call x3, Pallas kernels, tn_cols(): pl.pallas_call(functools.partial(tn_cols_body, n), grid_spec=pltpu.Prefet...  38.2 us
    pallas_call x2, Pallas kernels, attend_back(): pl.pallas_call(attend_back_body, grid=(heads, blocks), in_specs=in_specs,...  35.6 us
    pallas_call x5, Pallas kernels, grad_x_terms(): pl.pallas_call(grad_x_body, grid_spec=pltpu.PrefetchScalarGridSpec(num_sc...  28.3 us
  transfers between devices with their start and end apart: 86, of which 37 were waited for; matrix products, arithmetic and copies ran while one was open for 5% of the time, Pallas kernels for 41%

profile of v3, /device:TPU:0, one launch (start us, length us, event | category | flops | bytes accessed | tf_op | source)
XLA Modules:
  0.0 831.4 jit_solution(17590671993900878655)
XLA Ops:
  31.5 11.8 %collective-permute-done.refs_0_ = bf16[256,2048]{1,0:T(8,128)(2,1)} collective-permute-done((bf16[256,2048]{1,0:T(8,128)(2,1)}, bf16[256,2048]{1,0:T(8,128)(2,1)}, u32[]{:S(2)}, u32[]{:S(2)}) %collective-permute-start) | collective-permute-done | bytes 1048608 | tf_op jit(solution)/shard_map/ppermute | solution.py:81
  58.9 15.4 %collective-permute-done.6.refs_3_ = bf16[256,512]{1,0:T(8,128)(2,1)S(1)} collective-permute-done((bf16[256,512]{1,0:T(8,128)(2,1)}, bf16[256,512]{1,0:T(8,128)(2,1)S(1)}, u32[]{:S(2)}, u32[]{:S(2)}) %collective-permute-start.6) | collective-permute-done | bytes 262176 | tf_op jit(solution)/shard_map/ppermute | solution.py:81
  93.6 10.2 %collective-permute-done.10.refs_5_ = bf16[256,512]{1,0:T(8,128)(2,1)S(1)} collective-permute-done((bf16[256,512]{1,0:T(8,128)(2,1)S(1)}, bf16[256,512]{1,0:T(8,128)(2,1)S(1)}, u32[]{:S(2)}, u32[]{:S(2)}) %collective-permute-start.10) | collective-permute-done | bytes 262176 | tf_op jit(solution)/shard_map/ppermute | solution.py:81
  146.5 10.3 %attend.2.rest_0_ = bf16[2048,256]{1,0:T(8,128)(2,1)} custom-call(bf16[2048,256]{1,0:T(8,128)(2,1)} %get-tuple-element.386.q_ref, bf16[2048,512]{1,0:T(8,128)(2,1)} %get-tuple-element.387.k0.k1.v0.v1, bf16[2048,512]{1,0:T(8,128)(2,1)} %get-tuple-element.387.k0.k1.v0.v1, bf16[2048,512]{1,0:T(8,128)(2,1)} %get-tuple-element.387.k0.k1.v0.v1, ...), custom_call_target="tpu_custom_call" | custom-call | flops 83886080 | bytes 196608 | tf_op jit(solution)/shard_map/attend/pallas_call | solution.py:1012
  162.4 10.3 %attend.3 = bf16[2048,256]{1,0:T(8,128)(2,1)} custom-call(bf16[2048,256]{1,0:T(8,128)(2,1)} %get-tuple-element.386.q_ref, bf16[1024,512]{1,0:T(8,128)(2,1)} %copy-done.6, bf16[2048,512]{1,0:T(8,128)(2,1)} %get-tuple-element.387.k0.k1.v0.v1, bf16[1024,512]{1,0:T(8,128)(2,1)} %copy-done.6, ...), custom_call_target="tpu_custom_call", output_to_operand_aliasing={{}: (6, {})} | custom-call | flops 83886080 | bytes 196608 | tf_op jit(solution)/shard_map/attend/pallas_call | solution.py:1012
  172.7 7.7 collective-permute-done.21
  185.3 25.6 %all-to-all-done.heads = bf16[8,256,256]{2,1,0:T(8,128)(2,1)S(1)} async-done(((bf16[8,256,256]{2,1,0:T(8,128)(2,1)}), bf16[8,256,256]{2,1,0:T(8,128)(2,1)S(1)}, u32[]{:S(2)}, u32[]{:S(2)}) %all-to-all-start) | async-done | bytes 1048608 | tf_op jit(solution)/shard_map/all_to_all | solution.py:1244
  211.8 10.3 %out_project.1 = (f32[256,2048]{1,0:T(8,128)}, f32[256,2048]{1,0:T(8,128)}, bf16[256,2048]{1,0:T(8,128)(2,1)}, bf16[256,2048]{1,0:T(8,128)(2,1)}) custom-call(s32[4]{0:T(128)} %pad_add_fusion.1.idx, bf16[8,256,256]{2,1,0:T(8,128)(2,1)} %copy-done.16, bf16[256,2048]{1,0:T(8,128)(2,1)} %x_ref.3, f32[1,2048]{1,0:T(1,128)} %bitcast.81, ...), custom_call_target="tpu_custom_call" | custom-call | flops 134217728 | bytes 1048576 | tf_op jit(solution)/shard_map/out_project/pallas_call | solution.py:710
  224.9 11.1 %ffn_set.6 = (bf16[1024,2048]{1,0:T(8,128)(2,1)}, bf16[1024,2048]{1,0:T(8,128)(2,1)}, bf16[1024,1536]{1,0:T(8,128)(2,1)}, bf16[1024,1536]{1,0:T(8,128)(2,1)}, bf...) custom-call(bf16[256,2048]{1,0:T(8,128)(2,1)} %get-tuple-element.449.refs_0_, bf16[256,2048]{1,0:T(8,128)(2,1)} %dy.1, ...), custom_call_target="tpu_custom_call" | custom-call | flops 225443840 | bytes 1052672 | tf_op jit(solution)/shard_map/ffn_set/pallas_call | solution.py:889
  236.0 25.1 %collective-permute-done.30 = bf16[688,512]{1,0:T(8,128)(2,1)} collective-permute-done((bf16[688,512]{1,0:T(8,128)(2,1)S(1)}, bf16[688,512]{1,0:T(8,128)(2,1)}, u32[]{:S(2)}, u32[]{:S(2)}) %collective-permute-start.30) | collective-permute-done | bytes 704544 | tf_op jit(solution)/shard_map/ppermute | solution.py:1174
  272.2 17.8 %ffn_set.7 = (bf16[1024,2048]{1,0:T(8,128)(2,1)}, bf16[1024,2048]{1,0:T(8,128)(2,1)}, bf16[1024,1536]{1,0:T(8,128)(2,1)}, bf16[1024,1536]{1,0:T(8,128)(2,1)}, bf...) custom-call(bf16[256,2048]{1,0:T(8,128)(2,1)} %collective-permute-do, ...), custom_call_target="tpu_custom_call", output_to_operand_aliasing={{0}: (7, {}), {1}: (8, {}), {2}: (9, {}), {3}: (10, {}), {4... | custom-call | flops 450887680 | bytes 1576960 | tf_op jit(solution)/shard_map/ffn_set/pallas_call | solution.py:889
  294.5 7.6 collective-permute-done.27.refs_1_
  303.0 11.1 %ffn_set.8 = (bf16[1024,2048]{1,0:T(8,128)(2,1)}, bf16[1024,2048]{1,0:T(8,128)(2,1)}, bf16[1024,1536]{1,0:T(8,128)(2,1)}, bf16[1024,1536]{1,0:T(8,128)(2,1)}, bf...) custom-call(bf16[128,2048]{1,0:T(8,128)(2,1)} %copy-done.24, ...), custom_call_target="tpu_custom_call", output_to_operand_aliasing={{0}: (7, {}), {1}: (8, {}), {2}: (9, {}), {3}: (10, {}), {4... | custom-call | flops 225443840 | bytes 1052672 | tf_op jit(solution)/shard_map/ffn_set/pallas_call | solution.py:889
  314.1 17.1 %all-gather.19.cloned.1.call-done = bf16[2752,512]{1,0:T(8,128)(2,1)} async-done(((bf16[688,512]{1,0:T(8,128)(2,1)}), bf16[2752,512]{1,0:T(8,128)(2,1)}) %all-gather.19.cloned.1.call-update) | async-done | bytes 2818064 | tf_op jit(solution)/shard_map/all_gather | solution.py:177
  331.2 11.4 %ffn_set.9 = (bf16[1024,1536]{1,0:T(8,128)(2,1)}, bf16[1024,1536]{1,0:T(8,128)(2,1)}, bf16[1024,1536]{1,0:T(8,128)(2,1)}, f32[256,2048]{1,0:T(8,128)}) custom-call(bf16[128,2048]{1,0:T(8,128)(2,1)} %copy-done.24, bf16[128,2048]{1,0:T(8,128)(2,1)} %copy-done.23, ...), custom_call_target="tpu_custom_call", output_to_operand_aliasing={{0}: (8, {}), {1}: (9, {}), {2}: (10, {})} | custom-call | flops 225443840 | bytes 1052672 | tf_op jit(solution)/shard_map/ffn_set/pallas_call | solution.py:889
  347.2 18.7 %ffn_set.10 = (bf16[1024,1536]{1,0:T(8,128)(2,1)}, bf16[1024,1536]{1,0:T(8,128)(2,1)}, bf16[1024,1536]{1,0:T(8,128)(2,1)}, f32[512,2048]{1,0:T(8,128)}) custom-call(bf16[256,2048]{1,0:T(8,128)(2,1)} %collective-permute-done.24.refs_0_, bf16[256,2048]{1,0:T(8,128)(2,1)} %copy-done.14, ...), custom_call_target="tpu_custom_call", output_to_operand_aliasing={{0}: (8, {}), {1}: (9, {}), {2}: (10, {})} | custom-call | flops 450887680 | bytes 1576960 | tf_op jit(solution)/shard_map/ffn_set/pallas_call | solution.py:889
  370.9 11.7 %ffn_set.11 = (bf16[1024,1536]{1,0:T(8,128)(2,1)}, bf16[1024,1536]{1,0:T(8,128)(2,1)}, bf16[1024,1536]{1,0:T(8,128)(2,1)}, f32[256,2048]{1,0:T(8,128)}) custom-call(bf16[256,2048]{1,0:T(8,128)(2,1)} %get-tuple-element.449.refs_0_, bf16[256,2048]{1,0:T(8,128)(2,1)} %dy.1, ...), custom_call_target="tpu_custom_call", output_to_operand_aliasing={{0}: (6, {}), {1}: (7, {}), {2}: (8, {})} | custom-call | flops 225443840 | bytes 1052672 | tf_op jit(solution)/shard_map/ffn_set/pallas_call | solution.py:889
  382.5 12.7 %tn_cols.3 = (bf16[1536,1024]{1,0:T(8,128)(2,1)}, bf16[1536,1024]{1,0:T(8,128)(2,1)}) custom-call(s32[2]{0:T(128)} %pad_add_fusion.2.idx, bf16[1024,1536]{1,0:T(8,128)(2,1)} %get-tuple-element.471.a.hid, bf16[1024,2048]{1,0:T(8,128)(2,1)} %get-tuple-element.455.b), custom_call_target="tpu_custom_call" | custom-call | flops 402653184 | bytes 851968 | tf_op jit(solution)/shard_map/tn_cols/pallas_call | solution.py:349
  397.8 12.8 %tn_cols.4 = (bf16[1536,1024]{1,0:T(8,128)(2,1)}, bf16[1536,1024]{1,0:T(8,128)(2,1)}) custom-call(s32[2]{0:T(128)} %pad_add_fusion.2.idx, bf16[1024,1536]{1,0:T(8,128)(2,1)} %get-tuple-element.458.a, bf16[1024,2048]{1,0:T(8,128)(2,1)} %get-tuple-element.459.b), custom_call_target="tpu_custom_call" | custom-call | flops 402653184 | bytes 851968 | tf_op jit(solution)/shard_map/tn_cols/pallas_call | solution.py:349
  410.6 10.5 %collective-permute-done.34.f = bf16[256,2048]{1,0:T(8,128)(2,1)} collective-permute-done((bf16[256,2048]{1,0:T(8,128)(2,1)}, bf16[256,2048]{1,0:T(8,128)(2,1)}, u32[]{:S(2)}, u32[]{:S(2)}) %collective-permute-start.34) | collective-permute-done | bytes 1048608 | tf_op jit(solution)/shard_map/ppermute | solution.py:106
  430.0 12.8 %out_back.1 = (f32[256,2048]{1,0:T(8,128)}, bf16[256,2048]{1,0:T(8,128)(2,1)}, f32[1,2048]{1,0:T(1,128)}, bf16[8,256,256]{2,1,0:T(8,128)(2,1)}) custom-call(s32[4]{0:T(128)} %pad_add_fusion.1.idx, f32[256,2048]{1,0:T(8,128)} %get-tuple-element.461.own, bf16[256,2048]{1,0:T(8,128)(2,1)} %collective-permute-done.34.f, ...), custom_call_target="tpu_custom_call" | custom-call | flops 134217728 | bytes 1179648 | tf_op jit(solution)/shard_map/out_back/pallas_call | solution.py:775
  448.5 13.2 %down_rows.1.near = bf16[1024,2048]{1,0:T(8,128)(2,1)} custom-call(bf16[1024,1536]{1,0:T(8,128)(2,1)} %get-tuple-element.471.a.hid, bf16[688,2048]{1,0:T(8,128)(2,1)} %own.1, bf16[4,688,512]{2,1,0:T(8,128)(2,1)} %bitcast.53), custom_call_target="tpu_custom_call" | custom-call | flops 360710144 | bytes 1138688 | tf_op jit(solution)/shard_map/down_rows/pallas_call | solution.py:939
  461.7 12.7 %tn_cols.5 = (bf16[1536,1024]{1,0:T(8,128)(2,1)}, bf16[1536,1024]{1,0:T(8,128)(2,1)}) custom-call(s32[2]{0:T(128)} %pad_add_fusion.2.idx, bf16[1024,1536]{1,0:T(8,128)(2,1)} %get-tuple-element.473.a, bf16[1024,2048]{1,0:T(8,128)(2,1)} %get-tuple-element.459.b), custom_call_target="tpu_custom_call" | custom-call | flops 402653184 | bytes 851968 | tf_op jit(solution)/shard_map/tn_cols/pallas_call | solution.py:349
  474.4 10.2 %collective-permute-done.37.b = bf16[1536,512]{1,0:T(8,128)(2,1)} collective-permute-done((bf16[1536,512]{1,0:T(8,128)(2,1)S(1)}, bf16[1536,512]{1,0:T(8,128)(2,1)}, u32[]{:S(2)}, u32[]{:S(2)}) %collective-permute-start.37) | collective-permute-done | bytes 1572896 | tf_op jit(solution)/shard_map/ppermute | solution.py:126
  501.4 17.7 %attend_back.2 = (bf16[2048,768]{1,0:T(8,128)(2,1)}, f32[2048,256]{1,0:T(8,128)}, f32[2048,256]{1,0:T(8,128)}) custom-call(bf16[2048,256]{1,0:T(8,128)(2,1)} %get-tuple-element.386.q_ref, bf16[2048,256]{1,0:T(8,128)(2,1)} %bitcast.70, bf16[1024,512]{1,0:T(8,128)(2,1)} %copy-done.6, bf16[2048,512]{1,0:T(8,128)(2,1)} %get-tuple-element.387.k0.k1.v0.v1, ...), custom_call_target="tpu_custom_call" | custom-call | flops 209715200 | bytes 458752 | tf_op jit(solution)/shard_map/attend_back/pallas_call | solution.py:1093
  553.3 17.8 %attend_back.3 = (bf16[2048,768]{1,0:T(8,128)(2,1)}, f32[2048,256]{1,0:T(8,128)}, f32[2048,256]{1,0:T(8,128)}) custom-call(bf16[2048,256]{1,0:T(8,128)(2,1)} %get-tuple-element.386.q_ref, bf16[2048,256]{1,0:T(8,128)(2,1)} %bitcast.71, bf16[2048,512]{1,0:T(8,128)(2,1)} %get-tuple-element.387.k0.k1.v0.v1, ...), custom_call_target="tpu_custom_call", output_to_operand_aliasing={{0}: (9, {})} | custom-call | flops 209715200 | bytes 458752 | tf_op jit(solution)/shard_map/attend_back/pallas_call | solution.py:1093
  571.1 11.0 %collective-permute-done.48.refs_0_ = bf16[688,512]{1,0:T(8,128)(2,1)S(1)} collective-permute-done((bf16[688,512]{1,0:T(8,128)(2,1)S(1)}, bf16[688,512]{1,0:T(8,128)(2,1)S(1)}, u32[]{:S(2)}, u32[]{:S(2)}) %collective-permute-start.48) | collective-permute-done | bytes 704544 | tf_op jit(solution)/shard_map/ppermute | solution.py:1174
  626.6 13.3 %tn_rows.1 = (bf16[1024,768]{1,0:T(8,128)(2,1)}, bf16[1024,768]{1,0:T(8,128)(2,1)}, f32[2048,1]{1,0:T(8,128)}) custom-call(s32[2]{0:T(128)} %pad_add_fusion.2.idx, bf16[2048,2048]{1,0:T(8,128)(2,1)} %get-tuple-element.533.a, bf16[2048,768]{1,0:T(8,128)(2,1)} %finish_keys.3.rows.b, bf16[2048,768]{1,0:T(8,128)(2,1)} %copy-done.2), custom_call_target="tpu_custom_call" | custom-call | flops 402653184 | bytes 917504 | tf_op jit(solution)/shard_map/tn_rows/pallas_call | solution.py:439
  648.1 19.0 %collective-permute-done.51.refs_0_ = bf16[688,512]{1,0:T(8,128)(2,1)S(1)} collective-permute-done((bf16[688,512]{1,0:T(8,128)(2,1)S(1)}, bf16[688,512]{1,0:T(8,128)(2,1)S(1)}, u32[]{:S(2)}, u32[]{:S(2)}) %collective-permute-start.51) | collective-permute-done | bytes 704544 | tf_op jit(solution)/shard_map/ppermute | solution.py:1174
  695.0 7.8 collective-permute-done.56.f
  729.4 12.9 %collective-permute-done.61.f = bf16[256,512]{1,0:T(8,128)(2,1)S(1)} collective-permute-done((bf16[256,512]{1,0:T(8,128)(2,1)}, bf16[256,512]{1,0:T(8,128)(2,1)S(1)}, u32[]{:S(2)}, u32[]{:S(2)}) %collective-permute-start.61) | collective-permute-done | bytes 262176 | tf_op jit(solution)/shard_map/ppermute | solution.py:106
  768.4 10.2 %collective-permute-done.65.f = bf16[256,512]{1,0:T(8,128)(2,1)S(1)} collective-permute-done((bf16[256,512]{1,0:T(8,128)(2,1)}, bf16[256,512]{1,0:T(8,128)(2,1)S(1)}, u32[]{:S(2)}, u32[]{:S(2)}) %collective-permute-start.65) | collective-permute-done | bytes 262176 | tf_op jit(solution)/shard_map/ppermute | solution.py:106
  (420 shorter events, 387.5 us)
Async XLA Ops:
  7.2 254.7 %all-gather.15.cloned.1.call-start = ((), (), s32[]{:S(2)}) async-start(), calls=%async_computation.4 | async-start | bytes 3522560 | tf_op jit(solution)/shard_map/all_gather | solution.py:177
  44.8 30.8 %collective-permute-start.4 = (bf16[256,2048]{1,0:T(8,128)(2,1)}, bf16[256,2048]{1,0:T(8,128)(2,1)S(1)}, u32[]{:S(2)}, u32[]{:S(2)}) collective-permute-start(bf16[256,2048]{1,0:T(8,128)(2,1)} %collective-permute-done.refs_0_), channel_id=1, source_target_pairs={{0,2},{2,4},{4,6},{6,7},{7,5},{5,3},{3,1},{1,0},{8,10},{10,12},{12... | collective-permute-start | bytes 3145736 | tf_op jit(solution)/shard_map/ppermute | solution.py:81
  116.4 64.1 %collective-permute-start.20 = (bf16[2048,512]{1,0:T(8,128)(2,1)}, bf16[2048,512]{1,0:T(8,128)(2,1)}, u32[]{:S(2)}, u32[]{:S(2)}) collective-permute-start(bf16[2048,512]{1,0:T(8,128)(2,1)} %bitcast.66), channel_id=1, source_target_pairs={{0,16},{8,24},{16,0},{24,8},{1,17},{9,25},{17,1},{25,9},{2,18},{10... | collective-permute-start | bytes 6291464 | tf_op jit(solution)/shard_map/ppermute | solution.py:126
  145.6 34.8 %collective-permute-start.21 = (bf16[688,512]{1,0:T(8,128)(2,1)}, bf16[688,512]{1,0:T(8,128)(2,1)}, u32[]{:S(2)}, u32[]{:S(2)}) collective-permute-start(bf16[688,512]{1,0:T(8,128)(2,1)} %get-tuple-element.382), channel_id=1, source_target_pairs={{0,4},{1,5},{2,6},{3,7},{4,0},{5,1},{6,2},{7,3},{8,12},{9,13},{10,... | collective-permute-start | bytes 2113544 | tf_op jit(solution)/shard_map/ppermute | solution.py:1174
  180.5 30.4 %collective-permute-start.23 = (bf16[2048,512]{1,0:T(8,128)(2,1)}, bf16[2048,512]{1,0:T(8,128)(2,1)}, u32[]{:S(2)}, u32[]{:S(2)}) collective-permute-start(bf16[2048,512]{1,0:T(8,128)(2,1)} %collective-permute-done.20.refs_1_), channel_id=1, source_target_pairs={{0,8},{8,0},{16,24},{24,16},{1,9},{9,1},{17,25},{25,17},{2,10},{10... | collective-permute-start | bytes 6291464 | tf_op jit(solution)/shard_map/ppermute | solution.py:126
  184.6 117.5 %all-gather.17.cloned.1.call-start = ((), (), s32[]{:S(2)}) async-start(), calls=%async_computation.5 | async-start | bytes 3522560 | tf_op jit(solution)/shard_map/all_gather | solution.py:177
  222.2 39.7 %collective-permute-start.25 = (bf16[256,2048]{1,0:T(8,128)(2,1)}, bf16[256,2048]{1,0:T(8,128)(2,1)S(1)}, u32[]{:S(2)}, u32[]{:S(2)}) collective-permute-start(bf16[256,2048]{1,0:T(8,128)(2,1)} %get-tuple-element.449.refs_0_), channel_id=1, source_target_pairs={{0,1},{2,0},{3,2},{1,3},{4,5},{6,4},{7,6},{5,7},{8,9},{10,8},{11,1... | collective-permute-start | bytes 3145736 | tf_op jit(solution)/shard_map/ppermute | solution.py:82
  223.6 38.2 %collective-permute-start.24 = (bf16[256,2048]{1,0:T(8,128)(2,1)}, bf16[256,2048]{1,0:T(8,128)(2,1)}, u32[]{:S(2)}, u32[]{:S(2)}) collective-permute-start(bf16[256,2048]{1,0:T(8,128)(2,1)} %get-tuple-element.449.refs_0_), channel_id=1, source_target_pairs={{0,2},{2,3},{3,1},{1,0},{4,6},{6,7},{7,5},{5,4},{8,10},{10,11},{11... | collective-permute-start | bytes 3145736 | tf_op jit(solution)/shard_map/ppermute | solution.py:81
  224.2 36.9 %collective-permute-start.30 = (bf16[688,512]{1,0:T(8,128)(2,1)S(1)}, bf16[688,512]{1,0:T(8,128)(2,1)}, u32[]{:S(2)}, u32[]{:S(2)}) collective-permute-start(bf16[688,512]{1,0:T(8,128)(2,1)S(1)} %copy-done.42), channel_id=1, source_target_pairs={{0,4},{1,5},{2,6},{3,7},{4,0},{5,1},{6,2},{7,3},{8,12},{9,13},{10,... | collective-permute-start | bytes 2113544 | tf_op jit(solution)/shard_map/ppermute | solution.py:1174
  261.9 69.3 %all-gather.19.cloned.1.call-start = ((), (), s32[]{:S(2)}) async-start(), calls=%async_computation.6 | async-start | bytes 3522560 | tf_op jit(solution)/shard_map/all_gather | solution.py:177
  261.9 32.5 %collective-permute-start.31 = (bf16[688,512]{1,0:T(8,128)(2,1)}, bf16[688,512]{1,0:T(8,128)(2,1)}, u32[]{:S(2)}, u32[]{:S(2)}) collective-permute-start(bf16[688,512]{1,0:T(8,128)(2,1)} %constant_dynamic-slice_fusion.3), channel_id=1, source_target_pairs={{0,4},{1,5},{2,6},{3,7},{4,0},{5,1},{6,2},{7,3},{8,12},{9,13},{10,... | collective-permute-start | bytes 2113544 | tf_op jit(solution)/shard_map/ppermute | solution.py:1174
  267.8 34.2 %collective-permute-start.27 = (bf16[128,2048]{1,0:T(8,128)(2,1)}, bf16[128,2048]{1,0:T(8,128)(2,1)S(1)}, u32[]{:S(2)}, u32[]{:S(2)}) collective-permute-start(bf16[128,2048]{1,0:T(8,128)(2,1)} %slice.118), channel_id=1, source_target_pairs={{0,1},{2,0},{3,2},{1,3},{4,5},{6,4},{7,6},{5,7},{8,9},{10,8},{11,1... | collective-permute-start | bytes 1572872 | tf_op jit(solution)/shard_map/ppermute | solution.py:87
  269.8 32.3 %collective-permute-start.26 = (bf16[128,2048]{1,0:T(8,128)(2,1)}, bf16[128,2048]{1,0:T(8,128)(2,1)S(1)}, u32[]{:S(2)}, u32[]{:S(2)}) collective-permute-start(bf16[128,2048]{1,0:T(8,128)(2,1)} %slice.117), channel_id=1, source_target_pairs={{0,2},{2,3},{3,1},{1,0},{4,6},{6,7},{7,5},{5,4},{8,10},{10,11},{11... | collective-permute-start | bytes 1572872 | tf_op jit(solution)/shard_map/ppermute | solution.py:86
  442.7 41.8 %collective-permute-start.38 = (bf16[1536,1024]{1,0:T(8,128)(2,1)}, bf16[1536,1024]{1,0:T(8,128)(2,1)}, u32[]{:S(2)}, u32[]{:S(2)}) collective-permute-start(bf16[1536,1024]{1,0:T(8,128)(2,1)} %get-tuple-element.470), channel_id=1, source_target_pairs={{0,8},{8,0},{16,24},{24,16},{1,9},{9,1},{17,25},{25,17},{2,10},{10... | collective-permute-start | bytes 9437192 | tf_op jit(solution)/shard_map/ppermute | solution.py:126
  442.8 41.8 %all-to-all-start.1 = ((bf16[8,256,256]{2,1,0:T(8,128)(2,1)}), bf16[8,256,256]{2,1,0:T(8,128)(2,1)S(1)}, u32[]{:S(2)}, u32[]{:S(2)}) async-start(bf16[8,256,256]{2,1,0:T(8,128)(2,1)} %get-tuple-element.464), calls=%async_computation.1 | async-start | bytes 2097152 | tf_op jit(solution)/shard_map/all_to_all | solution.py:1306
  447.4 219.7 %reduce-scatter.2.cloned.1.call-start = ((), (), s32[]{:S(2)}) async-start(), calls=%async_computation.3 | async-start | bytes 10485760 | tf_op jit(solution)/shard_map/reduce_scatter | solution.py:1345
  447.9 36.7 %collective-permute-start.37 = (bf16[1536,512]{1,0:T(8,128)(2,1)S(1)}, bf16[1536,512]{1,0:T(8,128)(2,1)}, u32[]{:S(2)}, u32[]{:S(2)}) collective-permute-start(bf16[1536,512]{1,0:T(8,128)(2,1)S(1)} %copy-done.70), channel_id=1, source_target_pairs={{0,16},{8,24},{16,0},{24,8},{1,17},{9,25},{17,1},{25,9},{2,18},{10... | collective-permute-start | bytes 4718600 | tf_op jit(solution)/shard_map/ppermute | solution.py:126
  484.6 44.9 %collective-permute-start.41 = (bf16[1536,1024]{1,0:T(8,128)(2,1)}, bf16[1536,1024]{1,0:T(8,128)(2,1)}, u32[]{:S(2)}, u32[]{:S(2)}) collective-permute-start(bf16[1536,1024]{1,0:T(8,128)(2,1)} %get-tuple-element.488), channel_id=1, source_target_pairs={{0,8},{8,0},{16,24},{24,16},{1,9},{9,1},{17,25},{25,17},{2,10},{10... | collective-permute-start | bytes 9437192 | tf_op jit(solution)/shard_map/ppermute | solution.py:126
  490.7 38.8 %collective-permute-start.42 = (bf16[1536,512]{1,0:T(8,128)(2,1)}, bf16[1536,512]{1,0:T(8,128)(2,1)S(1)}, u32[]{:S(2)}, u32[]{:S(2)}) collective-permute-start(bf16[1536,512]{1,0:T(8,128)(2,1)} %get-tuple-element.483), channel_id=1, source_target_pairs={{0,16},{8,24},{16,0},{24,8},{1,17},{9,25},{17,1},{25,9},{2,18},{10... | collective-permute-start | bytes 4718600 | tf_op jit(solution)/shard_map/ppermute | solution.py:126
  495.5 34.0 %collective-permute-start.43 = (bf16[688,512]{1,0:T(8,128)(2,1)S(1)}, bf16[688,512]{1,0:T(8,128)(2,1)S(1)}, u32[]{:S(2)}, u32[]{:S(2)}) collective-permute-start(bf16[688,512]{1,0:T(8,128)(2,1)S(1)} %slice.150), channel_id=1, source_target_pairs={{0,4},{1,5},{2,6},{3,7},{4,0},{5,1},{6,2},{7,3},{8,12},{9,13},{10,... | collective-permute-start | bytes 2113544 | tf_op jit(solution)/shard_map/ppermute | solution.py:1174
  538.9 45.4 %collective-permute-start.47 = (bf16[1536,512]{1,0:T(8,128)(2,1)}, bf16[1536,512]{1,0:T(8,128)(2,1)S(1)}, u32[]{:S(2)}, u32[]{:S(2)}) collective-permute-start(bf16[1536,512]{1,0:T(8,128)(2,1)} %get-tuple-element.502), channel_id=1, source_target_pairs={{0,16},{8,24},{16,0},{24,8},{1,17},{9,25},{17,1},{25,9},{2,18},{10... | collective-permute-start | bytes 4718600 | tf_op jit(solution)/shard_map/ppermute | solution.py:126
  543.8 38.4 %collective-permute-start.45 = (bf16[256,2048]{1,0:T(8,128)(2,1)}, bf16[256,2048]{1,0:T(8,128)(2,1)S(1)}, u32[]{:S(2)}, u32[]{:S(2)}) collective-permute-start(bf16[256,2048]{1,0:T(8,128)(2,1)} %get-tuple-element.497), channel_id=1, source_target_pairs={{0,2},{2,3},{3,1},{1,0},{4,6},{6,7},{7,5},{5,4},{8,10},{10,11},{11... | collective-permute-start | bytes 3145736 | tf_op jit(solution)/shard_map/ppermute | solution.py:106
  544.5 39.9 %collective-permute-start.46 = (bf16[256,2048]{1,0:T(8,128)(2,1)}, bf16[256,2048]{1,0:T(8,128)(2,1)S(1)}, u32[]{:S(2)}, u32[]{:S(2)}) collective-permute-start(bf16[256,2048]{1,0:T(8,128)(2,1)} %get-tuple-element.498), channel_id=1, source_target_pairs={{0,1},{2,0},{3,2},{1,3},{4,5},{6,4},{7,6},{5,7},{8,9},{10,8},{11,1... | collective-permute-start | bytes 3145736 | tf_op jit(solution)/shard_map/ppermute | solution.py:107
  545.8 38.5 %collective-permute-start.44 = (bf16[1024,512]{1,0:T(8,128)(2,1)S(1)}, bf16[1024,512]{1,0:T(8,128)(2,1)S(1)}, u32[]{:S(2)}, u32[]{:S(2)}) collective-permute-start(bf16[1024,512]{1,0:T(8,128)(2,1)S(1)} %pad_maximum_fusion.2), channel_id=1, source_target_pairs={{8,0},{16,8},{24,16},{9,1},{17,9},{25,17},{10,2},{18,10},{26,18},{... | collective-permute-start | bytes 3145736 | tf_op jit(solution)/shard_map/ppermute | solution.py:193
  551.2 31.0 %collective-permute-start.48 = (bf16[688,512]{1,0:T(8,128)(2,1)S(1)}, bf16[688,512]{1,0:T(8,128)(2,1)S(1)}, u32[]{:S(2)}, u32[]{:S(2)}) collective-permute-start(bf16[688,512]{1,0:T(8,128)(2,1)S(1)} %slice.153), channel_id=1, source_target_pairs={{0,4},{1,5},{2,6},{3,7},{4,0},{5,1},{6,2},{7,3},{8,12},{9,13},{10,... | collective-permute-start | bytes 2113544 | tf_op jit(solution)/shard_map/ppermute | solution.py:1174
  592.3 132.4 %all-gather.21.cloned.1.call-start = ((), (), s32[]{:S(2)}) async-start(), calls=%async_computation.7 | async-start | bytes 3522560 | tf_op jit(solution)/shard_map/all_gather | solution.py:177
  597.9 160.8 %all-gather.23.cloned.1.call-start = ((), (), s32[]{:S(2)}) async-start(), calls=%async_computation.8 | async-start | bytes 3522560 | tf_op jit(solution)/shard_map/all_gather | solution.py:177
  600.7 210.3 %all-gather.27.cloned.1.call-start = ((), (), s32[]{:S(2)}) async-start(), calls=%async_computation.10 | async-start | bytes 3522560 | tf_op jit(solution)/shard_map/all_gather | solution.py:177
  622.6 44.6 %collective-permute-start.51 = (bf16[688,512]{1,0:T(8,128)(2,1)S(1)}, bf16[688,512]{1,0:T(8,128)(2,1)S(1)}, u32[]{:S(2)}, u32[]{:S(2)}) collective-permute-start(bf16[688,512]{1,0:T(8,128)(2,1)S(1)} %slice.154), channel_id=1, source_target_pairs={{0,4},{1,5},{2,6},{3,7},{4,0},{5,1},{6,2},{7,3},{8,12},{9,13},{10,... | collective-permute-start | bytes 2113544 | tf_op jit(solution)/shard_map/ppermute | solution.py:1174
  674.1 147.3 %all-gather.25.cloned.1.call-start = ((), (), s32[]{:S(2)}) async-start(), calls=%async_computation.9 | async-start | bytes 1310720 | tf_op jit(solution)/shard_map/all_gather | solution.py:177
  712.1 31.3 %collective-permute-start.58 = (bf16[256,2048]{1,0:T(8,128)(2,1)}, bf16[256,2048]{1,0:T(8,128)(2,1)S(1)}, u32[]{:S(2)}, u32[]{:S(2)}) collective-permute-start(bf16[256,2048]{1,0:T(8,128)(2,1)} %get-tuple-element.566), channel_id=1, source_target_pairs={{0,2},{2,4},{4,6},{6,7},{7,5},{5,3},{3,1},{1,0},{8,10},{10,12},{12... | collective-permute-start | bytes 3145736 | tf_op jit(solution)/shard_map/ppermute | solution.py:106
  749.7 30.8 %collective-permute-start.63 = (bf16[256,2048]{1,0:T(8,128)(2,1)}, bf16[256,2048]{1,0:T(8,128)(2,1)S(1)}, u32[]{:S(2)}, u32[]{:S(2)}) collective-permute-start(bf16[256,2048]{1,0:T(8,128)(2,1)} %get-tuple-element.584), channel_id=1, source_target_pairs={{0,2},{2,4},{4,6},{6,7},{7,5},{5,3},{3,1},{1,0},{8,10},{10,12},{12... | collective-permute-start | bytes 3145736 | tf_op jit(solution)/shard_map/ppermute | solution.py:106
  (126 other events, 1878.0 us)
Sparse Core Ops, SparseCore 0:
  180.6 25.9 all-gather.14
  262.0 27.7 all-gather.16
  302.2 28.9 all-gather.18
  592.4 74.3 reduce-scatter.1
  668.2 26.6 all-gather.20
  696.4 32.0 all-gather.22
  730.2 28.1 all-gather.26
  794.0 13.2 all-gather.24

commit v4 on v3

--- a/solution.py
+++ b/solution.py
@@ -1312,8 +1312,9 @@
     red_gate.send(red_down.sent)
     sf_all = down_rows(after(hid_all, red_down.sent), own_w[2], [g[2] for g in got])
     red_up = Halves(*tn_cols(after(up_all, red_down.sent), h_all), 1)
-    grad_heads, red_down.got, red_gate.got, sf_all, red_up.sent = together(
-        grad_heads, red_down.got, red_gate.got, sf_all, red_up.sent
+    out_local = tn_whole(my_heads, after(grad_mid_low, red_down.sent))
+    grad_heads, red_down.got, red_gate.got, sf_all, red_up.sent, out_local = together(
+        grad_heads, red_down.got, red_gate.got, sf_all, red_up.sent, out_local
     )
     red_down.finish()
     down_back = send_back(red_down)
@@ -1341,9 +1342,7 @@
     d_joint, ak, av, got_back, sf.f, sf.b, red_up.got, *gate_back = together(
         d_joint, ak, av, got_back, sf.f, sf.b, red_up.got, *gate_back
     )
-    out_local = tn_whole(my_heads, after(grad_mid_low, ak))
-    out_dp = lax.psum_scatter(out_local, "dp", scatter_dimension=1, tiled=True)
-    ak = after(ak, out_local)
+    out_dp = lax.psum_scatter(after(out_local, ak), "dp", scatter_dimension=1, tiled=True)
     d_joint = finish_keys(0, ak, av, (bk, 1, 0), (bv, 1, 0), cos, sin, d_joint)
     d_joint = finish_keys(1, ak, av, (got_back, 0, 0), (got_back, 0, 1), cos, sin, d_joint)
 
@@ -1351,7 +1350,7 @@
         rels = [r % n_tensor for r in rels]
         return grad_x_terms(after(ring_owners, *deps), rels, d_joint, w_joint, rows, kind)
 
-    red_up.finish(out_local)
+    red_up.finish(ak)
     up_back = send_back(red_up)
     sx = Scatter(after(terms([far], BF16), red_up.value), ring)
     near = terms([far - 1, 1 - far], F32, red_up.value)

time: 848 us -> 841 us (level)
  waiting for transfers between devices: 250 us -> 234 us
  transfers between devices with their start and end apart: 86 -> 86, of which waited for: 37 -> 35; matrix products, arithmetic and copies ran while one was open for 5% -> 5% of each run, Pallas kernels for 41% -> 42%
where the time goes in v4:
time: 841 us; the launch traced here: 824 us
  Pallas kernels  413 us (49%)
  waiting for transfers between devices  234 us (28%)
  starting transfers between devices  95 us (11%)
  local copies, waits for them, and re-layouts  40.5 us (5%)
  other arithmetic  25.9 us (3%)
  between operations  16 us (2%)
    pallas_call x6, Pallas kernels, ffn_set(): pl.pallas_call(functools.partial(ffn_body, n_in, n_w, first, units, len(h...  81.9 us
    ppermute x6, waiting for transfers between devices, to_group(): return lax.ppermute(piece, 'tensor', pairs)  67.4 us
    ppermute x12, waiting for transfers between devices, send(): self.f = lax.ppermute(self.sent[0], 'tensor', self.ahead)  50.8 us
    pallas_call x8, Pallas kernels, qkv_chunk(): pl.pallas_call(functools.partial(qkv_body, n_in), grid_spec=pltpu.Prefetc...  40.3 us
    ppermute x8, waiting for transfers between devices, step(): self.f = lax.ppermute(f, 'tensor', self.ahead)  39.1 us
    pallas_call x3, Pallas kernels, tn_cols(): pl.pallas_call(functools.partial(tn_cols_body, n), grid_spec=pltpu.Prefet...  38.2 us
    pallas_call x2, Pallas kernels, attend_back(): pl.pallas_call(attend_back_body, grid=(heads, blocks), in_specs=in_specs,...  35.5 us
    pallas_call x5, Pallas kernels, grad_x_terms(): pl.pallas_call(grad_x_body, grid_spec=pltpu.PrefetchScalarGridSpec(num_sc...  28.3 us
  transfers between devices with their start and end apart: 86, of which 35 were waited for; matrix products, arithmetic and copies ran while one was open for 5% of the time, Pallas kernels for 42%

profile of v4, /device:TPU:0, one launch (start us, length us, event | category | flops | bytes accessed | tf_op | source)
XLA Modules:
  0.0 824.3 jit_solution(6469067145068313561)
XLA Ops:
  31.5 11.8 %collective-permute-done.refs_0_ = bf16[256,2048]{1,0:T(8,128)(2,1)} collective-permute-done((bf16[256,2048]{1,0:T(8,128)(2,1)}, bf16[256,2048]{1,0:T(8,128)(2,1)}, u32[]{:S(2)}, u32[]{:S(2)}) %collective-permute-start) | collective-permute-done | bytes 1048608 | tf_op jit(solution)/shard_map/ppermute | solution.py:81
  58.9 15.4 %collective-permute-done.6.refs_3_ = bf16[256,512]{1,0:T(8,128)(2,1)S(1)} collective-permute-done((bf16[256,512]{1,0:T(8,128)(2,1)}, bf16[256,512]{1,0:T(8,128)(2,1)S(1)}, u32[]{:S(2)}, u32[]{:S(2)}) %collective-permute-start.6) | collective-permute-done | bytes 262176 | tf_op jit(solution)/shard_map/ppermute | solution.py:81
  93.6 10.2 %collective-permute-done.10.refs_5_ = bf16[256,512]{1,0:T(8,128)(2,1)S(1)} collective-permute-done((bf16[256,512]{1,0:T(8,128)(2,1)S(1)}, bf16[256,512]{1,0:T(8,128)(2,1)S(1)}, u32[]{:S(2)}, u32[]{:S(2)}) %collective-permute-start.10) | collective-permute-done | bytes 262176 | tf_op jit(solution)/shard_map/ppermute | solution.py:81
  146.6 10.3 %attend.2.rest_0_ = bf16[2048,256]{1,0:T(8,128)(2,1)} custom-call(bf16[2048,256]{1,0:T(8,128)(2,1)} %get-tuple-element.387.q_ref, bf16[2048,512]{1,0:T(8,128)(2,1)} %get-tuple-element.388.k0.k1.v0.v1, bf16[2048,512]{1,0:T(8,128)(2,1)} %get-tuple-element.388.k0.k1.v0.v1, bf16[2048,512]{1,0:T(8,128)(2,1)} %get-tuple-element.388.k0.k1.v0.v1, ...), custom_call_target="tpu_custom_call" | custom-call | flops 83886080 | bytes 196608 | tf_op jit(solution)/shard_map/attend/pallas_call | solution.py:1012
  162.4 10.3 %attend.3 = bf16[2048,256]{1,0:T(8,128)(2,1)} custom-call(bf16[2048,256]{1,0:T(8,128)(2,1)} %get-tuple-element.387.q_ref, bf16[1024,512]{1,0:T(8,128)(2,1)} %copy-done.6, bf16[2048,512]{1,0:T(8,128)(2,1)} %get-tuple-element.388.k0.k1.v0.v1, bf16[1024,512]{1,0:T(8,128)(2,1)} %copy-done.6, ...), custom_call_target="tpu_custom_call", output_to_operand_aliasing={{}: (6, {})} | custom-call | flops 83886080 | bytes 196608 | tf_op jit(solution)/shard_map/attend/pallas_call | solution.py:1012
  172.7 7.8 collective-permute-done.21
  185.3 25.6 %all-to-all-done.heads = bf16[8,256,256]{2,1,0:T(8,128)(2,1)S(1)} async-done(((bf16[8,256,256]{2,1,0:T(8,128)(2,1)}), bf16[8,256,256]{2,1,0:T(8,128)(2,1)S(1)}, u32[]{:S(2)}, u32[]{:S(2)}) %all-to-all-start) | async-done | bytes 1048608 | tf_op jit(solution)/shard_map/all_to_all | solution.py:1244
  211.9 10.3 %out_project.1 = (f32[256,2048]{1,0:T(8,128)}, f32[256,2048]{1,0:T(8,128)}, bf16[256,2048]{1,0:T(8,128)(2,1)}, bf16[256,2048]{1,0:T(8,128)(2,1)}) custom-call(s32[4]{0:T(128)} %pad_add_fusion.1.idx, bf16[8,256,256]{2,1,0:T(8,128)(2,1)} %copy-done.16, bf16[256,2048]{1,0:T(8,128)(2,1)} %x_ref.3, f32[1,2048]{1,0:T(1,128)} %bitcast.81, ...), custom_call_target="tpu_custom_call" | custom-call | flops 134217728 | bytes 1048576 | tf_op jit(solution)/shard_map/out_project/pallas_call | solution.py:710
  225.0 11.1 %ffn_set.6 = (bf16[1024,2048]{1,0:T(8,128)(2,1)}, bf16[1024,2048]{1,0:T(8,128)(2,1)}, bf16[1024,1536]{1,0:T(8,128)(2,1)}, bf16[1024,1536]{1,0:T(8,128)(2,1)}, bf...) custom-call(bf16[256,2048]{1,0:T(8,128)(2,1)} %get-tuple-element.450.refs_0_, bf16[256,2048]{1,0:T(8,128)(2,1)} %dy.1, ...), custom_call_target="tpu_custom_call" | custom-call | flops 225443840 | bytes 1052672 | tf_op jit(solution)/shard_map/ffn_set/pallas_call | solution.py:889
  236.1 25.1 %collective-permute-done.30 = bf16[688,512]{1,0:T(8,128)(2,1)} collective-permute-done((bf16[688,512]{1,0:T(8,128)(2,1)S(1)}, bf16[688,512]{1,0:T(8,128)(2,1)}, u32[]{:S(2)}, u32[]{:S(2)}) %collective-permute-start.30) | collective-permute-done | bytes 704544 | tf_op jit(solution)/shard_map/ppermute | solution.py:1174
  269.8 10.5 %collective-permute-start.26 = (bf16[128,2048]{1,0:T(8,128)(2,1)}, bf16[128,2048]{1,0:T(8,128)(2,1)S(1)}, u32[]{:S(2)}, u32[]{:S(2)}) collective-permute-start(bf16[128,2048]{1,0:T(8,128)(2,1)} %slice.117), channel_id=1, source_target_pairs={{0,2},{2,3},{3,1},{1,0},{4,6},{6,7},{7,5},{5,4},{8,10},{10,11},{11... | collective-permute-start | bytes 1572872 | tf_op jit(solution)/shard_map/ppermute | solution.py:86
  280.4 17.8 %ffn_set.7 = (bf16[1024,2048]{1,0:T(8,128)(2,1)}, bf16[1024,2048]{1,0:T(8,128)(2,1)}, bf16[1024,1536]{1,0:T(8,128)(2,1)}, bf16[1024,1536]{1,0:T(8,128)(2,1)}, bf...) custom-call(bf16[256,2048]{1,0:T(8,128)(2,1)} %collective-permute-do, ...), custom_call_target="tpu_custom_call", output_to_operand_aliasing={{0}: (7, {}), {1}: (8, {}), {2}: (9, {}), {3}: (10, {}), {4... | custom-call | flops 450887680 | bytes 1576960 | tf_op jit(solution)/shard_map/ffn_set/pallas_call | solution.py:889
  303.1 11.3 %ffn_set.8 = (bf16[1024,2048]{1,0:T(8,128)(2,1)}, bf16[1024,2048]{1,0:T(8,128)(2,1)}, bf16[1024,1536]{1,0:T(8,128)(2,1)}, bf16[1024,1536]{1,0:T(8,128)(2,1)}, bf...) custom-call(bf16[128,2048]{1,0:T(8,128)(2,1)} %copy-done.24, ...), custom_call_target="tpu_custom_call", output_to_operand_aliasing={{0}: (7, {}), {1}: (8, {}), {2}: (9, {}), {3}: (10, {}), {4... | custom-call | flops 225443840 | bytes 1052672 | tf_op jit(solution)/shard_map/ffn_set/pallas_call | solution.py:889
  314.4 16.9 %all-gather.19.cloned.1.call-done = bf16[2752,512]{1,0:T(8,128)(2,1)} async-done(((bf16[688,512]{1,0:T(8,128)(2,1)}), bf16[2752,512]{1,0:T(8,128)(2,1)}) %all-gather.19.cloned.1.call-update) | async-done | bytes 2818064 | tf_op jit(solution)/shard_map/all_gather | solution.py:177
  331.3 11.4 %ffn_set.9 = (bf16[1024,1536]{1,0:T(8,128)(2,1)}, bf16[1024,1536]{1,0:T(8,128)(2,1)}, bf16[1024,1536]{1,0:T(8,128)(2,1)}, f32[256,2048]{1,0:T(8,128)}) custom-call(bf16[128,2048]{1,0:T(8,128)(2,1)} %copy-done.24, bf16[128,2048]{1,0:T(8,128)(2,1)} %copy-done.23, ...), custom_call_target="tpu_custom_call", output_to_operand_aliasing={{0}: (8, {}), {1}: (9, {}), {2}: (10, {})} | custom-call | flops 225443840 | bytes 1052672 | tf_op jit(solution)/shard_map/ffn_set/pallas_call | solution.py:889
  347.3 18.7 %ffn_set.10 = (bf16[1024,1536]{1,0:T(8,128)(2,1)}, bf16[1024,1536]{1,0:T(8,128)(2,1)}, bf16[1024,1536]{1,0:T(8,128)(2,1)}, f32[512,2048]{1,0:T(8,128)}) custom-call(bf16[256,2048]{1,0:T(8,128)(2,1)} %collective-permute-done.24.refs_0_, bf16[256,2048]{1,0:T(8,128)(2,1)} %copy-done.14, ...), custom_call_target="tpu_custom_call", output_to_operand_aliasing={{0}: (8, {}), {1}: (9, {}), {2}: (10, {})} | custom-call | flops 450887680 | bytes 1576960 | tf_op jit(solution)/shard_map/ffn_set/pallas_call | solution.py:889
  371.1 11.6 %ffn_set.11 = (bf16[1024,1536]{1,0:T(8,128)(2,1)}, bf16[1024,1536]{1,0:T(8,128)(2,1)}, bf16[1024,1536]{1,0:T(8,128)(2,1)}, f32[256,2048]{1,0:T(8,128)}) custom-call(bf16[256,2048]{1,0:T(8,128)(2,1)} %get-tuple-element.450.refs_0_, bf16[256,2048]{1,0:T(8,128)(2,1)} %dy.1, ...), custom_call_target="tpu_custom_call", output_to_operand_aliasing={{0}: (6, {}), {1}: (7, {}), {2}: (8, {})} | custom-call | flops 225443840 | bytes 1052672 | tf_op jit(solution)/shard_map/ffn_set/pallas_call | solution.py:889
  382.6 12.8 %tn_cols.3 = (bf16[1536,1024]{1,0:T(8,128)(2,1)}, bf16[1536,1024]{1,0:T(8,128)(2,1)}) custom-call(s32[2]{0:T(128)} %pad_add_fusion.2.idx, bf16[1024,1536]{1,0:T(8,128)(2,1)} %get-tuple-element.472.a.hid, bf16[1024,2048]{1,0:T(8,128)(2,1)} %get-tuple-element.456.b), custom_call_target="tpu_custom_call" | custom-call | flops 402653184 | bytes 851968 | tf_op jit(solution)/shard_map/tn_cols/pallas_call | solution.py:349
  398.1 12.7 %tn_cols.4 = (bf16[1536,1024]{1,0:T(8,128)(2,1)}, bf16[1536,1024]{1,0:T(8,128)(2,1)}) custom-call(s32[2]{0:T(128)} %pad_add_fusion.2.idx, bf16[1024,1536]{1,0:T(8,128)(2,1)} %get-tuple-element.459.a, bf16[1024,2048]{1,0:T(8,128)(2,1)} %get-tuple-element.460.b), custom_call_target="tpu_custom_call" | custom-call | flops 402653184 | bytes 851968 | tf_op jit(solution)/shard_map/tn_cols/pallas_call | solution.py:349
  410.8 10.5 %collective-permute-done.34.f = bf16[256,2048]{1,0:T(8,128)(2,1)} collective-permute-done((bf16[256,2048]{1,0:T(8,128)(2,1)}, bf16[256,2048]{1,0:T(8,128)(2,1)}, u32[]{:S(2)}, u32[]{:S(2)}) %collective-permute-start.34) | collective-permute-done | bytes 1048608 | tf_op jit(solution)/shard_map/ppermute | solution.py:106
  430.2 12.6 %out_back.1 = (f32[256,2048]{1,0:T(8,128)}, bf16[256,2048]{1,0:T(8,128)(2,1)}, f32[1,2048]{1,0:T(1,128)}, bf16[8,256,256]{2,1,0:T(8,128)(2,1)}) custom-call(s32[4]{0:T(128)} %pad_add_fusion.1.idx, f32[256,2048]{1,0:T(8,128)} %get-tuple-element.462.own, bf16[256,2048]{1,0:T(8,128)(2,1)} %collective-permute-done.34.f, ...), custom_call_target="tpu_custom_call" | custom-call | flops 134217728 | bytes 1179648 | tf_op jit(solution)/shard_map/out_back/pallas_call | solution.py:775
  448.3 6.6 tn_whole.1
  455.0 13.2 %down_rows.1.near = bf16[1024,2048]{1,0:T(8,128)(2,1)} custom-call(bf16[1024,1536]{1,0:T(8,128)(2,1)} %get-tuple-element.472.a.hid, bf16[688,2048]{1,0:T(8,128)(2,1)} %own.1, bf16[4,688,512]{2,1,0:T(8,128)(2,1)} %bitcast.53), custom_call_target="tpu_custom_call" | custom-call | flops 360710144 | bytes 1138688 | tf_op jit(solution)/shard_map/down_rows/pallas_call | solution.py:939
  468.2 12.8 %tn_cols.5 = (bf16[1536,1024]{1,0:T(8,128)(2,1)}, bf16[1536,1024]{1,0:T(8,128)(2,1)}) custom-call(s32[2]{0:T(128)} %pad_add_fusion.2.idx, bf16[1024,1536]{1,0:T(8,128)(2,1)} %get-tuple-element.474.a, bf16[1024,2048]{1,0:T(8,128)(2,1)} %get-tuple-element.460.b), custom_call_target="tpu_custom_call" | custom-call | flops 402653184 | bytes 851968 | tf_op jit(solution)/shard_map/tn_cols/pallas_call | solution.py:349
  501.8 17.8 %attend_back.2 = (bf16[2048,768]{1,0:T(8,128)(2,1)}, f32[2048,256]{1,0:T(8,128)}, f32[2048,256]{1,0:T(8,128)}) custom-call(bf16[2048,256]{1,0:T(8,128)(2,1)} %get-tuple-element.387.q_ref, bf16[2048,256]{1,0:T(8,128)(2,1)} %bitcast.70, bf16[1024,512]{1,0:T(8,128)(2,1)} %copy-done.6, bf16[2048,512]{1,0:T(8,128)(2,1)} %get-tuple-element.388.k0.k1.v0.v1, ...), custom_call_target="tpu_custom_call" | custom-call | flops 209715200 | bytes 458752 | tf_op jit(solution)/shard_map/attend_back/pallas_call | solution.py:1093
  553.3 17.8 %attend_back.3 = (bf16[2048,768]{1,0:T(8,128)(2,1)}, f32[2048,256]{1,0:T(8,128)}, f32[2048,256]{1,0:T(8,128)}) custom-call(bf16[2048,256]{1,0:T(8,128)(2,1)} %get-tuple-element.387.q_ref, bf16[2048,256]{1,0:T(8,128)(2,1)} %bitcast.71, bf16[2048,512]{1,0:T(8,128)(2,1)} %get-tuple-element.388.k0.k1.v0.v1, ...), custom_call_target="tpu_custom_call", output_to_operand_aliasing={{0}: (9, {})} | custom-call | flops 209715200 | bytes 458752 | tf_op jit(solution)/shard_map/attend_back/pallas_call | solution.py:1093
  571.1 11.1 %collective-permute-done.48.refs_0_ = bf16[688,512]{1,0:T(8,128)(2,1)S(1)} collective-permute-done((bf16[688,512]{1,0:T(8,128)(2,1)S(1)}, bf16[688,512]{1,0:T(8,128)(2,1)S(1)}, u32[]{:S(2)}, u32[]{:S(2)}) %collective-permute-start.48) | collective-permute-done | bytes 704544 | tf_op jit(solution)/shard_map/ppermute | solution.py:1174
  619.9 13.2 %tn_rows.1 = (bf16[1024,768]{1,0:T(8,128)(2,1)}, bf16[1024,768]{1,0:T(8,128)(2,1)}, f32[2048,1]{1,0:T(8,128)}) custom-call(s32[2]{0:T(128)} %pad_add_fusion.2.idx, bf16[2048,2048]{1,0:T(8,128)(2,1)} %get-tuple-element.533.a, bf16[2048,768]{1,0:T(8,128)(2,1)} %finish_keys.3.rows.b, bf16[2048,768]{1,0:T(8,128)(2,1)} %copy-done.2), custom_call_target="tpu_custom_call" | custom-call | flops 402653184 | bytes 917504 | tf_op jit(solution)/shard_map/tn_rows/pallas_call | solution.py:439
  641.4 19.0 %collective-permute-done.51.refs_0_ = bf16[688,512]{1,0:T(8,128)(2,1)S(1)} collective-permute-done((bf16[688,512]{1,0:T(8,128)(2,1)S(1)}, bf16[688,512]{1,0:T(8,128)(2,1)S(1)}, u32[]{:S(2)}, u32[]{:S(2)}) %collective-permute-start.51) | collective-permute-done | bytes 704544 | tf_op jit(solution)/shard_map/ppermute | solution.py:1174
  687.9 8.0 collective-permute-done.56.f
  722.9 12.3 %collective-permute-done.61.f = bf16[256,512]{1,0:T(8,128)(2,1)S(1)} collective-permute-done((bf16[256,512]{1,0:T(8,128)(2,1)}, bf16[256,512]{1,0:T(8,128)(2,1)S(1)}, u32[]{:S(2)}, u32[]{:S(2)}) %collective-permute-start.61) | collective-permute-done | bytes 262176 | tf_op jit(solution)/shard_map/ppermute | solution.py:106
  761.3 10.2 %collective-permute-done.65.f = bf16[256,512]{1,0:T(8,128)(2,1)S(1)} collective-permute-done((bf16[256,512]{1,0:T(8,128)(2,1)}, bf16[256,512]{1,0:T(8,128)(2,1)S(1)}, u32[]{:S(2)}, u32[]{:S(2)}) %collective-permute-start.65) | collective-permute-done | bytes 262176 | tf_op jit(solution)/shard_map/ppermute | solution.py:106
  (420 shorter events, 381.7 us)
Async XLA Ops:
  7.2 254.7 %all-gather.15.cloned.1.call-start = ((), (), s32[]{:S(2)}) async-start(), calls=%async_computation.4 | async-start | bytes 3522560 | tf_op jit(solution)/shard_map/all_gather | solution.py:177
  44.8 30.8 %collective-permute-start.4 = (bf16[256,2048]{1,0:T(8,128)(2,1)}, bf16[256,2048]{1,0:T(8,128)(2,1)S(1)}, u32[]{:S(2)}, u32[]{:S(2)}) collective-permute-start(bf16[256,2048]{1,0:T(8,128)(2,1)} %collective-permute-done.refs_0_), channel_id=1, source_target_pairs={{0,2},{2,4},{4,6},{6,7},{7,5},{5,3},{3,1},{1,0},{8,10},{10,12},{12... | collective-permute-start | bytes 3145736 | tf_op jit(solution)/shard_map/ppermute | solution.py:81
  116.4 64.1 %collective-permute-start.20 = (bf16[2048,512]{1,0:T(8,128)(2,1)}, bf16[2048,512]{1,0:T(8,128)(2,1)}, u32[]{:S(2)}, u32[]{:S(2)}) collective-permute-start(bf16[2048,512]{1,0:T(8,128)(2,1)} %bitcast.66), channel_id=1, source_target_pairs={{0,16},{8,24},{16,0},{24,8},{1,17},{9,25},{17,1},{25,9},{2,18},{10... | collective-permute-start | bytes 6291464 | tf_op jit(solution)/shard_map/ppermute | solution.py:126
  145.7 34.8 %collective-permute-start.21 = (bf16[688,512]{1,0:T(8,128)(2,1)}, bf16[688,512]{1,0:T(8,128)(2,1)}, u32[]{:S(2)}, u32[]{:S(2)}) collective-permute-start(bf16[688,512]{1,0:T(8,128)(2,1)} %get-tuple-element.383), channel_id=1, source_target_pairs={{0,4},{1,5},{2,6},{3,7},{4,0},{5,1},{6,2},{7,3},{8,12},{9,13},{10,... | collective-permute-start | bytes 2113544 | tf_op jit(solution)/shard_map/ppermute | solution.py:1174
  184.6 117.5 %all-gather.17.cloned.1.call-start = ((), (), s32[]{:S(2)}) async-start(), calls=%async_computation.5 | async-start | bytes 3522560 | tf_op jit(solution)/shard_map/all_gather | solution.py:177
  222.2 39.7 %collective-permute-start.25 = (bf16[256,2048]{1,0:T(8,128)(2,1)}, bf16[256,2048]{1,0:T(8,128)(2,1)S(1)}, u32[]{:S(2)}, u32[]{:S(2)}) collective-permute-start(bf16[256,2048]{1,0:T(8,128)(2,1)} %get-tuple-element.450.refs_0_), channel_id=1, source_target_pairs={{0,1},{2,0},{3,2},{1,3},{4,5},{6,4},{7,6},{5,7},{8,9},{10,8},{11,1... | collective-permute-start | bytes 3145736 | tf_op jit(solution)/shard_map/ppermute | solution.py:82
  223.7 38.2 %collective-permute-start.24 = (bf16[256,2048]{1,0:T(8,128)(2,1)}, bf16[256,2048]{1,0:T(8,128)(2,1)}, u32[]{:S(2)}, u32[]{:S(2)}) collective-permute-start(bf16[256,2048]{1,0:T(8,128)(2,1)} %get-tuple-element.450.refs_0_), channel_id=1, source_target_pairs={{0,2},{2,3},{3,1},{1,0},{4,6},{6,7},{7,5},{5,4},{8,10},{10,11},{11... | collective-permute-start | bytes 3145736 | tf_op jit(solution)/shard_map/ppermute | solution.py:81
  224.3 36.9 %collective-permute-start.30 = (bf16[688,512]{1,0:T(8,128)(2,1)S(1)}, bf16[688,512]{1,0:T(8,128)(2,1)}, u32[]{:S(2)}, u32[]{:S(2)}) collective-permute-start(bf16[688,512]{1,0:T(8,128)(2,1)S(1)} %copy-done.43), channel_id=1, source_target_pairs={{0,4},{1,5},{2,6},{3,7},{4,0},{5,1},{6,2},{7,3},{8,12},{9,13},{10,... | collective-permute-start | bytes 2113544 | tf_op jit(solution)/shard_map/ppermute | solution.py:1174
  262.0 69.4 %all-gather.19.cloned.1.call-start = ((), (), s32[]{:S(2)}) async-start(), calls=%async_computation.6 | async-start | bytes 3522560 | tf_op jit(solution)/shard_map/all_gather | solution.py:177
  262.0 36.2 %collective-permute-start.31 = (bf16[688,512]{1,0:T(8,128)(2,1)}, bf16[688,512]{1,0:T(8,128)(2,1)}, u32[]{:S(2)}, u32[]{:S(2)}) collective-permute-start(bf16[688,512]{1,0:T(8,128)(2,1)} %constant_dynamic-slice_fusion.3), channel_id=1, source_target_pairs={{0,4},{1,5},{2,6},{3,7},{4,0},{5,1},{6,2},{7,3},{8,12},{9,13},{10,... | collective-permute-start | bytes 2113544 | tf_op jit(solution)/shard_map/ppermute | solution.py:1174
  264.9 33.3 %collective-permute-start.28 = (bf16[128,2048]{1,0:T(8,128)(2,1)S(1)}, bf16[128,2048]{1,0:T(8,128)(2,1)S(1)}, u32[]{:S(2)}, u32[]{:S(2)}) collective-permute-start(bf16[128,2048]{1,0:T(8,128)(2,1)S(1)} %slice.119), channel_id=1, source_target_pairs={{0,2},{2,3},{3,1},{1,0},{4,6},{6,7},{7,5},{5,4},{8,10},{10,11},{11... | collective-permute-start | bytes 1572872 | tf_op jit(solution)/shard_map/ppermute | solution.py:86
  265.8 32.4 %collective-permute-start.29 = (bf16[128,2048]{1,0:T(8,128)(2,1)S(1)}, bf16[128,2048]{1,0:T(8,128)(2,1)S(1)}, u32[]{:S(2)}, u32[]{:S(2)}) collective-permute-start(bf16[128,2048]{1,0:T(8,128)(2,1)S(1)} %slice.120), channel_id=1, source_target_pairs={{0,1},{2,0},{3,2},{1,3},{4,5},{6,4},{7,6},{5,7},{8,9},{10,8},{11,1... | collective-permute-start | bytes 1572872 | tf_op jit(solution)/shard_map/ppermute | solution.py:87
  267.9 34.2 %collective-permute-start.27 = (bf16[128,2048]{1,0:T(8,128)(2,1)}, bf16[128,2048]{1,0:T(8,128)(2,1)S(1)}, u32[]{:S(2)}, u32[]{:S(2)}) collective-permute-start(bf16[128,2048]{1,0:T(8,128)(2,1)} %slice.118), channel_id=1, source_target_pairs={{0,1},{2,0},{3,2},{1,3},{4,5},{6,4},{7,6},{5,7},{8,9},{10,8},{11,1... | collective-permute-start | bytes 1572872 | tf_op jit(solution)/shard_map/ppermute | solution.py:87
  269.8 32.3 %collective-permute-start.26 = (bf16[128,2048]{1,0:T(8,128)(2,1)}, bf16[128,2048]{1,0:T(8,128)(2,1)S(1)}, u32[]{:S(2)}, u32[]{:S(2)}) collective-permute-start(bf16[128,2048]{1,0:T(8,128)(2,1)} %slice.117), channel_id=1, source_target_pairs={{0,2},{2,3},{3,1},{1,0},{4,6},{6,7},{7,5},{5,4},{8,10},{10,11},{11... | collective-permute-start | bytes 1572872 | tf_op jit(solution)/shard_map/ppermute | solution.py:86
  442.8 41.7 %collective-permute-start.38 = (bf16[1536,1024]{1,0:T(8,128)(2,1)}, bf16[1536,1024]{1,0:T(8,128)(2,1)}, u32[]{:S(2)}, u32[]{:S(2)}) collective-permute-start(bf16[1536,1024]{1,0:T(8,128)(2,1)} %get-tuple-element.471), channel_id=1, source_target_pairs={{0,8},{8,0},{16,24},{24,16},{1,9},{9,1},{17,25},{25,17},{2,10},{10... | collective-permute-start | bytes 9437192 | tf_op jit(solution)/shard_map/ppermute | solution.py:126
  442.9 41.6 %all-to-all-start.1 = ((bf16[8,256,256]{2,1,0:T(8,128)(2,1)}), bf16[8,256,256]{2,1,0:T(8,128)(2,1)S(1)}, u32[]{:S(2)}, u32[]{:S(2)}) async-start(bf16[8,256,256]{2,1,0:T(8,128)(2,1)} %get-tuple-element.465), calls=%async_computation.1 | async-start | bytes 2097152 | tf_op jit(solution)/shard_map/all_to_all | solution.py:1306
  447.5 212.9 %reduce-scatter.2.cloned.1.call-start = ((), (), s32[]{:S(2)}) async-start(), calls=%async_computation.3 | async-start | bytes 10485760 | tf_op jit(solution)/shard_map/reduce_scatter | solution.py:1345
  447.7 36.8 %collective-permute-start.37 = (bf16[1536,512]{1,0:T(8,128)(2,1)}, bf16[1536,512]{1,0:T(8,128)(2,1)S(1)}, u32[]{:S(2)}, u32[]{:S(2)}) collective-permute-start(bf16[1536,512]{1,0:T(8,128)(2,1)} %get-tuple-element.469), channel_id=1, source_target_pairs={{0,16},{8,24},{16,0},{24,8},{1,17},{9,25},{17,1},{25,9},{2,18},{10... | collective-permute-start | bytes 4718600 | tf_op jit(solution)/shard_map/ppermute | solution.py:126
  484.5 45.0 %collective-permute-start.41 = (bf16[1536,1024]{1,0:T(8,128)(2,1)}, bf16[1536,1024]{1,0:T(8,128)(2,1)}, u32[]{:S(2)}, u32[]{:S(2)}) collective-permute-start(bf16[1536,1024]{1,0:T(8,128)(2,1)} %get-tuple-element.492), channel_id=1, source_target_pairs={{0,8},{8,0},{16,24},{24,16},{1,9},{9,1},{17,25},{25,17},{2,10},{10... | collective-permute-start | bytes 9437192 | tf_op jit(solution)/shard_map/ppermute | solution.py:126
  490.7 38.7 %collective-permute-start.42 = (bf16[1536,512]{1,0:T(8,128)(2,1)}, bf16[1536,512]{1,0:T(8,128)(2,1)S(1)}, u32[]{:S(2)}, u32[]{:S(2)}) collective-permute-start(bf16[1536,512]{1,0:T(8,128)(2,1)} %get-tuple-element.487), channel_id=1, source_target_pairs={{0,16},{8,24},{16,0},{24,8},{1,17},{9,25},{17,1},{25,9},{2,18},{10... | collective-permute-start | bytes 4718600 | tf_op jit(solution)/shard_map/ppermute | solution.py:126
  495.6 33.8 %collective-permute-start.43 = (bf16[688,512]{1,0:T(8,128)(2,1)S(1)}, bf16[688,512]{1,0:T(8,128)(2,1)S(1)}, u32[]{:S(2)}, u32[]{:S(2)}) collective-permute-start(bf16[688,512]{1,0:T(8,128)(2,1)S(1)} %slice.150), channel_id=1, source_target_pairs={{0,4},{1,5},{2,6},{3,7},{4,0},{5,1},{6,2},{7,3},{8,12},{9,13},{10,... | collective-permute-start | bytes 2113544 | tf_op jit(solution)/shard_map/ppermute | solution.py:1174
  538.9 45.4 %collective-permute-start.47 = (bf16[1536,512]{1,0:T(8,128)(2,1)}, bf16[1536,512]{1,0:T(8,128)(2,1)S(1)}, u32[]{:S(2)}, u32[]{:S(2)}) collective-permute-start(bf16[1536,512]{1,0:T(8,128)(2,1)} %get-tuple-element.506), channel_id=1, source_target_pairs={{0,16},{8,24},{16,0},{24,8},{1,17},{9,25},{17,1},{25,9},{2,18},{10... | collective-permute-start | bytes 4718600 | tf_op jit(solution)/shard_map/ppermute | solution.py:126
  543.8 38.4 %collective-permute-start.45 = (bf16[256,2048]{1,0:T(8,128)(2,1)}, bf16[256,2048]{1,0:T(8,128)(2,1)S(1)}, u32[]{:S(2)}, u32[]{:S(2)}) collective-permute-start(bf16[256,2048]{1,0:T(8,128)(2,1)} %get-tuple-element.501), channel_id=1, source_target_pairs={{0,2},{2,3},{3,1},{1,0},{4,6},{6,7},{7,5},{5,4},{8,10},{10,11},{11... | collective-permute-start | bytes 3145736 | tf_op jit(solution)/shard_map/ppermute | solution.py:106
  544.5 39.8 %collective-permute-start.46 = (bf16[256,2048]{1,0:T(8,128)(2,1)}, bf16[256,2048]{1,0:T(8,128)(2,1)S(1)}, u32[]{:S(2)}, u32[]{:S(2)}) collective-permute-start(bf16[256,2048]{1,0:T(8,128)(2,1)} %get-tuple-element.502), channel_id=1, source_target_pairs={{0,1},{2,0},{3,2},{1,3},{4,5},{6,4},{7,6},{5,7},{8,9},{10,8},{11,1... | collective-permute-start | bytes 3145736 | tf_op jit(solution)/shard_map/ppermute | solution.py:107
  545.8 38.5 %collective-permute-start.44 = (bf16[1024,512]{1,0:T(8,128)(2,1)S(1)}, bf16[1024,512]{1,0:T(8,128)(2,1)S(1)}, u32[]{:S(2)}, u32[]{:S(2)}) collective-permute-start(bf16[1024,512]{1,0:T(8,128)(2,1)S(1)} %pad_maximum_fusion.2), channel_id=1, source_target_pairs={{8,0},{16,8},{24,16},{9,1},{17,9},{25,17},{10,2},{18,10},{26,18},{... | collective-permute-start | bytes 3145736 | tf_op jit(solution)/shard_map/ppermute | solution.py:193
  551.2 31.0 %collective-permute-start.48 = (bf16[688,512]{1,0:T(8,128)(2,1)S(1)}, bf16[688,512]{1,0:T(8,128)(2,1)S(1)}, u32[]{:S(2)}, u32[]{:S(2)}) collective-permute-start(bf16[688,512]{1,0:T(8,128)(2,1)S(1)} %slice.153), channel_id=1, source_target_pairs={{0,4},{1,5},{2,6},{3,7},{4,0},{5,1},{6,2},{7,3},{8,12},{9,13},{10,... | collective-permute-start | bytes 2113544 | tf_op jit(solution)/shard_map/ppermute | solution.py:1174
  586.2 131.9 %all-gather.21.cloned.1.call-start = ((), (), s32[]{:S(2)}) async-start(), calls=%async_computation.7 | async-start | bytes 3522560 | tf_op jit(solution)/shard_map/all_gather | solution.py:177
  591.7 159.8 %all-gather.23.cloned.1.call-start = ((), (), s32[]{:S(2)}) async-start(), calls=%async_computation.8 | async-start | bytes 3522560 | tf_op jit(solution)/shard_map/all_gather | solution.py:177
  594.8 209.2 %all-gather.27.cloned.1.call-start = ((), (), s32[]{:S(2)}) async-start(), calls=%async_computation.10 | async-start | bytes 3522560 | tf_op jit(solution)/shard_map/all_gather | solution.py:177
  616.0 44.4 %collective-permute-start.51 = (bf16[688,512]{1,0:T(8,128)(2,1)S(1)}, bf16[688,512]{1,0:T(8,128)(2,1)S(1)}, u32[]{:S(2)}, u32[]{:S(2)}) collective-permute-start(bf16[688,512]{1,0:T(8,128)(2,1)S(1)} %slice.154), channel_id=1, source_target_pairs={{0,4},{1,5},{2,6},{3,7},{4,0},{5,1},{6,2},{7,3},{8,12},{9,13},{10,... | collective-permute-start | bytes 2113544 | tf_op jit(solution)/shard_map/ppermute | solution.py:1174
  667.3 147.2 %all-gather.25.cloned.1.call-start = ((), (), s32[]{:S(2)}) async-start(), calls=%async_computation.9 | async-start | bytes 1310720 | tf_op jit(solution)/shard_map/all_gather | solution.py:177
  705.0 31.3 %collective-permute-start.58 = (bf16[256,2048]{1,0:T(8,128)(2,1)}, bf16[256,2048]{1,0:T(8,128)(2,1)S(1)}, u32[]{:S(2)}, u32[]{:S(2)}) collective-permute-start(bf16[256,2048]{1,0:T(8,128)(2,1)} %get-tuple-element.568), channel_id=1, source_target_pairs={{0,2},{2,4},{4,6},{6,7},{7,5},{5,3},{3,1},{1,0},{8,10},{10,12},{12... | collective-permute-start | bytes 3145736 | tf_op jit(solution)/shard_map/ppermute | solution.py:106
  (126 other events, 1852.9 us)
Sparse Core Ops, SparseCore 0:
  180.6 25.9 all-gather.14
  262.1 27.8 all-gather.16
  302.3 28.9 all-gather.18
  585.5 74.1 reduce-scatter.1
  661.2 26.6 all-gather.20
  689.4 32.1 all-gather.22
  723.1 28.2 all-gather.26
  786.9 13.2 all-gather.24
